TPU v7x, 512 devices: a whole 4x4x16 slice. The times are simulated.
512 devices in a mesh: prow: 16 (over x, y), pcol: 32 (over z, core).
Axes of the slice: x: 4, y: 4, z: 16, core: 2. Of those that a mesh axis runs over, the one named last changes fastest.
Arguments:
- a_matrix: float32 [16384, 8192], P('prow', 'pcol'), as said below
- row_perms: int32 [2, 128], replicated, may hold values from 0 to 127, each once within a row
- dest_rows: int32 [2, 128], replicated, may hold values from 0 to 127, as said below
- row_mask: int32 [2, 128], replicated, may hold values 0 or 1
- col_mask: int32 [2, 64], replicated, may hold values 0 or 1
Outputs:
- schur_out: float32 [16384, 8192], P('prow', 'pcol')
- l_panels: float32 [16384, 256], P('prow')
Inputs may be any that keep to these rules, and one draw needn't show every extreme that they name: `a_matrix`: the two leading diagonal blocks of the window carry 16 sqrt(128) on their diagonal, on top of entries of order one. `dest_rows`: for each section, a permutation of the 128 block rows that keeps a block row's position among the 8 block rows of its device; block rows of one device whose positions differ by less than 16 go to different devices.
All inputs are finite; a program needn't handle non-finite values.
Results may differ from a plain program's by a relative error of at most 0.0001.
Values sent between devices are 32-bit elements; how exact they have to be, the bound alone decides.
No kernel may reach another device: no remote copies, remote signals or barrier semaphores. Data moves between devices by JAX's collectives and lax.ppermute only.
A program may use at most 64 MiB of HBM per device.

v0:
```python
import jax
import jax.numpy as jnp
from jax import lax
from jax.sharding import PartitionSpec as P

SWEEPS = 3


def spread(block, axis, owner):
    block = jnp.where(lax.axis_index(axis) == owner, block, jnp.zeros_like(block))
    return lax.psum(block, axis)


def refine(pivot_block):
    width = pivot_block.shape[0]
    identity = jnp.eye(width, dtype=pivot_block.dtype)
    scale = width * (jnp.mean(pivot_block * pivot_block) + 1e-06)
    approx = pivot_block.T / scale
    for sweep in range(SWEEPS):
        inner = jnp.dot(pivot_block, approx, precision=lax.Precision.HIGHEST)
        approx = jnp.dot(approx, 2.0 * identity - inner, precision=lax.Precision.HIGHEST)
    return approx


def block_flags(mask_row, owner, count, section):
    local = lax.dynamic_slice_in_dim(mask_row, owner * count, count)
    global_ids = owner * count + jnp.arange(count, dtype=jnp.int32)
    return ((local == 1) & (global_ids > section)).astype(jnp.float32)


def shards(a_matrix, row_perms, dest_rows, row_mask, col_mask):
    width = row_perms.shape[1]
    rows_here = a_matrix.shape[0] // width
    cols_here = a_matrix.shape[1] // width
    n_owners = lax.axis_size("prow")
    capacity = (rows_here + n_owners - 1) // n_owners
    my_row = lax.axis_index("prow")
    my_col = lax.axis_index("pcol")
    owner_ids = jnp.arange(n_owners, dtype=jnp.int32)
    slot_ids = jnp.arange(rows_here, dtype=jnp.int32)
    slot_group = slot_ids // n_owners
    group_ids = jnp.arange(capacity, dtype=jnp.int32)
    group_map = (slot_group[:, None] == group_ids[None, :]).astype(jnp.float32)
    current = a_matrix
    panels = []
    for section in range(2):
        root_row = section // rows_here
        local_row = section % rows_here
        local_col = section % cols_here
        block = current[local_row * width : (local_row + 1) * width]
        pivoted = jnp.take(block, row_perms[section], axis=0)
        upper = spread(pivoted, "prow", root_row)
        current = current.at[local_row * width : (local_row + 1) * width].set(
            jnp.where(my_row == root_row, upper, block)
        )
        inverse = refine(upper[:, local_col * width : (local_col + 1) * width])
        column = current[:, local_col * width : (local_col + 1) * width]
        row_flags = block_flags(row_mask[section], my_row, rows_here, section)
        lower = jnp.dot(column, inverse, precision=lax.Precision.HIGHEST)
        lower = lower * jnp.repeat(row_flags, width)[:, None]
        gathered = spread(lower, "pcol", section // cols_here)
        panels.append(gathered)
        col_flags = block_flags(col_mask[section], my_col, cols_here, section)
        kept = upper * jnp.repeat(col_flags, width)[None, :]
        targets = lax.dynamic_slice_in_dim(dest_rows[section], my_row * rows_here, rows_here)
        target_dev = targets // rows_here
        send_map = (
            (target_dev[None, None, :] == owner_ids[:, None, None])
            & (slot_group[None, None, :] == group_ids[None, :, None])
        ).astype(jnp.float32)
        mine = my_row * rows_here + slot_ids
        all_targets = dest_rows[section].reshape(n_owners, rows_here)
        matches = (all_targets[None, :, :] == mine[:, None, None]).astype(jnp.float32)
        recv_map = jnp.einsum("tpr,rk->tpk", matches, group_map, precision=lax.Precision.HIGHEST)
        product = jnp.dot(gathered, kept, precision=lax.Precision.HIGHEST)
        outgoing = jnp.einsum(
            "qkr,rbc->qkbc",
            send_map,
            product.reshape(rows_here, width, -1),
            precision=lax.Precision.HIGHEST,
        ).reshape(n_owners * capacity * width, -1)
        arrived = lax.all_to_all(outgoing, "prow", split_axis=0, concat_axis=0, tiled=True).reshape(
            n_owners, capacity, width, -1
        )
        placed = jnp.einsum(
            "tpk,pkbc->tbc", recv_map, arrived, precision=lax.Precision.HIGHEST
        ).reshape(rows_here * width, -1)
        current = current - placed
    return (current, jnp.concatenate(panels, axis=1))


def solution(mesh):
    placed = (P("prow", "pcol"), P(), P(), P(), P())
    return jax.shard_map(
        shards,
        mesh=mesh,
        in_specs=placed,
        out_specs=(P("prow", "pcol"), P("prow", None)),
        check_vma=False,
    )
```

profile of v0, /device:TPU:1, one launch (start us, length us, event | category | flops | bytes accessed | tf_op | source)
XLA Modules:
  0.0 773.6 jit_solution(13413972947805506345)
XLA Ops:
  7.3 1.2 copy.34
  8.5 0.8 gather_fusion
  9.3 0.7 select_select_fusion.1
  10.3 0.1 and_select_fusion.1
  10.4 118.2 %all-reduce.5.cloned.1.call-done = f32[128,256]{1,0:T(8,128)} async-done(((f32[128,256]{1,0:T(8,128)}), f32[128,256]{1,0:T(8,128)}) %all-reduce.5.cloned.1.call-update) | async-done | bytes 131088 | tf_op jit(solution)/shard_map/psum | solution.py:11
  128.6 1.5 multiply_reduce_fusion.1
  130.8 1.2 convolution_subtract_fusion.5
  132.0 1.1 fusion.25
  133.1 1.0 convolution_subtract_fusion.4
  134.2 0.2 fusion.77
  134.4 1.0 convolution_subtract_fusion.3
  135.4 0.2 fusion.78
  135.6 0.9 select_dynamic-update-slice_fusion.1
  136.6 1.4 fusion.5
  138.1 208.5 %all-reduce.7.cloned.1.call-done = f32[1024,128]{1,0:T(8,128)} async-done(((f32[1024,128]{1,0:T(8,128)}), f32[1024,128]{1,0:T(8,128)}) %all-reduce.7.cloned.1.call-update) | async-done | bytes 524304 | tf_op jit(solution)/shard_map/psum | solution.py:11
  346.7 2.0 fusion.14
  348.7 1.5 fusion.8
  350.2 2.5 copy.10
  352.8 6.5 all-to-all-start
  359.5 0.2 fusion.20
  359.8 28.7 %all-to-all-done = f32[16,128,256]{2,1,0:T(8,128)S(1)} async-done(((f32[16,128,256]{2,1,0:T(8,128)}), f32[16,128,256]{2,1,0:T(8,128)S(1)}, u32[]{:S(2)}, u32[]{:S(2)}) %all-to-all-start) | async-done | bytes 2097184 | tf_op jit(solution)/shard_map/all_to_all | solution.py:82
  388.5 2.2 fusion.2
  390.8 0.3 copy.12
  391.1 0.1 bitcast_subtract_fusion.1
  391.3 0.8 gather_fusion.1
  392.0 0.7 select_select_fusion
  392.8 0.2 all-reduce.11.cloned.1.call-start
  393.2 110.2 %all-reduce.9.cloned.1.call-done = f32[128,256]{1,0:T(8,128)} async-done(((f32[128,256]{1,0:T(8,128)}), f32[128,256]{1,0:T(8,128)}) %all-reduce.9.cloned.1.call-update) | async-done | bytes 131088 | tf_op jit(solution)/shard_map/psum | solution.py:11
  503.4 1.5 multiply_reduce_fusion
  505.6 1.2 convolution_subtract_fusion.2
  506.8 1.1 fusion.22
  507.9 1.0 convolution_subtract_fusion.1
  509.0 0.2 fusion.79
  509.2 1.0 convolution_subtract_fusion
  510.2 0.2 fusion.80
  510.4 0.9 select_dynamic-update-slice_fusion
  511.4 1.4 fusion.4
  512.9 208.5 %all-reduce.11.cloned.1.call-done = f32[1024,128]{1,0:T(8,128)} async-done(((f32[1024,128]{1,0:T(8,128)}), f32[1024,128]{1,0:T(8,128)}) %all-reduce.11.cloned.1.call-update) | async-done | bytes 524304 | tf_op jit(solution)/shard_map/psum | solution.py:11
  721.5 2.0 fusion.12
  723.5 1.5 fusion.6
  725.0 2.5 copy.14
  727.6 6.5 all-to-all-start.1
  734.2 0.3 fusion.18
  734.5 2.3 pad_maximum_fusion
  736.7 26.6 %all-to-all-done.1 = f32[16,128,256]{2,1,0:T(8,128)S(1)} async-done(((f32[16,128,256]{2,1,0:T(8,128)}), f32[16,128,256]{2,1,0:T(8,128)S(1)}, u32[]{:S(2)}, u32[]{:S(2)}) %all-to-all-start.1) | async-done | bytes 2097184 | tf_op jit(solution)/shard_map/all_to_all | solution.py:82
  763.3 2.2 fusion
  765.6 0.3 copy.16
  765.9 1.1 bitcast_subtract_fusion
  (44 shorter events, 1.1 us)
Async XLA Ops:
  7.2 1.3 copy-start.4
  7.2 3.1 copy-start.5
  7.2 2.9 copy-start.6
  7.2 3.1 copy-start.7
  7.2 121.4 %all-reduce.5.cloned.1.call-start = ((), (), s32[]{:S(2)}) async-start(), calls=%async_computation.2 | async-start | bytes 262144 | tf_op jit(solution)/shard_map/psum | solution.py:11
  10.1 336.6 %all-reduce.7.cloned.1.call-start = ((), (), s32[]{:S(2)}) async-start(), calls=%async_computation.3 | async-start | bytes 1048576 | tf_op jit(solution)/shard_map/psum | solution.py:11
  128.6 218.1 %copy-start.2 = (f32[128,256]{1,0:T(8,128)S(1)}, f32[128,256]{1,0:T(8,128)}, u32[]{:S(2)}) copy-start(f32[128,256]{1,0:T(8,128)} %all-reduce.5.cloned.1.call-done) | copy-start | bytes 393220
  136.6 213.7 %copy-start = (f32[1024,256]{1,0:T(8,128)}, f32[1024,256]{1,0:T(8,128)S(1)}, u32[]{:S(2)}) copy-start(f32[1024,256]{1,0:T(8,128)S(1)} %select_dynamic-update-slice_fusion.1) | copy-start | bytes 3145732
  352.8 35.7 %all-to-all-start = ((f32[16,128,256]{2,1,0:T(8,128)}), f32[16,128,256]{2,1,0:T(8,128)S(1)}, u32[]{:S(2)}, u32[]{:S(2)}) async-start(f32[16,128,256]{2,1,0:T(8,128)} %copy.10), calls=%async_computation | async-start | bytes 4194304 | tf_op jit(solution)/shard_map/all_to_all | solution.py:82
  359.3 144.1 %all-reduce.9.cloned.1.call-start = ((), (), s32[]{:S(2)}) async-start(), calls=%async_computation.4 | async-start | bytes 262144 | tf_op jit(solution)/shard_map/psum | solution.py:11
  388.5 2.6 copy-start.1
  392.8 328.7 %all-reduce.11.cloned.1.call-start = ((), (), s32[]{:S(2)}) async-start(), calls=%async_computation.5 | async-start | bytes 1048576 | tf_op jit(solution)/shard_map/psum | solution.py:11
  503.4 218.1 %copy-start.3 = (f32[128,256]{1,0:T(8,128)S(1)}, f32[128,256]{1,0:T(8,128)}, u32[]{:S(2)}) copy-start(f32[128,256]{1,0:T(8,128)} %all-reduce.9.cloned.1.call-done) | copy-start | bytes 393220
  727.6 35.8 %all-to-all-start.1 = ((f32[16,128,256]{2,1,0:T(8,128)}), f32[16,128,256]{2,1,0:T(8,128)S(1)}, u32[]{:S(2)}, u32[]{:S(2)}) async-start(f32[16,128,256]{2,1,0:T(8,128)} %copy.14), calls=%async_computation.1 | async-start | bytes 4194304 | tf_op jit(solution)/shard_map/all_to_all | solution.py:82
Sparse Core Ops, SparseCore 0:
  11.8 116.7 all-reduce.4
  138.1 208.5 all-reduce.6
  392.9 110.4 all-reduce.8
  512.9 208.5 all-reduce.10
where the time goes:
time: 774 us
  waiting for transfers between devices  701 us (91%)
  matrix products  24.4 us (3%)
  between operations  15.4 us (2%)
  starting transfers between devices  13.4 us (2%)
  other arithmetic  10.4 us (1%)
  local copies, waits for them, and re-layouts  9.03 us (1%)
    psum x4, waiting for transfers between devices, spread(): return lax.psum(block, axis)  645 us
    all_to_all x2, waiting for transfers between devices, shards(): lax.all_to_all(outgoing, 'prow', split_axis=0, concat_axis=0, tiled=True)  55.4 us
  transfers between devices with their start and end apart: 6, of which 6 were waited for; matrix products, arithmetic and copies ran while one was open for 0% of the time, Pallas kernels for 0%

commit v1 on v0

v1 whole, which is shorter than its diff:
```python
import jax
import jax.numpy as jnp
from jax import lax
from jax.experimental import pallas as pl
from jax.experimental.pallas import tpu as pltpu
from jax.sharding import Mesh
from jax.sharding import PartitionSpec as P

SWEEPS = 3
W = 128
NP = 16
NZ = 16
HI = lax.Precision.HIGHEST


def dot(a, b):
    return jnp.dot(a, b, precision=HI, preferred_element_type=jnp.float32)


def refine(pivot):
    row = lax.broadcasted_iota(jnp.int32, (W, W), 0)
    col = lax.broadcasted_iota(jnp.int32, (W, W), 1)
    two = jnp.where(row == col, 2.0, 0.0).astype(jnp.float32)
    scale = W * (jnp.mean(pivot * pivot) + 1e-6)
    approx = pivot.T / scale
    for _ in range(SWEEPS):
        approx = dot(approx, two - dot(pivot, approx))
    return approx


def route_kernel(meta, share, passed, half, out):
    core = meta[0]
    kept = meta[5] == 1
    out[...] = jnp.zeros_like(out)
    for j in range(4):
        block = jnp.where(kept, jnp.where(core == 0, share[j, 0], share[j, 1]), passed[j])
        half[j] = block[:, :W]
        half[4 + j] = block[:, W:]
        out[meta[48 + 2 * j + core], 0] = block[:, :W]
        if j == 0:
            out[:, 1] = jnp.broadcast_to(block[None, :, :W], (NP, 8, W))
            out[:, 2] = jnp.broadcast_to(block[None, :, W:], (NP, 8, W))


def pack_kernel(meta, half, got, out):
    core = meta[0]
    out[:8] = half[...]
    for j in range(4):
        out[8 + j] = got[meta[56 + 2 * j + core], 0]
    out[12] = jnp.where(core == 0, got[0, 1], got[meta[4], 1])
    out[13] = got[0, 2]


def factor_kernel(meta, own, oth, perm, lpan, plow, send, lsrc):
    core = meta[0]
    first = core == 0

    def tile(ref, t):
        return ref[:, t].reshape(W, W)

    def even(t):
        return jnp.where(first, tile(own, t), tile(oth, t))

    def odd(t):
        return jnp.where(first, tile(oth, t), tile(own, t))

    def flag(i):
        return meta[i].astype(jnp.float32)

    inv0 = refine(dot(perm[0], even(12)))
    kept01 = dot(perm[0], even(13)) * flag(2)
    low_src = dot(odd(12), inv0) * flag(3)
    lsrc[...] = low_src
    inv1 = refine(dot(perm[1], odd(13) - dot(low_src, kept01)))
    for ref, parity in ((own, core), (oth, 1 - core)):
        col0 = jnp.concatenate([tile(ref, j) for j in range(4)], axis=0)
        ext0 = jnp.concatenate([tile(ref, 8 + j) for j in range(4)], axis=0)
        col1 = jnp.concatenate([tile(ref, 4 + j) for j in range(4)], axis=0)
        low0 = dot(col0, inv0)
        ext0 = dot(ext0, inv0)
        ext0 = jnp.concatenate(
            [ext0[j * W : (j + 1) * W] * flag(24 + 2 * j + parity) for j in range(4)], axis=0
        )
        low1 = dot(col1 - dot(ext0, kept01), inv1)
        for j in range(4):
            slot = 2 * j + parity
            here = pl.ds(pl.multiple_of(slot * W, W), W)
            part = slice(j * W, (j + 1) * W)
            lpan[here, :W] = low0[part] * flag(8 + slot)
            lpan[here, W:] = low1[part] * flag(16 + slot)
            plow[here, :] = ext0[part]
    for slot in range(8):
        half = pl.ds(pl.multiple_of(slot * W + core * (W // 2), W // 2), W // 2)
        send[meta[32 + slot]] = lpan[half, W:]


def first_kernel(meta, a, rows, plow, lsrc, perm, flags, cur, kept):
    up0 = dot(perm[0], rows[:W])
    kept0 = up0 * flags[0:1]
    up1 = dot(perm[1], rows[W:] - dot(lsrc[...], kept0))
    kept[...] = up1 * flags[1:2]
    prod = dot(plow[...], kept0)
    cur[...] = a[...] - prod

    @pl.when(meta[1] == 1)
    def _():
        cur[:W] = up0 - prod[:W]
        cur[W : 2 * W] = up1


def second_kernel(meta, cur, own, oth, kept, out, low):
    core = meta[0]
    h = W // 2
    for slot in range(8):
        dev = meta[40 + slot]
        low[pl.ds(pl.multiple_of(slot * W + core * h, h), h), :] = own[dev]
        low[pl.ds(pl.multiple_of(slot * W + (1 - core) * h, h), h), :] = oth[dev]
    out[...] = cur[...] - dot(low[...], kept[...])


def f32(*shape):
    return jax.ShapeDtypeStruct(shape, jnp.float32)


def call(kernel, out_shape, n_in, scratch=(), flops=0, moved=0):
    smem = pl.BlockSpec(memory_space=pltpu.SMEM)
    vmem = pl.BlockSpec(memory_space=pltpu.VMEM)
    multi = isinstance(out_shape, (tuple, list))
    return pl.pallas_call(
        kernel,
        out_shape=out_shape,
        in_specs=[smem] + [vmem] * n_in,
        out_specs=[vmem] * len(out_shape) if multi else vmem,
        scratch_shapes=list(scratch),
        compiler_params=pltpu.CompilerParams(vmem_limit_bytes=40 * 2**20),
        cost_estimate=pl.CostEstimate(flops=flops, bytes_accessed=moved, transcendentals=0),
    )


def pick(parts, index):
    return lax.dynamic_index_in_dim(parts, index, 0, keepdims=False)


def shards(a, row_perms, dest_rows, row_mask, col_mask):
    me = lax.axis_index("prow")
    z = lax.axis_index("z")
    core = lax.axis_index("core")
    ids = jnp.arange(W, dtype=jnp.int32)
    slots = jnp.arange(8, dtype=jnp.int32)

    src_rows = jnp.sum(
        jnp.where(dest_rows[:, :, None] == ids[None, None, :], ids[None, :, None], 0), axis=1
    )
    row_ok = ((row_mask == 1) & (ids[None, :] > jnp.arange(2, dtype=jnp.int32)[:, None])).astype(jnp.int32)

    def mine(v):
        return lax.dynamic_slice_in_dim(v, me * 8, 8)

    dest_dev0 = mine(dest_rows[0]) // 8
    dest_dev1 = mine(dest_rows[1]) // 8
    src0 = mine(src_rows[0])
    src_dev1 = mine(src_rows[1]) // 8
    head_src = src_rows[0, 1]
    meta = jnp.concatenate(
        [
            jnp.stack(
                [
                    core,
                    (me == 0).astype(jnp.int32),
                    (col_mask[0, 1] == 1).astype(jnp.int32),
                    row_ok[0, head_src],
                    head_src // 8,
                    (core == (z >= 8)).astype(jnp.int32),
                    *[jnp.int32(0)] * 2,
                ]
            ).astype(jnp.int32),
            mine(row_ok[0]),
            mine(row_ok[1]),
            row_ok[0][src0],
            dest_dev1,
            src_dev1,
            dest_dev0,
            src0 // 8,
        ]
    )
    perm = (row_perms[:, :, None] == ids[None, None, :]).astype(jnp.float32)
    col_ids = (z * 2 + core) * 2 + jnp.arange(2, dtype=jnp.int32)
    col_ok = (lax.dynamic_slice_in_dim(col_mask, col_ids[0], 2, axis=1) == 1) & (
        col_ids[None, :] > jnp.arange(2, dtype=jnp.int32)[:, None]
    )
    flags = jnp.repeat(col_ok.astype(jnp.float32), W, axis=1)
    flags = jnp.concatenate([flags, jnp.zeros((6, 2 * W), jnp.float32)], axis=0)

    cut = a.reshape(8, NZ, 8, 2 * W).transpose(1, 0, 2, 3)
    over = lax.ppermute(cut[8:], "core", [(0, 1)])
    chunks = jnp.where(core == 0, cut[:8], over)
    share = jnp.where((z == 0) & (core == 0), chunks[0], jnp.zeros_like(chunks[0]))
    for k in range(8):
        pairs = [(1, 2 * (8 + k) + 1)] + ([(0, 2 * k)] if k else [])
        share = share + lax.ppermute(chunks[k], ("z", "core"), pairs)
    share = share.reshape(4, 2, 8, 2 * W)
    passed = lax.ppermute(pick(share.transpose(1, 0, 2, 3), 1 - core), "core", [(0, 1), (1, 0)])

    rows = a[: 2 * W]
    for step in (8, 4, 2, 1):
        pairs = [(p, p + step) for p in range(0, NP, 2 * step)]
        got = lax.ppermute(rows, "prow", pairs)
        rows = jnp.where(me % (2 * step) == step, got, rows)

    half, out0 = call(route_kernel, (f32(8, 8, W), f32(NP, 3, 8, W)), 2, moved=2**19)(meta, share, passed)
    got0 = lax.all_to_all(out0, "prow", 0, 0, tiled=True)
    payload = call(pack_kernel, f32(14, 8, W), 2, moved=2**19)(meta, half, got0)

    own = lax.all_gather(payload, "z", axis=0, tiled=False)
    oth = lax.ppermute(own, "core", [(0, 1), (1, 0)])

    lpan, plow, send, lsrc = call(
        factor_kernel,
        (f32(8 * W, 2 * W), f32(8 * W, W), f32(NP, W // 2, W), f32(W, W)),
        3,
        flops=5 * 10**8,
        moved=4 * 2**20,
    )(meta, own, oth, perm)

    got1 = lax.all_to_all(send, "prow", 0, 0, tiled=True)
    cur, kept = call(
        first_kernel, (f32(8 * W, 2 * W), f32(W, 2 * W)), 6, flops=5 * 10**8, moved=3 * 2**20
    )(meta, a, rows, plow, lsrc, perm, flags)
    oth1 = lax.ppermute(got1, "core", [(0, 1), (1, 0)])
    schur = call(
        second_kernel,
        f32(8 * W, 2 * W),
        4,
        scratch=(pltpu.VMEM((8 * W, W), jnp.float32),),
        flops=5 * 10**8,
        moved=3 * 2**20,
    )(meta, cur, got1, oth1, kept)
    return schur, lpan


def solution(mesh):
    fine = Mesh(mesh.devices.reshape(NP, NZ, 2), ("prow", "z", "core"))
    placed = (P("prow", ("z", "core")), P(), P(), P(), P())
    return jax.shard_map(
        shards,
        mesh=fine,
        in_specs=placed,
        out_specs=(P("prow", ("z", "core")), P("prow", None)),
        check_vma=False,
    )
```

time: 774 us -> 140 us (0.18)
  waiting for transfers between devices: 701 us -> 20.3 us
  starting transfers between devices: 13.4 us -> 59 us
  blocking collectives: 0 us -> 27.7 us
  matrix products: 24.4 us -> 0 us
  Pallas kernels: 0 us -> 14.5 us
  between operations: 15.4 us -> 5.76 us
  other arithmetic: 10.4 us -> 2.46 us
    psum x4 -> x0, waiting for transfers between devices: 645 us -> none  [spread(): return lax.psum(block, axis)]
    ppermute x0 -> x16, starting transfers between devices: none -> 48.1 us  [the longest x8 17.8 us: shards(): share = share + lax.ppermute(chunks[k], ('z', 'core'), pairs)]
    all_to_all x2, waiting for transfers between devices: 55.4 us -> 7.56 us  [the longest x1 5.2 us: shards(): got1 = lax.all_to_all(send, 'prow', 0, 0, tiled=True)]
    all_gather x0 -> x1, blocking collectives: none -> 27.7 us  [shards(): own = lax.all_gather(payload, 'z', axis=0, tiled=False)]
    dot_general x22 -> x0, matrix products: 24.4 us -> none  [the longest x6 6.56 us: refine(): inner = jnp.dot(pivot_block, approx, precision=lax.Precision.HIGHEST)]
    pallas_call x0 -> x5, Pallas kernels: none -> 14.5 us  [the longest x1 7.91 us: shards(): call(factor_kernel, (f32(8 * W, 2 * W), f32(8 * W, W), f32(NP, W // 2, W)...]
    ppermute x0 -> x16, waiting for transfers between devices: none -> 12.8 us  [the longest x1 6.64 us: shards(): over = lax.ppermute(cut[8:], 'core', [(0, 1)])]
  transfers between devices with their start and end apart: 6 -> 18, of which waited for: 6 -> 5; matrix products, arithmetic and copies ran while one was open for 0% -> 4% of each run, Pallas kernels for 0% -> 8%
where the time goes in v1:
time: 140 us; the launch traced here: 139 us
  starting transfers between devices  59 us (42%)
  blocking collectives  27.7 us (20%)
  waiting for transfers between devices  20.3 us (14%)
  Pallas kernels  14.5 us (10%)
  local copies, waits for them, and re-layouts  8.86 us (6%)
  between operations  5.76 us (4%)
  other arithmetic  2.46 us (2%)
    all_gather x1, blocking collectives, shards(): own = lax.all_gather(payload, 'z', axis=0, tiled=False)  27.7 us
    ppermute x8, starting transfers between devices, shards(): share = share + lax.ppermute(chunks[k], ('z', 'core'), pairs)  17.8 us
    ppermute x4, starting transfers between devices, shards(): got = lax.ppermute(rows, 'prow', pairs)  12.6 us
    ppermute x1, starting transfers between devices, shards(): oth = lax.ppermute(own, 'core', [(0, 1), (1, 0)])  10.3 us
    pallas_call x1, Pallas kernels, shards(): call(factor_kernel, (f32(8 * W, 2 * W), f32(8 * W, W), f32(NP, W // 2, W)...  7.91 us
    all_to_all x1, starting transfers between devices, shards(): got0 = lax.all_to_all(out0, 'prow', 0, 0, tiled=True)  6.75 us
    ppermute x1, waiting for transfers between devices, shards(): over = lax.ppermute(cut[8:], 'core', [(0, 1)])  6.64 us
    all_to_all x1, waiting for transfers between devices, shards(): got1 = lax.all_to_all(send, 'prow', 0, 0, tiled=True)  5.2 us
  transfers between devices with their start and end apart: 18, of which 5 were waited for; matrix products, arithmetic and copies ran while one was open for 4% of the time, Pallas kernels for 8%

profile of v1, /device:TPU:1, one launch (start us, length us, event | category | flops | bytes accessed | tf_op | source)
XLA Modules:
  0.0 138.7 jit_solution(6218842685294763116)
XLA Ops:
  0.6 1.3 copy.14
  2.0 1.3 collective-permute-start.4
  3.3 0.7 copy-done.4
  4.0 0.1 select_reduce_fusion
  4.1 0.7 copy-done.7
  4.8 0.1 fusion.6
  4.9 6.6 %collective-permute-done.4 = f32[8,8,8,256]{3,2,1,0:T(8,128)S(1)} collective-permute-done((f32[8,8,8,256]{3,2,1,0:T(8,128)S(1)}, f32[8,8,8,256]{3,2,1,0:T(8,128)S(1)}, u32[]{:S(2)}, u32[]{:S(2)}) %collective-permute-start.4) | collective-permute-done | bytes 524320 | tf_op jit(solution)/shard_map/ppermute | solution.py:195
  11.7 7.2 %collective-permute-start.10 = (f32[8,8,256]{2,1,0:T(8,128)S(1)}, f32[8,8,256]{2,1,0:T(8,128)S(1)}, u32[]{:S(2)}, u32[]{:S(2)}) collective-permute-start(f32[8,8,256]{2,1,0:T(8,128)S(1)} %get-tuple-element.21), channel_id=1, source_target_pairs={{1,27},{0,10},{33,59},{32,42},{65,91},{64,74},{97,123},{96,106},{1... | collective-permute-start | bytes 196616 | tf_op jit(solution)/shard_map/ppermute | solution.py:200
  18.9 1.3 collective-permute-start.11
  20.2 1.3 collective-permute-start.12
  21.5 0.1 and_select_fusion
  21.6 2.8 %collective-permute-start.5 = (f32[8,8,256]{2,1,0:T(8,128)S(1)}, f32[8,8,256]{2,1,0:T(8,128)S(1)}, u32[]{:S(2)}, u32[]{:S(2)}) collective-permute-start(f32[8,8,256]{2,1,0:T(8,128)S(1)} %get-tuple-element.18), channel_id=1, source_target_pairs={{1,17},{33,49},{65,81},{97,113},{129,145},{161,177},{193,209},{225... | collective-permute-start | bytes 196616 | tf_op jit(solution)/shard_map/ppermute | solution.py:200
  24.5 1.3 collective-permute-start.6
  25.8 1.3 collective-permute-start.7
  27.1 1.3 collective-permute-start.8
  28.4 1.3 collective-permute-start.9
  29.8 1.2 collective-permute-done.9
  31.1 1.9 %collective-permute-start.13 = (f32[4,8,256]{2,1,0:T(8,128)S(1)}, f32[4,8,256]{2,1,0:T(8,128)S(1)}, u32[]{:S(2)}, u32[]{:S(2)}) collective-permute-start(f32[4,8,256]{2,1,0:T(8,128)S(1)} %dynamic-slice_bitcast_fusion), channel_id=1, source_target_pairs={{0,1},{1,0},{2,3},{3,2},{4,5},{5,4},{6,7},{7,6},{8,9},{9,8},{10,11... | collective-permute-start | bytes 98312 | tf_op jit(solution)/shard_map/ppermute | solution.py:202
  33.0 0.1 and_select_fusion.2
  33.1 0.6 slice.63
  37.6 0.6 constant_dynamic-slice_fusion.6
  38.2 0.6 slice.62
  39.4 0.6 gather_fusion
  40.1 0.6 concatenate.6.meta
  40.7 1.2 shard_map.68
  42.0 6.8 %all-to-all-start = ((f32[16,3,8,128]{3,2,1,0:T(8,128)}), f32[16,3,8,128]{3,2,1,0:T(8,128)S(1)}, u32[]{:S(2)}, u32[]{:S(2)}) async-start(f32[16,3,8,128]{3,2,1,0:T(8,128)} %get-tuple-element.11), calls=%async_computation | async-start | bytes 393216 | tf_op jit(solution)/shard_map/all_to_all | solution.py:211
  48.8 4.8 %collective-permute-start = (f32[256,256]{1,0:T(8,128)S(1)}, f32[256,256]{1,0:T(8,128)S(1)}, u32[]{:S(2)}, u32[]{:S(2)}) collective-permute-start(f32[256,256]{1,0:T(8,128)S(1)} %slice.70), channel_id=1, source_target_pairs={{0,256},{1,257},{2,258},{3,259},{4,260},{5,261},{6,262},{7,263},{8... | collective-permute-start | bytes 786440 | tf_op jit(solution)/shard_map/ppermute | solution.py:207
  53.6 2.4 %all-to-all-done.got = f32[16,3,8,128]{3,2,1,0:T(8,128)S(1)} async-done(((f32[16,3,8,128]{3,2,1,0:T(8,128)}), f32[16,3,8,128]{3,2,1,0:T(8,128)S(1)}, u32[]{:S(2)}, u32[]{:S(2)}) %all-to-all-start) | async-done | bytes 196640 | tf_op jit(solution)/shard_map/all_to_all | solution.py:211
  55.9 0.6 shard_map.69
  56.5 27.7 %all-gather = f32[224,8,128]{2,1,0:T(8,128)S(1)} all-gather(f32[14,8,128]{2,1,0:T(8,128)S(1)} %shard_map.69), channel_id=2, replica_groups=mesh['prow'=16,'z'=16,'core'=2] {'z'}, dimensions={0}, use_global_device_ids=true | all-gather | bytes 974848 | tf_op jit(solution)/shard_map/all_gather | solution.py:214
  84.2 10.3 %collective-permute-start.14 = (f32[16,14,8,128]{3,2,1,0:T(8,128)S(1)}, f32[16,14,8,128]{3,2,1,0:T(8,128)S(1)}, u32[]{:S(2)}, u32[]{:S(2)}) collective-permute-start(f32[16,14,8,128]{3,2,1,0:T(8,128)S(1)} %bitcast.71), channel_id=1, source_target_pairs={{0,1},{1,0},{2,3},{3,2},{4,5},{5,4},{6,7},{7,6},{8,9},{9,8},{10,11... | collective-permute-start | bytes 2752520 | tf_op jit(solution)/shard_map/ppermute | solution.py:215
  94.6 1.9 %collective-permute-start.1 = (f32[256,256]{1,0:T(8,128)S(1)}, f32[256,256]{1,0:T(8,128)S(1)}, u32[]{:S(2)}, u32[]{:S(2)}) collective-permute-start(f32[256,256]{1,0:T(8,128)S(1)} %broadcast_select_fusion), channel_id=1, source_target_pairs={{0,128},{256,384},{1,129},{257,385},{2,130},{258,386},{3,131},{259... | collective-permute-start | bytes 786440 | tf_op jit(solution)/shard_map/ppermute | solution.py:207
  96.6 0.7 copy-done.5
  97.2 0.1 fusion.perm
  97.4 4.9 %collective-permute-done.1 = f32[256,256]{1,0:T(8,128)S(1)} collective-permute-done((f32[256,256]{1,0:T(8,128)S(1)}, f32[256,256]{1,0:T(8,128)S(1)}, u32[]{:S(2)}, u32[]{:S(2)}) %collective-permute-start.1) | collective-permute-done | bytes 262176 | tf_op jit(solution)/shard_map/ppermute | solution.py:207
  102.2 0.7 broadcast_select_fusion.1
  103.0 2.0 %collective-permute-start.2 = (f32[256,256]{1,0:T(8,128)}, f32[256,256]{1,0:T(8,128)}, u32[]{:S(2)}, u32[]{:S(2)}) collective-permute-start(f32[256,256]{1,0:T(8,128)} %broadcast_select_fusion.1), channel_id=1, source_target_pairs={{0,64},{128,192},{256,320},{384,448},{1,65},{129,193},{257,321},{3... | collective-permute-start | bytes 786440 | tf_op jit(solution)/shard_map/ppermute | solution.py:207
  105.0 7.9 %shard_map.70 = (f32[1024,256]{1,0:T(8,128)}, f32[1024,128]{1,0:T(8,128)S(1)}, f32[16,64,128]{2,1,0:T(8,128)S(1)}, f32[128,128]{1,0:T(8,128)S(1)}) custom-call(s32[64]{0:T(128)S(1)} %concatenate.6.meta, f32[16,14,8,128]{3,2,1,0:T(8,128)S(1)} %bitcast.72, f32[16,14,8,128]{3,2,1,0:T(8,128)S(1)} %collective-permute-done.14.oth, f32[2,128,128]{2,1,0:T(8,128)S(1)} %fusion.perm), custom_call_target="tpu_custom_call" | custom-call | flops 500000000 | bytes 4194304 | tf_op jit(solution)/shard_map/pallas_call | solution.py:217
  112.9 0.8 copy-done.1
  113.7 0.6 copy-done.2
  114.3 4.2 %all-to-all-start.1 = ((f32[16,64,128]{2,1,0:T(8,128)}), f32[16,64,128]{2,1,0:T(8,128)S(1)}, u32[]{:S(2)}, u32[]{:S(2)}) async-start(f32[16,64,128]{2,1,0:T(8,128)} %copy-done.1), calls=%async_computation.1 | async-start | bytes 1048576 | tf_op jit(solution)/shard_map/all_to_all | solution.py:225
  118.6 1.0 broadcast_select_fusion.2
  119.6 3.9 %collective-permute-start.3 = (f32[256,256]{1,0:T(8,128)S(1)}, f32[256,256]{1,0:T(8,128)}, u32[]{:S(2)}, u32[]{:S(2)}) collective-permute-start(f32[256,256]{1,0:T(8,128)S(1)} %broadcast_select_fusion.2), channel_id=1, source_target_pairs={{0,32},{64,96},{128,160},{192,224},{256,288},{320,352},{384,416},{... | collective-permute-start | bytes 786440 | tf_op jit(solution)/shard_map/ppermute | solution.py:207
  123.6 5.2 %all-to-all-done.1.own = f32[16,64,128]{2,1,0:T(8,128)S(1)} async-done(((f32[16,64,128]{2,1,0:T(8,128)}), f32[16,64,128]{2,1,0:T(8,128)S(1)}, u32[]{:S(2)}, u32[]{:S(2)}) %all-to-all-start.1) | async-done | bytes 524320 | tf_op jit(solution)/shard_map/all_to_all | solution.py:225
  128.8 4.1 %collective-permute-start.15 = (f32[16,64,128]{2,1,0:T(8,128)S(1)}, f32[16,64,128]{2,1,0:T(8,128)S(1)}, u32[]{:S(2)}, u32[]{:S(2)}) collective-permute-start(f32[16,64,128]{2,1,0:T(8,128)S(1)} %all-to-all-done.1.own), channel_id=1, source_target_pairs={{0,1},{1,0},{2,3},{3,2},{4,5},{5,4},{6,7},{7,6},{8,9},{9,8},{10,11... | collective-permute-start | bytes 1572872 | tf_op jit(solution)/shard_map/ppermute | solution.py:229
  133.1 0.8 copy-done.3
  133.9 2.2 %shard_map.71 = (f32[1024,256]{1,0:T(8,128)S(1)}, f32[128,256]{1,0:T(8,128)S(1)}) custom-call(s32[64]{0:T(128)S(1)} %concatenate.6.meta, f32[1024,256]{1,0:T(8,128)S(1)} %copy-done, f32[256,256]{1,0:T(8,128)S(1)} %broadcast_select_fusion.3.rows, f32[1024,128]{1,0:T(8,128)S(1)} %get-tuple-element.12.plow, f32[128,128]{1,0:T(8,128)S(1)} %copy-done.3, ...), custom_call_target="tpu_custom_call" | custom-call | flops 500000000 | bytes 3145728 | tf_op jit(solution)/shard_map/pallas_call | solution.py:226
  136.1 2.5 %shard_map.72 = f32[1024,256]{1,0:T(8,128)} custom-call(s32[64]{0:T(128)S(1)} %concatenate.6.meta, f32[1024,256]{1,0:T(8,128)S(1)} %get-tuple-element.14.cur, f32[16,64,128]{2,1,0:T(8,128)S(1)} %all-to-all-done.1.own, f32[16,64,128]{2,1,0:T(8,128)S(1)} %collective-permute-done.15.oth, f32[128,256]{1,0:T(8,128)S(1)} %get-tuple-element.16.kept), custom_call_target="tpu_custom_call" | custom-call | flops 500000000 | bytes 3145728 | tf_op jit(solution)/shard_map/pallas_call | solution.py:230
  (43 shorter events, 0.6 us)
Async XLA Ops:
  2.0 9.6 %collective-permute-start.4 = (f32[8,8,8,256]{3,2,1,0:T(8,128)S(1)}, f32[8,8,8,256]{3,2,1,0:T(8,128)S(1)}, u32[]{:S(2)}, u32[]{:S(2)}) collective-permute-start(f32[8,8,8,256]{3,2,1,0:T(8,128)S(1)} %slice.85), channel_id=1, source_target_pairs={{0,1},{2,3},{4,5},{6,7},{8,9},{10,11},{12,13},{14,15},{16,17},{18,... | collective-permute-start | bytes 1572872 | tf_op jit(solution)/shard_map/ppermute | solution.py:195
  3.3 0.7 copy-start.4
  4.1 0.7 copy-start.7
  11.6 26.5 %copy-start.6 = (s32[2,64]{1,0:T(2,128)S(1)}, s32[2,64]{1,0:T(2,128)}, u32[]{:S(2)}) copy-start(s32[2,64]{1,0:T(2,128)} %param.9) | copy-start | bytes 1540
  11.7 37.0 %copy-start = (f32[1024,256]{1,0:T(8,128)S(1)}, f32[1024,256]{1,0:T(8,128)}, u32[]{:S(2)}) copy-start(f32[1024,256]{1,0:T(8,128)} %a.1) | copy-start | bytes 3145732
  11.7 14.1 %collective-permute-start.10 = (f32[8,8,256]{2,1,0:T(8,128)S(1)}, f32[8,8,256]{2,1,0:T(8,128)S(1)}, u32[]{:S(2)}, u32[]{:S(2)}) collective-permute-start(f32[8,8,256]{2,1,0:T(8,128)S(1)} %get-tuple-element.21), channel_id=1, source_target_pairs={{1,27},{0,10},{33,59},{32,42},{65,91},{64,74},{97,123},{96,106},{1... | collective-permute-start | bytes 196616 | tf_op jit(solution)/shard_map/ppermute | solution.py:200
  18.9 8.1 %collective-permute-start.11 = (f32[8,8,256]{2,1,0:T(8,128)S(1)}, f32[8,8,256]{2,1,0:T(8,128)S(1)}, u32[]{:S(2)}, u32[]{:S(2)}) collective-permute-start(f32[8,8,256]{2,1,0:T(8,128)S(1)} %get-tuple-element.20), channel_id=1, source_target_pairs={{1,29},{0,12},{33,61},{32,44},{65,93},{64,76},{97,125},{96,108},{1... | collective-permute-start | bytes 196616 | tf_op jit(solution)/shard_map/ppermute | solution.py:200
  20.2 8.2 %collective-permute-start.12 = (f32[8,8,256]{2,1,0:T(8,128)S(1)}, f32[8,8,256]{2,1,0:T(8,128)S(1)}, u32[]{:S(2)}, u32[]{:S(2)}) collective-permute-start(f32[8,8,256]{2,1,0:T(8,128)S(1)} %get-tuple-element.19), channel_id=1, source_target_pairs={{1,31},{0,14},{33,63},{32,46},{65,95},{64,78},{97,127},{96,110},{1... | collective-permute-start | bytes 196616 | tf_op jit(solution)/shard_map/ppermute | solution.py:200
  21.6 8.2 %collective-permute-start.5 = (f32[8,8,256]{2,1,0:T(8,128)S(1)}, f32[8,8,256]{2,1,0:T(8,128)S(1)}, u32[]{:S(2)}, u32[]{:S(2)}) collective-permute-start(f32[8,8,256]{2,1,0:T(8,128)S(1)} %get-tuple-element.18), channel_id=1, source_target_pairs={{1,17},{33,49},{65,81},{97,113},{129,145},{161,177},{193,209},{225... | collective-permute-start | bytes 196616 | tf_op jit(solution)/shard_map/ppermute | solution.py:200
  24.5 5.3 %collective-permute-start.6 = (f32[8,8,256]{2,1,0:T(8,128)S(1)}, f32[8,8,256]{2,1,0:T(8,128)S(1)}, u32[]{:S(2)}, u32[]{:S(2)}) collective-permute-start(f32[8,8,256]{2,1,0:T(8,128)S(1)} %get-tuple-element.25), channel_id=1, source_target_pairs={{1,19},{0,2},{33,51},{32,34},{65,83},{64,66},{97,115},{96,98},{129... | collective-permute-start | bytes 196616 | tf_op jit(solution)/shard_map/ppermute | solution.py:200
  25.8 4.0 %collective-permute-start.7 = (f32[8,8,256]{2,1,0:T(8,128)S(1)}, f32[8,8,256]{2,1,0:T(8,128)S(1)}, u32[]{:S(2)}, u32[]{:S(2)}) collective-permute-start(f32[8,8,256]{2,1,0:T(8,128)S(1)} %get-tuple-element.24), channel_id=1, source_target_pairs={{1,21},{0,4},{33,53},{32,36},{65,85},{64,68},{97,117},{96,100},{12... | collective-permute-start | bytes 196616 | tf_op jit(solution)/shard_map/ppermute | solution.py:200
  27.1 2.7 %collective-permute-start.8 = (f32[8,8,256]{2,1,0:T(8,128)S(1)}, f32[8,8,256]{2,1,0:T(8,128)S(1)}, u32[]{:S(2)}, u32[]{:S(2)}) collective-permute-start(f32[8,8,256]{2,1,0:T(8,128)S(1)} %get-tuple-element.23), channel_id=1, source_target_pairs={{1,23},{0,6},{33,55},{32,38},{65,87},{64,70},{97,119},{96,102},{12... | collective-permute-start | bytes 196616 | tf_op jit(solution)/shard_map/ppermute | solution.py:200
  28.4 2.6 %collective-permute-start.9 = (f32[8,8,256]{2,1,0:T(8,128)S(1)}, f32[8,8,256]{2,1,0:T(8,128)S(1)}, u32[]{:S(2)}, u32[]{:S(2)}) collective-permute-start(f32[8,8,256]{2,1,0:T(8,128)S(1)} %get-tuple-element.22), channel_id=1, source_target_pairs={{1,25},{0,8},{33,57},{32,40},{65,89},{64,72},{97,121},{96,104},{12... | collective-permute-start | bytes 196616 | tf_op jit(solution)/shard_map/ppermute | solution.py:200
  31.1 9.6 %collective-permute-start.13 = (f32[4,8,256]{2,1,0:T(8,128)S(1)}, f32[4,8,256]{2,1,0:T(8,128)S(1)}, u32[]{:S(2)}, u32[]{:S(2)}) collective-permute-start(f32[4,8,256]{2,1,0:T(8,128)S(1)} %dynamic-slice_bitcast_fusion), channel_id=1, source_target_pairs={{0,1},{1,0},{2,3},{3,2},{4,5},{5,4},{6,7},{7,6},{8,9},{9,8},{10,11... | collective-permute-start | bytes 98312 | tf_op jit(solution)/shard_map/ppermute | solution.py:202
  42.0 14.0 %all-to-all-start = ((f32[16,3,8,128]{3,2,1,0:T(8,128)}), f32[16,3,8,128]{3,2,1,0:T(8,128)S(1)}, u32[]{:S(2)}, u32[]{:S(2)}) async-start(f32[16,3,8,128]{3,2,1,0:T(8,128)} %get-tuple-element.11), calls=%async_computation | async-start | bytes 393216 | tf_op jit(solution)/shard_map/all_to_all | solution.py:211
  48.8 45.8 %collective-permute-start = (f32[256,256]{1,0:T(8,128)S(1)}, f32[256,256]{1,0:T(8,128)S(1)}, u32[]{:S(2)}, u32[]{:S(2)}) collective-permute-start(f32[256,256]{1,0:T(8,128)S(1)} %slice.70), channel_id=1, source_target_pairs={{0,256},{1,257},{2,258},{3,259},{4,260},{5,261},{6,262},{7,263},{8... | collective-permute-start | bytes 786440 | tf_op jit(solution)/shard_map/ppermute | solution.py:207
  84.2 20.7 %collective-permute-start.14 = (f32[16,14,8,128]{3,2,1,0:T(8,128)S(1)}, f32[16,14,8,128]{3,2,1,0:T(8,128)S(1)}, u32[]{:S(2)}, u32[]{:S(2)}) collective-permute-start(f32[16,14,8,128]{3,2,1,0:T(8,128)S(1)} %bitcast.71), channel_id=1, source_target_pairs={{0,1},{1,0},{2,3},{3,2},{4,5},{5,4},{6,7},{7,6},{8,9},{9,8},{10,11... | collective-permute-start | bytes 2752520 | tf_op jit(solution)/shard_map/ppermute | solution.py:215
  94.6 7.6 %collective-permute-start.1 = (f32[256,256]{1,0:T(8,128)S(1)}, f32[256,256]{1,0:T(8,128)S(1)}, u32[]{:S(2)}, u32[]{:S(2)}) collective-permute-start(f32[256,256]{1,0:T(8,128)S(1)} %broadcast_select_fusion), channel_id=1, source_target_pairs={{0,128},{256,384},{1,129},{257,385},{2,130},{258,386},{3,131},{259... | collective-permute-start | bytes 786440 | tf_op jit(solution)/shard_map/ppermute | solution.py:207
  96.6 0.7 copy-start.5
  103.0 15.7 %collective-permute-start.2 = (f32[256,256]{1,0:T(8,128)}, f32[256,256]{1,0:T(8,128)}, u32[]{:S(2)}, u32[]{:S(2)}) collective-permute-start(f32[256,256]{1,0:T(8,128)} %broadcast_select_fusion.1), channel_id=1, source_target_pairs={{0,64},{128,192},{256,320},{384,448},{1,65},{129,193},{257,321},{3... | collective-permute-start | bytes 786440 | tf_op jit(solution)/shard_map/ppermute | solution.py:207
  112.9 0.8 copy-start.1
  113.7 0.6 copy-start.2
  114.3 14.5 %all-to-all-start.1 = ((f32[16,64,128]{2,1,0:T(8,128)}), f32[16,64,128]{2,1,0:T(8,128)S(1)}, u32[]{:S(2)}, u32[]{:S(2)}) async-start(f32[16,64,128]{2,1,0:T(8,128)} %copy-done.1), calls=%async_computation.1 | async-start | bytes 1048576 | tf_op jit(solution)/shard_map/all_to_all | solution.py:225
  119.6 13.4 %collective-permute-start.3 = (f32[256,256]{1,0:T(8,128)S(1)}, f32[256,256]{1,0:T(8,128)}, u32[]{:S(2)}, u32[]{:S(2)}) collective-permute-start(f32[256,256]{1,0:T(8,128)S(1)} %broadcast_select_fusion.2), channel_id=1, source_target_pairs={{0,32},{64,96},{128,160},{192,224},{256,288},{320,352},{384,416},{... | collective-permute-start | bytes 786440 | tf_op jit(solution)/shard_map/ppermute | solution.py:207
  128.8 7.3 %collective-permute-start.15 = (f32[16,64,128]{2,1,0:T(8,128)S(1)}, f32[16,64,128]{2,1,0:T(8,128)S(1)}, u32[]{:S(2)}, u32[]{:S(2)}) collective-permute-start(f32[16,64,128]{2,1,0:T(8,128)S(1)} %all-to-all-done.1.own), channel_id=1, source_target_pairs={{0,1},{1,0},{2,3},{3,2},{4,5},{5,4},{6,7},{7,6},{8,9},{9,8},{10,11... | collective-permute-start | bytes 1572872 | tf_op jit(solution)/shard_map/ppermute | solution.py:229
  133.0 0.8 copy-start.3

commit v2 on v1

v2 whole, which is shorter than its diff:
```python
import jax
import jax.numpy as jnp
from jax import lax
from jax.experimental import pallas as pl
from jax.experimental.pallas import tpu as pltpu
from jax.sharding import Mesh
from jax.sharding import PartitionSpec as P

SWEEPS = 3
W = 128
NP = 16
NZ = 16
HI = lax.Precision.HIGHEST


def dot(a, b):
    return jnp.dot(a, b, precision=HI, preferred_element_type=jnp.float32)


def order(perms, k):
    hit = lax.broadcasted_iota(jnp.int32, (W, W), 0) == perms[k : k + 1, :]
    return jnp.where(hit, 1.0, 0.0).astype(jnp.float32).T


def refine(pivot):
    row = lax.broadcasted_iota(jnp.int32, (W, W), 0)
    col = lax.broadcasted_iota(jnp.int32, (W, W), 1)
    two = jnp.where(row == col, 2.0, 0.0).astype(jnp.float32)
    scale = W * (jnp.mean(pivot * pivot) + 1e-6)
    approx = pivot.T / scale
    for _ in range(SWEEPS):
        approx = dot(approx, two - dot(pivot, approx))
    return approx


def index_kernel(dest, row_mask, col_mask, meta, src):
    me = lax.axis_index("x") * 4 + lax.axis_index("y")
    z = lax.axis_index("z")
    core = lax.axis_index("core")

    def invert(i, carry):
        src[0, dest[0, i]] = i
        src[1, dest[1, i]] = i
        return carry

    lax.fori_loop(0, W, invert, 0, unroll=8)

    def row_ok(k, i):
        return ((row_mask[k, i] == 1) & (i > k)).astype(jnp.int32)

    def col_ok(k, j):
        return ((col_mask[k, j] == 1) & (j > k)).astype(jnp.int32)

    head = src[0, 1]
    block = (z * 2 + core) * 2
    meta[0] = core
    meta[1] = (me == 0).astype(jnp.int32)
    meta[2] = col_ok(0, 1)
    meta[3] = row_ok(0, head)
    meta[4] = lax.shift_right_logical(head, 3)
    meta[5] = (core == (z >= 8).astype(jnp.int32)).astype(jnp.int32)
    for k in range(2):
        for j in range(2):
            meta[64 + 2 * k + j] = col_ok(k, block + j)
    for slot in range(8):
        here = me * 8 + slot
        meta[8 + slot] = row_ok(0, here)
        meta[16 + slot] = row_ok(1, here)
        meta[24 + slot] = row_ok(0, src[0, here])
        meta[32 + slot] = lax.shift_right_logical(dest[1, here], 3)
        meta[40 + slot] = lax.shift_right_logical(src[1, here], 3)
        meta[48 + slot] = lax.shift_right_logical(dest[0, here], 3)
        meta[56 + slot] = lax.shift_right_logical(src[0, here], 3)


def route_kernel(meta, share, passed, half, out):
    core = meta[0]
    kept = meta[5] == 1
    out[...] = jnp.zeros_like(out)
    for j in range(4):
        block = jnp.where(kept, jnp.where(core == 0, share[j, 0], share[j, 1]), passed[j])
        half[j] = block[:, :W]
        half[4 + j] = block[:, W:]
        out[meta[48 + 2 * j + core], 0] = block[:, :W]
        if j == 0:
            out[:, 1] = jnp.broadcast_to(block[None, :, :W], (NP, 8, W))
            out[:, 2] = jnp.broadcast_to(block[None, :, W:], (NP, 8, W))


def pack_kernel(meta, half, got, out):
    core = meta[0]
    out[:8] = half[...]
    for j in range(4):
        out[8 + j] = got[meta[56 + 2 * j + core], 0]
    out[12] = jnp.where(core == 0, got[0, 1], got[meta[4], 1])
    out[13] = got[0, 2]


def factor_kernel(meta, own, oth, perms, lpan, plow, send, lsrc):
    core = meta[0]
    first = core == 0

    def tile(ref, t):
        return ref[:, t].reshape(W, W)

    def even(t):
        return jnp.where(first, tile(own, t), tile(oth, t))

    def odd(t):
        return jnp.where(first, tile(oth, t), tile(own, t))

    def flag(i):
        return meta[i].astype(jnp.float32)

    inv0 = refine(dot(order(perms, 0), even(12)))
    kept01 = dot(order(perms, 0), even(13)) * flag(2)
    low_src = dot(odd(12), inv0) * flag(3)
    lsrc[...] = low_src
    inv1 = refine(dot(order(perms, 1), odd(13) - dot(low_src, kept01)))
    for ref, parity in ((own, core), (oth, 1 - core)):
        col0 = jnp.concatenate([tile(ref, j) for j in range(4)], axis=0)
        ext0 = jnp.concatenate([tile(ref, 8 + j) for j in range(4)], axis=0)
        col1 = jnp.concatenate([tile(ref, 4 + j) for j in range(4)], axis=0)
        low0 = dot(col0, inv0)
        ext0 = dot(ext0, inv0)
        ext0 = jnp.concatenate(
            [ext0[j * W : (j + 1) * W] * flag(24 + 2 * j + parity) for j in range(4)], axis=0
        )
        low1 = dot(col1 - dot(ext0, kept01), inv1)
        for j in range(4):
            slot = 2 * j + parity
            here = pl.ds(pl.multiple_of(slot * W, W), W)
            part = slice(j * W, (j + 1) * W)
            lpan[here, :W] = low0[part] * flag(8 + slot)
            lpan[here, W:] = low1[part] * flag(16 + slot)
            plow[here, :] = ext0[part]
    for slot in range(8):
        half = pl.ds(pl.multiple_of(slot * W + core * (W // 2), W // 2), W // 2)
        send[meta[32 + slot]] = lpan[half, W:]


def first_kernel(meta, a, rows, plow, lsrc, perms, cur, kept):
    def masked(block, k):
        return jnp.concatenate(
            [block[:, j * W : (j + 1) * W] * meta[64 + 2 * k + j].astype(jnp.float32) for j in range(2)],
            axis=1,
        )

    up0 = dot(order(perms, 0), rows[:W])
    kept0 = masked(up0, 0)
    up1 = dot(order(perms, 1), rows[W:] - dot(lsrc[...], kept0))
    kept[...] = masked(up1, 1)
    prod = dot(plow[...], kept0)
    cur[...] = a[...] - prod

    @pl.when(meta[1] == 1)
    def _():
        cur[:W] = up0 - prod[:W]
        cur[W : 2 * W] = up1


def second_kernel(meta, cur, own, oth, kept, out, low):
    core = meta[0]
    h = W // 2
    for slot in range(8):
        dev = meta[40 + slot]
        low[pl.ds(pl.multiple_of(slot * W + core * h, h), h), :] = own[dev]
        low[pl.ds(pl.multiple_of(slot * W + (1 - core) * h, h), h), :] = oth[dev]
    out[...] = cur[...] - dot(low[...], kept[...])


def f32(*shape):
    return jax.ShapeDtypeStruct(shape, jnp.float32)


def call(kernel, out_shape, n_in, scratch=(), flops=0, moved=0):
    smem = pl.BlockSpec(memory_space=pltpu.SMEM)
    vmem = pl.BlockSpec(memory_space=pltpu.VMEM)
    multi = isinstance(out_shape, (tuple, list))
    return pl.pallas_call(
        kernel,
        out_shape=out_shape,
        in_specs=[smem] + [vmem] * n_in,
        out_specs=[vmem] * len(out_shape) if multi else vmem,
        scratch_shapes=list(scratch),
        compiler_params=pltpu.CompilerParams(vmem_limit_bytes=16 * 2**20),
        cost_estimate=pl.CostEstimate(flops=flops, bytes_accessed=moved, transcendentals=0),
    )


def shards(a, row_perms, dest_rows, row_mask, col_mask):
    z = lax.axis_index("z")
    core = lax.axis_index("core")
    smem = pl.BlockSpec(memory_space=pltpu.SMEM)
    meta = pl.pallas_call(
        index_kernel,
        out_shape=jax.ShapeDtypeStruct((W,), jnp.int32),
        in_specs=[smem] * 3,
        out_specs=smem,
        scratch_shapes=[pltpu.SMEM((2, W), jnp.int32)],
    )(dest_rows, row_mask, col_mask)

    rows = lax.all_gather(a[: 2 * W], "x", axis=0, tiled=True)[: 2 * W]

    cut = a.reshape(8, NZ, 8, 2 * W)
    over = lax.ppermute(cut[:, 8:].transpose(1, 0, 2, 3), "core", [(0, 1)])
    pieces = [jnp.where(core == 0, cut[:, step % 8], over[8 - step]) for step in range(1, 9)]
    pieces, meta = lax.optimization_barrier((pieces, meta))
    share = jnp.where((z == 0) & (core == 0), pieces[7], jnp.zeros_like(pieces[7]))
    for step in range(1, 9):
        pairs = [(1, 2 * (NZ - step) + 1)]
        if step < 8:
            pairs.append((0, 2 * step))
        share = share + lax.ppermute(pieces[step - 1], ("z", "core"), pairs)
    share = share.reshape(4, 2, 8, 2 * W)
    passed = lax.ppermute(
        lax.dynamic_index_in_dim(share, 1 - core, 1, keepdims=False), "core", [(0, 1), (1, 0)]
    )

    half, out0 = call(route_kernel, (f32(8, 8, W), f32(NP, 3, 8, W)), 2, moved=2**19)(meta, share, passed)
    got0 = lax.all_to_all(out0, ("x", "y"), 0, 0, tiled=True)
    payload = call(pack_kernel, f32(14, 8, W), 2, moved=2**19)(meta, half, got0)

    payload, rows = lax.optimization_barrier((payload, rows))
    rows = lax.all_gather(rows, "y", axis=0, tiled=True)[: 2 * W]
    own = lax.all_gather(payload, "z", axis=0, tiled=False)
    oth = lax.ppermute(own, "core", [(0, 1), (1, 0)])
    oth, rows = lax.optimization_barrier((oth, rows))

    lpan, plow, send, lsrc = call(
        factor_kernel,
        (f32(8 * W, 2 * W), f32(8 * W, W), f32(NP, W // 2, W), f32(W, W)),
        3,
        flops=5 * 10**8,
        moved=4 * 2**20,
    )(meta, own, oth, row_perms)

    got1 = lax.all_to_all(send, ("x", "y"), 0, 0, tiled=True)
    cur, kept = call(
        first_kernel, (f32(8 * W, 2 * W), f32(W, 2 * W)), 5, flops=5 * 10**8, moved=3 * 2**20
    )(meta, a, rows, plow, lsrc, row_perms)
    oth1 = lax.ppermute(got1, "core", [(0, 1), (1, 0)])
    schur = call(
        second_kernel,
        f32(8 * W, 2 * W),
        4,
        scratch=(pltpu.VMEM((8 * W, W), jnp.float32),),
        flops=5 * 10**8,
        moved=3 * 2**20,
    )(meta, cur, got1, oth1, kept)
    return schur, lpan


def solution(mesh):
    fine = Mesh(mesh.devices.reshape(4, 4, NZ, 2), ("x", "y", "z", "core"))
    placed = (P(("x", "y"), ("z", "core")), P(), P(), P(), P())
    return jax.shard_map(
        shards,
        mesh=fine,
        in_specs=placed,
        out_specs=(P(("x", "y"), ("z", "core")), P(("x", "y"), None)),
        check_vma=False,
    )
```

time: 140 us -> 134 us (0.957)
  blocking collectives: 27.7 us -> 55.1 us
  starting transfers between devices: 59 us -> 32.8 us
  waiting for transfers between devices: 20.3 us -> 9.87 us
  between operations: 5.76 us -> 14.3 us
  local copies, waits for them, and re-layouts: 8.86 us -> 5.51 us
  other arithmetic: 2.46 us -> 0.1 us
  Pallas kernels: 14.5 us -> 15.9 us
    all_to_all x0 -> x2, blocking collectives: none -> 26.6 us  [the longest x1 13.6 us: shards(): got0 = lax.all_to_all(out0, ('x', 'y'), 0, 0, tiled=True)]
    ppermute x14 -> x10, starting transfers between devices: 33.6 us -> 18.9 us  [the longest x8 15.7 us: shards(): share = share + lax.ppermute(pieces[step - 1], ('z', 'core'), pairs)]
    all_to_all x2 -> x0, starting transfers between devices: 11 us -> none  [the longest x1 6.75 us: shards(): got0 = lax.all_to_all(out0, 'prow', 0, 0, tiled=True)]
    all_to_all x2 -> x0, waiting for transfers between devices: 7.56 us -> none  [the longest x1 5.2 us: shards(): got1 = lax.all_to_all(send, 'prow', 0, 0, tiled=True)]
    unnamed x18 -> x6, local copies, waits for them, and re-layouts: 4.3 us -> 0.02 us
    ppermute x14 -> x10, waiting for transfers between devices: 12.8 us -> 8.71 us  [the longest x1 6.26 us: shards(): over = lax.ppermute(cut[:, 8:].transpose(1, 0, 2, 3), 'core', [(0, 1)])]
    slice x6 -> x3, local copies, waits for them, and re-layouts: 1.23 us -> 4.39 us  [the longest x2 3.42 us: shards(): rows = lax.all_gather(a[:2 * W], 'x', axis=0, tiled=True)[:2 * W]]
    select_n x8 -> x1, other arithmetic: 2.12 us -> 0.07 us  [shards(): jnp.where(core == 0, cut[:, step % 8], over[8 - step])]
  transfers between devices with their start and end apart: 18 -> 14, of which waited for: 5 -> 4; matrix products, arithmetic and copies ran while one was open for 4% -> 2% of each run, Pallas kernels for 8% -> 4%
where the time goes in v2:
time: 134 us
  blocking collectives  55.1 us (41%)
  starting transfers between devices  32.8 us (24%)
  Pallas kernels  15.9 us (12%)
  between operations  14.3 us (11%)
  waiting for transfers between devices  9.87 us (7%)
  local copies, waits for them, and re-layouts  5.51 us (4%)
    all_gather x1, blocking collectives, shards(): own = lax.all_gather(payload, 'z', axis=0, tiled=False)  28.5 us
    ppermute x8, starting transfers between devices, shards(): share = share + lax.ppermute(pieces[step - 1], ('z', 'core'), pairs)  15.7 us
    all_to_all x1, blocking collectives, shards(): got0 = lax.all_to_all(out0, ('x', 'y'), 0, 0, tiled=True)  13.6 us
    all_to_all x1, blocking collectives, shards(): got1 = lax.all_to_all(send, ('x', 'y'), 0, 0, tiled=True)  13.1 us
    ppermute x1, starting transfers between devices, shards(): oth = lax.ppermute(own, 'core', [(0, 1), (1, 0)])  9.96 us
    pallas_call x1, Pallas kernels, shards(): call(factor_kernel, (f32(8 * W, 2 * W), f32(8 * W, W), f32(NP, W // 2, W)...  7.98 us
    ppermute x1, waiting for transfers between devices, shards(): over = lax.ppermute(cut[:, 8:].transpose(1, 0, 2, 3), 'core', [(0, 1)])  6.26 us
    ppermute x1, starting transfers between devices, shards(): oth1 = lax.ppermute(got1, 'core', [(0, 1), (1, 0)])  3.85 us
  transfers between devices with their start and end apart: 14, of which 4 were waited for; matrix products, arithmetic and copies ran while one was open for 2% of the time, Pallas kernels for 4%

profile of v2, /device:TPU:1, one launch (start us, length us, event | category | flops | bytes accessed | tf_op | source)
XLA Modules:
  0.0 133.7 jit_solution(5375910633602631343)
XLA Ops:
  7.2 0.0 copy-start
  7.2 0.0 all-gather.4.cloned.1.call-start
  7.2 1.7 %slice.77 = f32[256,256]{1,0:T(8,128)} slice(f32[1024,256]{1,0:T(8,128)} %a.1), slice={[0:256], [0:256]} | slice | bytes 524288 | tf_op jit(solution)/shard_map/slice | solution.py:203
  9.0 0.0 all-gather.4.cloned.1.call-update
  9.0 0.0 all-gather.6.cloned.1.call-start
  9.0 1.1 copy_bitcast_fusion
  10.1 1.3 collective-permute-start
  11.4 2.0 %shard_map.68.meta = s32[128]{0:T(128)} custom-call(s32[2,128]{1,0:T(2,128)} %dest.1, s32[2,128]{1,0:T(2,128)} %row_mask.1, s32[2,64]{1,0:T(2,128)} %col_mask.1), custom_call_target="tpu_custom_call" | custom-call | tf_op jit(solution)/shard_map/pallas_call | solution.py:195
  13.4 6.3 %collective-permute-done = f32[8,8,8,256]{3,2,1,0:T(8,128)S(1)} collective-permute-done((f32[8,8,8,256]{3,2,1,0:T(8,128)S(1)}, f32[8,8,8,256]{3,2,1,0:T(8,128)S(1)}, u32[]{:S(2)}, u32[]{:S(2)}) %collective-permute-start) | collective-permute-done | bytes 524320 | tf_op jit(solution)/shard_map/ppermute | solution.py:206
  19.7 0.0 copy-done
  19.7 0.1 fusion
  19.8 6.2 %collective-permute-start.1 = (f32[8,8,256]{2,1,0:T(8,128)S(1)}, f32[8,8,256]{2,1,0:T(8,128)S(1)}, u32[]{:S(2)}, u32[]{:S(2)}) collective-permute-start(f32[8,8,256]{2,1,0:T(8,128)S(1)} %get-tuple-element.25), channel_id=1, source_target_pairs={{1,31},{0,2},{33,63},{32,34},{65,95},{64,66},{97,127},{96,98},{129... | collective-permute-start | bytes 196616 | tf_op jit(solution)/shard_map/ppermute | solution.py:214
  26.0 1.3 collective-permute-start.2
  27.3 1.3 collective-permute-start.3
  28.6 1.3 collective-permute-start.4
  29.9 1.8 %collective-permute-start.5 = (f32[8,8,256]{2,1,0:T(8,128)S(1)}, f32[8,8,256]{2,1,0:T(8,128)S(1)}, u32[]{:S(2)}, u32[]{:S(2)}) collective-permute-start(f32[8,8,256]{2,1,0:T(8,128)S(1)} %get-tuple-element.29), channel_id=1, source_target_pairs={{1,23},{0,10},{33,55},{32,42},{65,87},{64,74},{97,119},{96,106},{1... | collective-permute-start | bytes 196616 | tf_op jit(solution)/shard_map/ppermute | solution.py:214
  31.7 0.0 collective-permute-done.1
  31.7 1.3 collective-permute-start.6
  33.0 0.0 collective-permute-done.2
  33.0 1.3 collective-permute-start.7
  34.3 0.0 collective-permute-done.3
  34.3 1.3 collective-permute-start.8
  35.6 0.0 collective-permute-done.4
  35.6 0.0 collective-permute-done.5
  35.6 0.0 collective-permute-done.6
  35.6 0.0 collective-permute-done.7
  35.6 1.3 collective-permute-done.8
  36.9 0.0 copy-start.1
  37.0 1.9 %collective-permute-start.9 = (f32[4,8,256]{2,1,0:T(8,128)S(1)}, f32[4,8,256]{2,1,0:T(8,128)S(1)}, u32[]{:S(2)}, u32[]{:S(2)}) collective-permute-start(f32[4,8,256]{2,1,0:T(8,128)S(1)} %dynamic-slice_bitcast_fusion), channel_id=1, source_target_pairs={{0,1},{1,0},{2,3},{3,2},{4,5},{5,4},{6,7},{7,6},{8,9},{9,8},{10,11... | collective-permute-start | bytes 98312 | tf_op jit(solution)/shard_map/ppermute | solution.py:216
  38.9 1.2 collective-permute-done.9.passed
  40.1 0.0 copy-done.1
  40.1 0.6 shard_map.69
  40.7 13.6 %all_to_all.10.got = f32[16,3,8,128]{3,2,1,0:T(8,128)S(1)} all-to-all(f32[16,3,8,128]{3,2,1,0:T(8,128)S(1)} %get-tuple-element.33), channel_id=1, replica_groups=mesh['x'=4,'y'=4,'z'=16,'core'=2] {'x','y'}, dimensions={0} | all-to-all | bytes 393216 | tf_op jit(solution)/shard_map/all_to_all | solution.py:221
  54.2 0.6 shard_map.70
  54.8 0.0 all-gather.4.cloned.1.call-done
  54.8 1.7 %slice.97 = f32[256,256]{1,0:T(8,128)} slice(f32[1024,256]{1,0:T(8,128)} %all-gather.4.cloned.1.call-done), slice={[0:256], [0:256]} | slice | bytes 524288 | tf_op jit(solution)/shard_map/slice | solution.py:203
  56.5 0.0 all-gather.6.cloned.1.call-update
  56.5 28.5 %all-gather = f32[224,8,128]{2,1,0:T(8,128)S(1)} all-gather(f32[14,8,128]{2,1,0:T(8,128)S(1)} %shard_map.70), channel_id=2, replica_groups=mesh['x'=4,'y'=4,'z'=16,'core'=2] {'z'}, dimensions={0}, use_global_device_ids=true | all-gather | bytes 974848 | tf_op jit(solution)/shard_map/all_gather | solution.py:226
  85.0 10.0 %collective-permute-start.10 = (f32[16,14,8,128]{3,2,1,0:T(8,128)S(1)}, f32[16,14,8,128]{3,2,1,0:T(8,128)S(1)}, u32[]{:S(2)}, u32[]{:S(2)}) collective-permute-start(f32[16,14,8,128]{3,2,1,0:T(8,128)S(1)} %bitcast.89), channel_id=1, source_target_pairs={{0,1},{1,0},{2,3},{3,2},{4,5},{5,4},{6,7},{7,6},{8,9},{9,8},{10,11... | collective-permute-start | bytes 2752520 | tf_op jit(solution)/shard_map/ppermute | solution.py:227
  95.0 0.0 all-gather.6.cloned.1.call-done
  95.0 1.0 slice.98.rows
  96.0 1.1 collective-permute-done.10.oth
  97.0 8.0 %shard_map.71 = (f32[1024,256]{1,0:T(8,128)}, f32[1024,128]{1,0:T(8,128)S(1)}, f32[16,64,128]{2,1,0:T(8,128)S(1)}, f32[128,128]{1,0:T(8,128)S(1)}) custom-call(s32[128]{0:T(128)S(1)} %copy-done.1, f32[16,14,8,128]{3,2,1,0:T(8,128)S(1)} %bitcast.90, f32[16,14,8,128]{3,2,1,0:T(8,128)S(1)} %collective-permute-done.10.oth, s32[2,128]{1,0:T(2,128)S(1)} %copy-done.2), custom_call_target="tpu_custom_call" | custom-call | flops 500000000 | bytes 4194304 | tf_op jit(solution)/shard_map/pallas_call | solution.py:230
  105.0 13.1 %all_to_all.11.own = f32[16,64,128]{2,1,0:T(8,128)S(1)} all-to-all(f32[16,64,128]{2,1,0:T(8,128)S(1)} %get-tuple-element.41), channel_id=1, replica_groups=mesh['x'=4,'y'=4,'z'=16,'core'=2] {'x','y'}, dimensions={0} | all-to-all | bytes 1048576 | tf_op jit(solution)/shard_map/all_to_all | solution.py:238
  118.1 3.9 %collective-permute-start.11 = (f32[16,64,128]{2,1,0:T(8,128)S(1)}, f32[16,64,128]{2,1,0:T(8,128)S(1)}, u32[]{:S(2)}, u32[]{:S(2)}) collective-permute-start(f32[16,64,128]{2,1,0:T(8,128)S(1)} %all_to_all.11.own), channel_id=1, source_target_pairs={{0,1},{1,0},{2,3},{3,2},{4,5},{5,4},{6,7},{7,6},{8,9},{9,8},{10,11... | collective-permute-start | bytes 1572872 | tf_op jit(solution)/shard_map/ppermute | solution.py:242
  122.0 2.3 %shard_map.72 = (f32[1024,256]{1,0:T(8,128)S(1)}, f32[128,256]{1,0:T(8,128)S(1)}) custom-call(s32[128]{0:T(128)S(1)} %copy-done.1, f32[1024,256]{1,0:T(8,128)S(1)} %copy-done, f32[256,256]{1,0:T(8,128)S(1)} %slice.98.rows, f32[1024,128]{1,0:T(8,128)S(1)} %get-tuple-element.38.plow, f32[128,128]{1,0:T(8,128)S(1)} %get-tuple-element.39.lsrc, ...), custom_call_target="tpu_custom_call" | custom-call | flops 500000000 | bytes 3145728 | tf_op jit(solution)/shard_map/pallas_call | solution.py:239
  124.3 0.0 collective-permute-done.11.oth
  124.3 2.5 %shard_map.73 = f32[1024,256]{1,0:T(8,128)} custom-call(s32[128]{0:T(128)S(1)} %copy-done.1, f32[1024,256]{1,0:T(8,128)S(1)} %get-tuple-element.40.cur, f32[16,64,128]{2,1,0:T(8,128)S(1)} %all_to_all.11.own, f32[16,64,128]{2,1,0:T(8,128)S(1)} %collective-permute-done.11.oth, f32[128,256]{1,0:T(8,128)S(1)} %get-tuple-element.42.kept), custom_call_target="tpu_custom_call" | custom-call | flops 500000000 | bytes 3145728 | tf_op jit(solution)/shard_map/pallas_call | solution.py:243
  (4 shorter events, 0.1 us)
Async XLA Ops:
  7.2 12.5 %copy-start = (f32[1024,256]{1,0:T(8,128)S(1)}, f32[1024,256]{1,0:T(8,128)}, u32[]{:S(2)}) copy-start(f32[1024,256]{1,0:T(8,128)} %a.1) | copy-start | bytes 3145732
  7.2 47.6 %all-gather.4.cloned.1.call-start = ((), (), s32[]{:S(2)}) async-start(), calls=%async_computation.2 | async-start | bytes 1310720 | tf_op jit(solution)/shard_map/all_gather | solution.py:203
  9.0 86.0 %all-gather.6.cloned.1.call-start = ((), (), s32[]{:S(2)}) async-start(), calls=%async_computation.3 | async-start | bytes 1310720 | tf_op jit(solution)/shard_map/all_gather | solution.py:225
  10.1 9.6 %collective-permute-start = (f32[8,8,8,256]{3,2,1,0:T(8,128)S(1)}, f32[8,8,8,256]{3,2,1,0:T(8,128)S(1)}, u32[]{:S(2)}, u32[]{:S(2)}) collective-permute-start(f32[8,8,8,256]{3,2,1,0:T(8,128)S(1)} %copy_bitcast_fusion), channel_id=1, source_target_pairs={{0,1},{2,3},{4,5},{6,7},{8,9},{10,11},{12,13},{14,15},{16,17},{18,... | collective-permute-start | bytes 1572872 | tf_op jit(solution)/shard_map/ppermute | solution.py:206
  19.8 11.9 %collective-permute-start.1 = (f32[8,8,256]{2,1,0:T(8,128)S(1)}, f32[8,8,256]{2,1,0:T(8,128)S(1)}, u32[]{:S(2)}, u32[]{:S(2)}) collective-permute-start(f32[8,8,256]{2,1,0:T(8,128)S(1)} %get-tuple-element.25), channel_id=1, source_target_pairs={{1,31},{0,2},{33,63},{32,34},{65,95},{64,66},{97,127},{96,98},{129... | collective-permute-start | bytes 196616 | tf_op jit(solution)/shard_map/ppermute | solution.py:214
  26.0 7.0 %collective-permute-start.2 = (f32[8,8,256]{2,1,0:T(8,128)S(1)}, f32[8,8,256]{2,1,0:T(8,128)S(1)}, u32[]{:S(2)}, u32[]{:S(2)}) collective-permute-start(f32[8,8,256]{2,1,0:T(8,128)S(1)} %get-tuple-element.26), channel_id=1, source_target_pairs={{1,29},{0,4},{33,61},{32,36},{65,93},{64,68},{97,125},{96,100},{12... | collective-permute-start | bytes 196616 | tf_op jit(solution)/shard_map/ppermute | solution.py:214
  27.3 7.0 %collective-permute-start.3 = (f32[8,8,256]{2,1,0:T(8,128)S(1)}, f32[8,8,256]{2,1,0:T(8,128)S(1)}, u32[]{:S(2)}, u32[]{:S(2)}) collective-permute-start(f32[8,8,256]{2,1,0:T(8,128)S(1)} %get-tuple-element.27), channel_id=1, source_target_pairs={{1,27},{0,6},{33,59},{32,38},{65,91},{64,70},{97,123},{96,102},{12... | collective-permute-start | bytes 196616 | tf_op jit(solution)/shard_map/ppermute | solution.py:214
  28.6 7.0 %collective-permute-start.4 = (f32[8,8,256]{2,1,0:T(8,128)S(1)}, f32[8,8,256]{2,1,0:T(8,128)S(1)}, u32[]{:S(2)}, u32[]{:S(2)}) collective-permute-start(f32[8,8,256]{2,1,0:T(8,128)S(1)} %get-tuple-element.28), channel_id=1, source_target_pairs={{1,25},{0,8},{33,57},{32,40},{65,89},{64,72},{97,121},{96,104},{12... | collective-permute-start | bytes 196616 | tf_op jit(solution)/shard_map/ppermute | solution.py:214
  29.9 5.7 %collective-permute-start.5 = (f32[8,8,256]{2,1,0:T(8,128)S(1)}, f32[8,8,256]{2,1,0:T(8,128)S(1)}, u32[]{:S(2)}, u32[]{:S(2)}) collective-permute-start(f32[8,8,256]{2,1,0:T(8,128)S(1)} %get-tuple-element.29), channel_id=1, source_target_pairs={{1,23},{0,10},{33,55},{32,42},{65,87},{64,74},{97,119},{96,106},{1... | collective-permute-start | bytes 196616 | tf_op jit(solution)/shard_map/ppermute | solution.py:214
  31.7 4.0 %collective-permute-start.6 = (f32[8,8,256]{2,1,0:T(8,128)S(1)}, f32[8,8,256]{2,1,0:T(8,128)S(1)}, u32[]{:S(2)}, u32[]{:S(2)}) collective-permute-start(f32[8,8,256]{2,1,0:T(8,128)S(1)} %get-tuple-element.30), channel_id=1, source_target_pairs={{1,21},{0,12},{33,53},{32,44},{65,85},{64,76},{97,117},{96,108},{1... | collective-permute-start | bytes 196616 | tf_op jit(solution)/shard_map/ppermute | solution.py:214
  33.0 2.7 %collective-permute-start.7 = (f32[8,8,256]{2,1,0:T(8,128)S(1)}, f32[8,8,256]{2,1,0:T(8,128)S(1)}, u32[]{:S(2)}, u32[]{:S(2)}) collective-permute-start(f32[8,8,256]{2,1,0:T(8,128)S(1)} %get-tuple-element.31), channel_id=1, source_target_pairs={{1,19},{0,14},{33,51},{32,46},{65,83},{64,78},{97,115},{96,110},{1... | collective-permute-start | bytes 196616 | tf_op jit(solution)/shard_map/ppermute | solution.py:214
  34.3 2.6 %collective-permute-start.8 = (f32[8,8,256]{2,1,0:T(8,128)S(1)}, f32[8,8,256]{2,1,0:T(8,128)S(1)}, u32[]{:S(2)}, u32[]{:S(2)}) collective-permute-start(f32[8,8,256]{2,1,0:T(8,128)S(1)} %get-tuple-element.24), channel_id=1, source_target_pairs={{1,17},{33,49},{65,81},{97,113},{129,145},{161,177},{193,209},{225... | collective-permute-start | bytes 196616 | tf_op jit(solution)/shard_map/ppermute | solution.py:214
  36.9 3.1 %copy-start.1 = (s32[128]{0:T(128)S(1)}, s32[128]{0:T(128)}, u32[]{:S(2)}) copy-start(s32[128]{0:T(128)} %shard_map.68.meta) | copy-start | bytes 1540
  37.0 3.1 %collective-permute-start.9 = (f32[4,8,256]{2,1,0:T(8,128)S(1)}, f32[4,8,256]{2,1,0:T(8,128)S(1)}, u32[]{:S(2)}, u32[]{:S(2)}) collective-permute-start(f32[4,8,256]{2,1,0:T(8,128)S(1)} %dynamic-slice_bitcast_fusion), channel_id=1, source_target_pairs={{0,1},{1,0},{2,3},{3,2},{4,5},{5,4},{6,7},{7,6},{8,9},{9,8},{10,11... | collective-permute-start | bytes 98312 | tf_op jit(solution)/shard_map/ppermute | solution.py:216
  85.0 12.1 %copy-start.2 = (s32[2,128]{1,0:T(2,128)S(1)}, s32[2,128]{1,0:T(2,128)}, u32[]{:S(2)}) copy-start(s32[2,128]{1,0:T(2,128)} %perms.3) | copy-start | bytes 3076
  85.0 12.0 %collective-permute-start.10 = (f32[16,14,8,128]{3,2,1,0:T(8,128)S(1)}, f32[16,14,8,128]{3,2,1,0:T(8,128)S(1)}, u32[]{:S(2)}, u32[]{:S(2)}) collective-permute-start(f32[16,14,8,128]{3,2,1,0:T(8,128)S(1)} %bitcast.89), channel_id=1, source_target_pairs={{0,1},{1,0},{2,3},{3,2},{4,5},{5,4},{6,7},{7,6},{8,9},{9,8},{10,11... | collective-permute-start | bytes 2752520 | tf_op jit(solution)/shard_map/ppermute | solution.py:227
  118.1 6.2 %collective-permute-start.11 = (f32[16,64,128]{2,1,0:T(8,128)S(1)}, f32[16,64,128]{2,1,0:T(8,128)S(1)}, u32[]{:S(2)}, u32[]{:S(2)}) collective-permute-start(f32[16,64,128]{2,1,0:T(8,128)S(1)} %all_to_all.11.own), channel_id=1, source_target_pairs={{0,1},{1,0},{2,3},{3,2},{4,5},{5,4},{6,7},{7,6},{8,9},{9,8},{10,11... | collective-permute-start | bytes 1572872 | tf_op jit(solution)/shard_map/ppermute | solution.py:242
Sparse Core Ops, SparseCore 0:
  10.7 36.0 all-gather.3
  56.6 29.8 all-gather.5

commit v3 on v2

v3 whole, which is shorter than its diff:
```python
import jax
import jax.numpy as jnp
from jax import lax
from jax.experimental import pallas as pl
from jax.experimental.pallas import tpu as pltpu
from jax.sharding import Mesh
from jax.sharding import PartitionSpec as P

SWEEPS = 3
W = 128
H = W // 2
NP = 16
NZ = 16
SLOTS = 8


def split(x):
    high = x.astype(jnp.bfloat16)
    rest = x - high.astype(jnp.float32)
    mid = rest.astype(jnp.bfloat16)
    low = (rest - mid.astype(jnp.float32)).astype(jnp.bfloat16)
    return high, mid, low


def dot16(a, b):
    return jnp.dot(a, b, preferred_element_type=jnp.float32)


def dot(a, b):
    ah, am, al = split(a)
    bh, bm, bl = split(b)
    lead = jnp.concatenate([ah, am], axis=1)
    tail = jnp.concatenate([ah, al], axis=1)
    right = jnp.concatenate([bh, bm], axis=1)
    first = dot16(lead, jnp.concatenate([right, right], axis=0))
    second = dot16(tail, jnp.concatenate([bl, bh], axis=0))
    n = b.shape[1]
    return first[:, :n] + (first[:, n:] + second)


def index_kernel(dest, row_mask, col_mask, meta, src):
    me = lax.axis_index("x") * 4 + lax.axis_index("y")
    z = lax.axis_index("z")
    core = lax.axis_index("core")

    def invert(i, carry):
        src[0, dest[0, i]] = i
        src[1, dest[1, i]] = i
        return carry

    lax.fori_loop(0, W, invert, 0, unroll=8)

    def row_ok(k, i):
        return ((row_mask[k, i] == 1) & (i > k)).astype(jnp.int32)

    def col_ok(k, j):
        return ((col_mask[k, j] == 1) & (j > k)).astype(jnp.int32)

    head = src[0, 1]
    block = (z * 2 + core) * 2
    meta[0] = core
    meta[1] = (me == 0).astype(jnp.int32)
    meta[2] = col_ok(0, 1)
    meta[3] = row_ok(0, head)
    meta[4] = lax.shift_right_logical(head, 3)
    meta[5] = ((z == 0) & (core == 0)).astype(jnp.int32)
    for k in range(2):
        for j in range(2):
            meta[64 + 2 * k + j] = col_ok(k, block + j)
    for slot in range(SLOTS):
        here = me * SLOTS + slot
        meta[8 + slot] = row_ok(0, here)
        meta[16 + slot] = row_ok(1, here)
        meta[24 + slot] = row_ok(0, src[0, here])
        meta[32 + slot] = lax.shift_right_logical(dest[1, here], 3)
        meta[40 + slot] = lax.shift_right_logical(src[1, here], 3)
        meta[48 + slot] = lax.shift_right_logical(dest[0, here], 3)
        meta[56 + slot] = lax.shift_right_logical(src[0, here], 3)


def route_kernel(meta, a, own, *refs):
    got, (out, panel, last) = refs[:-3], refs[-3:]
    share = own[...] * meta[5].astype(jnp.float32)
    for ref in got:
        share = share + ref[...]
    out[...] = jnp.zeros_like(out)
    for slot in range(SLOTS):
        left, right = share[slot, :, :W], share[slot, :, W:]
        out[meta[48 + slot], 0] = left
        if slot < 7:
            panel[slot] = left
            panel[7 + slot] = right
        else:
            last[0] = left
            last[1] = right
        if slot < 2:
            out[:, 1 + 2 * slot] = jnp.broadcast_to(left[None], (NP, 8, W))
            out[:, 2 + 2 * slot] = jnp.broadcast_to(right[None], (NP, 8, W))
    rows = a[: 2 * W].reshape(NP, 2, 8, 2 * W)
    out[:, 5:7] = rows[..., :W]
    out[:, 7:9] = rows[..., W:]


def pack_kernel(meta, passed, last, got, out, chunk):
    chunk[...] = got[0, 5:9]

    @pl.when(meta[0] == 1)
    def _():
        out[...] = passed[...]

    @pl.when(meta[0] == 0)
    def _():
        out[:2] = last[...]
        for slot in range(SLOTS):
            out[2 + slot] = got[meta[56 + slot], 0]
        out[10:12] = got[0, 1:3]
        out[12] = got[meta[4], 3]
        out[13] = got[0, 4]


def order(perms, k):
    hit = lax.broadcasted_iota(jnp.int32, (W, W), 0) == perms[k : k + 1, :]
    return jnp.where(hit, 1.0, 0.0).astype(jnp.float32).T


def refine(pivot):
    row = lax.broadcasted_iota(jnp.int32, (W, W), 0)
    col = lax.broadcasted_iota(jnp.int32, (W, W), 1)
    two = jnp.where(row == col, 2.0, 0.0).astype(jnp.float32)
    scale = W * (jnp.mean(pivot * pivot) + 1e-6)
    approx = pivot.T / scale
    for _ in range(SWEEPS):
        approx = dot(approx, two - dot(pivot, approx))
    return approx


def factor(meta, head, panel, chunk, perms, lpan, plow, send, lsrc):
    def tile(ref, t):
        return ref[:, t].reshape(W, W)

    def flag(i):
        return meta[i].astype(jnp.float32)

    def flagged(block, base):
        return jnp.concatenate(
            [block[s * W : (s + 1) * W] * flag(base + s) for s in range(SLOTS)], axis=0
        )

    inv0 = refine(dot(order(perms, 0), tile(head, 10)))
    kept01 = dot(order(perms, 0), tile(head, 11)) * flag(2)
    low_src = dot(tile(head, 12), inv0) * flag(3)
    lsrc[...] = low_src
    inv1 = refine(dot(order(perms, 1), tile(head, 13) - dot(low_src, kept01)))
    col0 = jnp.concatenate([tile(panel, s) for s in range(7)] + [tile(head, 0)], axis=0)
    lpan[:, :W] = flagged(dot(col0, inv0), 8)
    ext0 = jnp.concatenate([tile(head, 2 + s) for s in range(SLOTS)], axis=0)
    ext0 = flagged(dot(ext0, inv0), 24)
    plow[...] = ext0
    col1 = jnp.concatenate([tile(panel, 7 + s) for s in range(7)] + [tile(head, 1)], axis=0)
    lpan[:, W:] = flagged(dot(col1 - dot(ext0, kept01), inv1), 16)
    for slot in range(SLOTS):
        half = pl.ds(pl.multiple_of(slot * W + meta[0] * H, H), H)
        send[meta[32 + slot], :H] = lpan[half, W:]
    send[:, H:] = jnp.broadcast_to(chunk[...].reshape(1, 32, W), (NP, 32, W))


def factor_kernel(meta, own, oth, *refs):
    @pl.when(meta[0] == 0)
    def _():
        factor(meta, own, oth, *refs)

    @pl.when(meta[0] == 1)
    def _():
        factor(meta, oth, own, *refs)


def first_kernel(meta, a, got, plow, lsrc, perms, cur, kept):
    def masked(block, k):
        return jnp.concatenate(
            [block[:, j * W : (j + 1) * W] * meta[64 + 2 * k + j].astype(jnp.float32) for j in range(2)],
            axis=1,
        )

    rows = jnp.concatenate(
        [got[:, H : H + 16].reshape(2 * W, W), got[:, H + 16 :].reshape(2 * W, W)], axis=1
    )
    up0 = dot(order(perms, 0), rows[:W])
    kept0 = masked(up0, 0)
    up1 = dot(order(perms, 1), rows[W:] - dot(lsrc[...], kept0))
    kept[...] = masked(up1, 1)
    prod = dot(plow[...], kept0)
    cur[...] = a[...] - prod

    @pl.when(meta[1] == 1)
    def _():
        cur[:W] = up0 - prod[:W]
        cur[W : 2 * W] = up1


def second_kernel(meta, cur, own, oth, kept, out, low):
    core = meta[0]
    for slot in range(SLOTS):
        dev = meta[40 + slot]
        low[pl.ds(pl.multiple_of(slot * W + core * H, H), H), :] = own[dev, :H]
        low[pl.ds(pl.multiple_of(slot * W + (1 - core) * H, H), H), :] = oth[dev]
    out[...] = cur[...] - dot(low[...], kept[...])


def f32(*shape):
    return jax.ShapeDtypeStruct(shape, jnp.float32)


def call(kernel, out_shape, n_in, scratch=(), flops=0, moved=0):
    smem = pl.BlockSpec(memory_space=pltpu.SMEM)
    vmem = pl.BlockSpec(memory_space=pltpu.VMEM)
    multi = isinstance(out_shape, (tuple, list))
    return pl.pallas_call(
        kernel,
        out_shape=out_shape,
        in_specs=[smem] + [vmem] * n_in,
        out_specs=[vmem] * len(out_shape) if multi else vmem,
        scratch_shapes=list(scratch),
        compiler_params=pltpu.CompilerParams(vmem_limit_bytes=24 * 2**20),
        cost_estimate=pl.CostEstimate(flops=flops, bytes_accessed=moved, transcendentals=0),
    )


def shards(a, row_perms, dest_rows, row_mask, col_mask):
    core = lax.axis_index("core")
    smem = pl.BlockSpec(memory_space=pltpu.SMEM)
    meta = pl.pallas_call(
        index_kernel,
        out_shape=jax.ShapeDtypeStruct((W,), jnp.int32),
        in_specs=[smem] * 3,
        out_specs=smem,
        scratch_shapes=[pltpu.SMEM((2, W), jnp.int32)],
    )(dest_rows, row_mask, col_mask)

    cut = a.reshape(SLOTS, NZ, 8, 2 * W)
    over = lax.ppermute(cut[:, 8:].transpose(1, 0, 2, 3), "core", [(0, 1)])
    pieces = [jnp.where(core == 0, cut[:, step % 8], over[8 - step]) for step in range(1, 9)]
    pieces, meta = lax.optimization_barrier((pieces, meta))
    got = []
    for step in range(1, 9):
        pairs = [(1, 2 * (NZ - step))]
        if step < 8:
            pairs.append((0, 2 * step))
        got.append(lax.ppermute(pieces[step - 1], ("z", "core"), pairs))

    out0, panel, last = call(
        route_kernel, (f32(NP, 9, 8, W), f32(14, 8, W), f32(2, 8, W)), 10, moved=2**20
    )(meta, a[: 2 * W], pieces[7], *got)
    passed = lax.ppermute(panel, "core", [(0, 1)])
    got0 = lax.all_to_all(out0, ("x", "y"), 0, 0, tiled=True)
    payload, chunk = call(pack_kernel, (f32(14, 8, W), f32(4, 8, W)), 3, moved=2**19)(
        meta, passed, last, got0
    )

    own = lax.all_gather(payload, "z", axis=0, tiled=False)
    oth = lax.ppermute(own, "core", [(0, 1), (1, 0)])

    lpan, plow, send, lsrc = call(
        factor_kernel,
        (f32(SLOTS * W, 2 * W), f32(SLOTS * W, W), f32(NP, H + 32, W), f32(W, W)),
        4,
        flops=5 * 10**8,
        moved=4 * 2**20,
    )(meta, own, oth, chunk, row_perms)

    got1 = lax.all_to_all(send, ("x", "y"), 0, 0, tiled=True)
    oth1 = lax.ppermute(got1[:, :H], "core", [(0, 1), (1, 0)])
    cur, kept = call(
        first_kernel, (f32(SLOTS * W, 2 * W), f32(W, 2 * W)), 5, flops=5 * 10**8, moved=3 * 2**20
    )(meta, a, got1, plow, lsrc, row_perms)
    schur = call(
        second_kernel,
        f32(SLOTS * W, 2 * W),
        4,
        scratch=(pltpu.VMEM((SLOTS * W, W), jnp.float32),),
        flops=5 * 10**8,
        moved=3 * 2**20,
    )(meta, cur, got1, oth1, kept)
    return schur, lpan


def solution(mesh):
    fine = Mesh(mesh.devices.reshape(4, 4, NZ, 2), ("x", "y", "z", "core"))
    placed = (P(("x", "y"), ("z", "core")), P(), P(), P(), P())
    return jax.shard_map(
        shards,
        mesh=fine,
        in_specs=placed,
        out_specs=(P(("x", "y"), ("z", "core")), P(("x", "y"), None)),
        check_vma=False,
    )
```

time: 134 us -> 117 us (0.87)
  between operations: 14.3 us -> 0.87 us
  blocking collectives: 55.1 us -> 42.1 us
  waiting for transfers between devices: 9.87 us -> 18.7 us
  starting transfers between devices: 32.8 us -> 40.1 us
  local copies, waits for them, and re-layouts: 5.51 us -> 1.24 us
  Pallas kernels: 15.9 us -> 13.6 us
    all_to_all x1 -> x0, blocking collectives: 13.6 us -> none  [shards(): got0 = lax.all_to_all(out0, ('x', 'y'), 0, 0, tiled=True)]
    all_to_all x0 -> x1, waiting for transfers between devices: none -> 7.23 us  [shards(): got0 = lax.all_to_all(out0, ('x', 'y'), 0, 0, tiled=True)]
    all_to_all x0 -> x1, starting transfers between devices: none -> 6.76 us  [shards(): got0 = lax.all_to_all(out0, ('x', 'y'), 0, 0, tiled=True)]
    slice x3 -> x2, local copies, waits for them, and re-layouts: 4.39 us -> 0.05 us  [the longest x1 0.03 us: shards(): oth1 = lax.ppermute(got1[:, :H], 'core', [(0, 1), (1, 0)])]
    all_to_all x1, blocking collectives: 13.1 us -> 16.8 us  [shards(): got1 = lax.all_to_all(send, ('x', 'y'), 0, 0, tiled=True)]
    all_gather x1, blocking collectives: 28.5 us -> 25.3 us  [shards(): own = lax.all_gather(payload, 'z', axis=0, tiled=False)]
    pallas_call x5, Pallas kernels: 13.9 us -> 11.6 us  [the longest x1 5.8 us: shards(): call(factor_kernel, (f32(SLOTS * W, 2 * W), f32(SLOTS * W, W), f32(NP, H...]
  transfers between devices with their start and end apart: 14 -> 13, of which waited for: 4 -> 5; matrix products, arithmetic and copies ran while one was open for 2% -> 0% of each run, Pallas kernels for 4% -> 3%
where the time goes in v3:
time: 117 us
  blocking collectives  42.1 us (36%)
  starting transfers between devices  40.1 us (34%)
  waiting for transfers between devices  18.7 us (16%)
  Pallas kernels  13.6 us (12%)
  local copies, waits for them, and re-layouts  1.24 us (1%)
    all_gather x1, blocking collectives, shards(): own = lax.all_gather(payload, 'z', axis=0, tiled=False)  25.3 us
    all_to_all x1, blocking collectives, shards(): got1 = lax.all_to_all(send, ('x', 'y'), 0, 0, tiled=True)  16.8 us
    ppermute x8, starting transfers between devices, shards(): got.append(lax.ppermute(pieces[step - 1], ('z', 'core'), pairs))  16.3 us
    ppermute x1, starting transfers between devices, shards(): oth = lax.ppermute(own, 'core', [(0, 1), (1, 0)])  10.8 us
    all_to_all x1, waiting for transfers between devices, shards(): got0 = lax.all_to_all(out0, ('x', 'y'), 0, 0, tiled=True)  7.23 us
    all_to_all x1, starting transfers between devices, shards(): got0 = lax.all_to_all(out0, ('x', 'y'), 0, 0, tiled=True)  6.76 us
    ppermute x1, waiting for transfers between devices, shards(): over = lax.ppermute(cut[:, 8:].transpose(1, 0, 2, 3), 'core', [(0, 1)])  6.26 us
    pallas_call x1, Pallas kernels, shards(): call(factor_kernel, (f32(SLOTS * W, 2 * W), f32(SLOTS * W, W), f32(NP, H...  5.8 us
  transfers between devices with their start and end apart: 13, of which 5 were waited for; matrix products, arithmetic and copies ran while one was open for 0% of the time, Pallas kernels for 3%

profile of v3, /device:TPU:1, one launch (start us, length us, event | category | flops | bytes accessed | tf_op | source)
XLA Modules:
  0.0 116.7 jit_solution(15343048269035856407)
XLA Ops:
  0.6 0.0 copy-start
  0.6 1.2 %copy_bitcast_fusion = f32[8,8,8,256]{3,2,1,0:T(8,128)S(1)} fusion(f32[8,16,8,256]{3,2,1,0:T(8,128)} %bitcast.84), kind=kLoop, calls=%fused_computation | loop fusion | bytes 1048576 | tf_op jit(solution)/shard_map/transpose | solution.py:240
  1.8 1.3 %collective-permute-start = (f32[8,8,8,256]{3,2,1,0:T(8,128)S(1)}, f32[8,8,8,256]{3,2,1,0:T(8,128)S(1)}, u32[]{:S(2)}, u32[]{:S(2)}) collective-permute-start(f32[8,8,8,256]{3,2,1,0:T(8,128)S(1)} %copy_bitcast_fusion), channel_id=1, source_target_pairs={{0,1},{2,3},{4,5},{6,7},{8,9},{10,11},{12,13},{14,15},{16,17},{18,... | collective-permute-start | bytes 1572872 | tf_op jit(solution)/shard_map/ppermute | solution.py:240
  3.1 2.0 %shard_map.68.meta = s32[128]{0:T(128)} custom-call(s32[2,128]{1,0:T(2,128)} %dest.1, s32[2,128]{1,0:T(2,128)} %row_mask.1, s32[2,64]{1,0:T(2,128)} %col_mask.1), custom_call_target="tpu_custom_call" | custom-call | tf_op jit(solution)/shard_map/pallas_call | solution.py:231
  5.1 6.3 %collective-permute-done = f32[8,8,8,256]{3,2,1,0:T(8,128)S(1)} collective-permute-done((f32[8,8,8,256]{3,2,1,0:T(8,128)S(1)}, f32[8,8,8,256]{3,2,1,0:T(8,128)S(1)}, u32[]{:S(2)}, u32[]{:S(2)}) %collective-permute-start) | collective-permute-done | bytes 524320 | tf_op jit(solution)/shard_map/ppermute | solution.py:240
  11.4 0.0 copy-done
  11.4 0.1 fusion
  11.5 0.0 copy-start.1
  11.5 6.8 %collective-permute-start.1 = (f32[8,8,256]{2,1,0:T(8,128)S(1)}, f32[8,8,256]{2,1,0:T(8,128)S(1)}, u32[]{:S(2)}, u32[]{:S(2)}) collective-permute-start(f32[8,8,256]{2,1,0:T(8,128)S(1)} %get-tuple-element.24), channel_id=1, source_target_pairs={{1,30},{0,2},{33,62},{32,34},{65,94},{64,66},{97,126},{96,98},{129... | collective-permute-start | bytes 196616 | tf_op jit(solution)/shard_map/ppermute | solution.py:248
  18.2 1.3 %collective-permute-start.2 = (f32[8,8,256]{2,1,0:T(8,128)S(1)}, f32[8,8,256]{2,1,0:T(8,128)S(1)}, u32[]{:S(2)}, u32[]{:S(2)}) collective-permute-start(f32[8,8,256]{2,1,0:T(8,128)S(1)} %get-tuple-element.25), channel_id=1, source_target_pairs={{1,28},{0,4},{33,60},{32,36},{65,92},{64,68},{97,124},{96,100},{12... | collective-permute-start | bytes 196616 | tf_op jit(solution)/shard_map/ppermute | solution.py:248
  19.5 1.3 %collective-permute-start.3 = (f32[8,8,256]{2,1,0:T(8,128)S(1)}, f32[8,8,256]{2,1,0:T(8,128)S(1)}, u32[]{:S(2)}, u32[]{:S(2)}) collective-permute-start(f32[8,8,256]{2,1,0:T(8,128)S(1)} %get-tuple-element.26), channel_id=1, source_target_pairs={{1,26},{0,6},{33,58},{32,38},{65,90},{64,70},{97,122},{96,102},{12... | collective-permute-start | bytes 196616 | tf_op jit(solution)/shard_map/ppermute | solution.py:248
  20.8 1.3 %collective-permute-start.4 = (f32[8,8,256]{2,1,0:T(8,128)S(1)}, f32[8,8,256]{2,1,0:T(8,128)S(1)}, u32[]{:S(2)}, u32[]{:S(2)}) collective-permute-start(f32[8,8,256]{2,1,0:T(8,128)S(1)} %get-tuple-element.27), channel_id=1, source_target_pairs={{1,24},{0,8},{33,56},{32,40},{65,88},{64,72},{97,120},{96,104},{12... | collective-permute-start | bytes 196616 | tf_op jit(solution)/shard_map/ppermute | solution.py:248
  22.1 1.8 %collective-permute-start.5 = (f32[8,8,256]{2,1,0:T(8,128)S(1)}, f32[8,8,256]{2,1,0:T(8,128)S(1)}, u32[]{:S(2)}, u32[]{:S(2)}) collective-permute-start(f32[8,8,256]{2,1,0:T(8,128)S(1)} %get-tuple-element.28), channel_id=1, source_target_pairs={{1,22},{0,10},{33,54},{32,42},{65,86},{64,74},{97,118},{96,106},{1... | collective-permute-start | bytes 196616 | tf_op jit(solution)/shard_map/ppermute | solution.py:248
  23.9 0.0 collective-permute-done.1.refs_0_
  23.9 1.3 %collective-permute-start.6 = (f32[8,8,256]{2,1,0:T(8,128)S(1)}, f32[8,8,256]{2,1,0:T(8,128)S(1)}, u32[]{:S(2)}, u32[]{:S(2)}) collective-permute-start(f32[8,8,256]{2,1,0:T(8,128)S(1)} %get-tuple-element.29), channel_id=1, source_target_pairs={{1,20},{0,12},{33,52},{32,44},{65,84},{64,76},{97,116},{96,108},{1... | collective-permute-start | bytes 196616 | tf_op jit(solution)/shard_map/ppermute | solution.py:248
  25.2 0.0 collective-permute-done.2.refs_1_
  25.2 1.3 %collective-permute-start.7 = (f32[8,8,256]{2,1,0:T(8,128)S(1)}, f32[8,8,256]{2,1,0:T(8,128)S(1)}, u32[]{:S(2)}, u32[]{:S(2)}) collective-permute-start(f32[8,8,256]{2,1,0:T(8,128)S(1)} %get-tuple-element.30), channel_id=1, source_target_pairs={{1,18},{0,14},{33,50},{32,46},{65,82},{64,78},{97,114},{96,110},{1... | collective-permute-start | bytes 196616 | tf_op jit(solution)/shard_map/ppermute | solution.py:248
  26.5 0.0 collective-permute-done.3.refs_2_
  26.5 1.3 %collective-permute-start.8 = (f32[8,8,256]{2,1,0:T(8,128)S(1)}, f32[8,8,256]{2,1,0:T(8,128)S(1)}, u32[]{:S(2)}, u32[]{:S(2)}) collective-permute-start(f32[8,8,256]{2,1,0:T(8,128)S(1)} %get-tuple-element.23.own), channel_id=1, source_target_pairs={{1,16},{33,48},{65,80},{97,112},{129,144},{161,176},{193,208},{225... | collective-permute-start | bytes 196616 | tf_op jit(solution)/shard_map/ppermute | solution.py:248
  27.9 0.0 collective-permute-done.4.refs_3_
  27.9 0.0 collective-permute-done.5.refs_4_
  27.9 0.0 collective-permute-done.6.refs_5_
  27.9 0.0 collective-permute-done.7.refs_6_
  27.9 1.2 %collective-permute-done.8.refs_7_ = f32[8,8,256]{2,1,0:T(8,128)S(1)} collective-permute-done((f32[8,8,256]{2,1,0:T(8,128)S(1)}, f32[8,8,256]{2,1,0:T(8,128)S(1)}, u32[]{:S(2)}, u32[]{:S(2)}) %collective-permute-start.8) | collective-permute-done | bytes 65568 | tf_op jit(solution)/shard_map/ppermute | solution.py:248
  29.1 0.0 copy-done.1
  29.2 1.4 %shard_map.69 = (f32[16,9,8,128]{3,2,1,0:T(8,128)}, f32[14,8,128]{2,1,0:T(8,128)S(1)}, f32[2,8,128]{2,1,0:T(8,128)S(1)}) custom-call(s32[128]{0:T(128)S(1)} %copy-done.1, f32[256,256]{1,0:T(8,128)S(1)} %slice.74.a, f32[8,8,256]{2,1,0:T(8,128)S(1)} %get-tuple-element.23.own, f32[8,8,256]{2,1,0:T(8,128)S(1)} %collective-permute-done.1.refs_0_, ...), custom_call_target="tpu_custom_call" | custom-call | bytes 1048576 | tf_op jit(solution)/shard_map/pallas_call | solution.py:250
  30.6 6.8 %all-to-all-start = ((f32[16,9,8,128]{3,2,1,0:T(8,128)}), f32[16,9,8,128]{3,2,1,0:T(8,128)S(1)}, u32[]{:S(2)}, u32[]{:S(2)}) async-start(f32[16,9,8,128]{3,2,1,0:T(8,128)} %get-tuple-element.33), calls=%async_computation | async-start | bytes 1179648 | tf_op jit(solution)/shard_map/all_to_all | solution.py:254
  37.4 1.3 %collective-permute-start.9 = (f32[14,8,128]{2,1,0:T(8,128)S(1)}, f32[14,8,128]{2,1,0:T(8,128)S(1)}, u32[]{:S(2)}, u32[]{:S(2)}) collective-permute-start(f32[14,8,128]{2,1,0:T(8,128)S(1)} %get-tuple-element.31), channel_id=1, source_target_pairs={{0,1},{2,3},{4,5},{6,7},{8,9},{10,11},{12,13},{14,15},{16,17},{18,... | collective-permute-start | bytes 172040 | tf_op jit(solution)/shard_map/ppermute | solution.py:253
  38.7 1.8 %collective-permute-done.9.passed = f32[14,8,128]{2,1,0:T(8,128)S(1)} collective-permute-done((f32[14,8,128]{2,1,0:T(8,128)S(1)}, f32[14,8,128]{2,1,0:T(8,128)S(1)}, u32[]{:S(2)}, u32[]{:S(2)}) %collective-permute-start.9) | collective-permute-done | bytes 57376 | tf_op jit(solution)/shard_map/ppermute | solution.py:253
  40.5 7.2 %all-to-all-done.got = f32[16,9,8,128]{3,2,1,0:T(8,128)S(1)} async-done(((f32[16,9,8,128]{3,2,1,0:T(8,128)}), f32[16,9,8,128]{3,2,1,0:T(8,128)S(1)}, u32[]{:S(2)}, u32[]{:S(2)}) %all-to-all-start) | async-done | bytes 589856 | tf_op jit(solution)/shard_map/all_to_all | solution.py:254
  47.7 0.6 shard_map.70
  48.3 25.3 %all-gather = f32[224,8,128]{2,1,0:T(8,128)S(1)} all-gather(f32[14,8,128]{2,1,0:T(8,128)S(1)} %get-tuple-element.34), channel_id=2, replica_groups=mesh['x'=4,'y'=4,'z'=16,'core'=2] {'z'}, dimensions={0}, use_global_device_ids=true | all-gather | bytes 974848 | tf_op jit(solution)/shard_map/all_gather | solution.py:259
  73.6 0.0 copy-start.2
  73.6 10.8 %collective-permute-start.10 = (f32[16,14,8,128]{3,2,1,0:T(8,128)S(1)}, f32[16,14,8,128]{3,2,1,0:T(8,128)S(1)}, u32[]{:S(2)}, u32[]{:S(2)}) collective-permute-start(f32[16,14,8,128]{3,2,1,0:T(8,128)S(1)} %bitcast.86), channel_id=1, source_target_pairs={{0,1},{1,0},{2,3},{3,2},{4,5},{5,4},{6,7},{7,6},{8,9},{9,8},{10,11... | collective-permute-start | bytes 2752520 | tf_op jit(solution)/shard_map/ppermute | solution.py:260
  84.4 2.1 %collective-permute-done.10.oth = f32[16,14,8,128]{3,2,1,0:T(8,128)S(1)} collective-permute-done((f32[16,14,8,128]{3,2,1,0:T(8,128)S(1)}, f32[16,14,8,128]{3,2,1,0:T(8,128)S(1)}, u32[]{:S(2)}, u32[]{:S(2)}) %collective-permute-start.10) | collective-permute-done | bytes 917536 | tf_op jit(solution)/shard_map/ppermute | solution.py:260
  86.5 0.0 copy-done.2
  86.5 5.8 %shard_map.71 = (f32[1024,256]{1,0:T(8,128)}, f32[1024,128]{1,0:T(8,128)S(1)}, f32[16,96,128]{2,1,0:T(8,128)S(1)}, f32[128,128]{1,0:T(8,128)S(1)}) custom-call(s32[128]{0:T(128)S(1)} %copy-done.1, f32[16,14,8,128]{3,2,1,0:T(8,128)S(1)} %bitcast.87, f32[16,14,8,128]{3,2,1,0:T(8,128)S(1)} %collective-permute-done.10.oth, ...), custom_call_target="tpu_custom_call" | custom-call | flops 500000000 | bytes 4194304 | tf_op jit(solution)/shard_map/pallas_call | solution.py:262
  92.3 16.8 %all_to_all.10.got.own = f32[16,96,128]{2,1,0:T(8,128)S(1)} all-to-all(f32[16,96,128]{2,1,0:T(8,128)S(1)} %get-tuple-element.36), channel_id=1, replica_groups=mesh['x'=4,'y'=4,'z'=16,'core'=2] {'x','y'}, dimensions={0} | all-to-all | bytes 1572864 | tf_op jit(solution)/shard_map/all_to_all | solution.py:270
  109.1 3.7 %collective-permute-start.11 = (f32[16,64,128]{2,1,0:T(8,128)S(1)}, f32[16,64,128]{2,1,0:T(8,128)S(1)}, u32[]{:S(2)}, u32[]{:S(2)}) collective-permute-start(f32[16,64,128]{2,1,0:T(8,128)S(1)} %slice.93), channel_id=1, source_target_pairs={{0,1},{1,0},{2,3},{3,2},{4,5},{5,4},{6,7},{7,6},{8,9},{9,8},{10,11... | collective-permute-start | bytes 1572872 | tf_op jit(solution)/shard_map/ppermute | solution.py:271
  112.8 1.7 %shard_map.72 = (f32[1024,256]{1,0:T(8,128)S(1)}, f32[128,256]{1,0:T(8,128)S(1)}) custom-call(s32[128]{0:T(128)S(1)} %copy-done.1, f32[1024,256]{1,0:T(8,128)S(1)} %copy-done, f32[16,96,128]{2,1,0:T(8,128)S(1)} %all_to_all.10.got.own, f32[1024,128]{1,0:T(8,128)S(1)} %get-tuple-element.37.plow, f32[128,128]{1,0:T(8,128)S(1)} %get-tuple-element.38.lsrc, ...), custom_call_target="tpu_custom_call" | custom-call | flops 500000000 | bytes 3145728 | tf_op jit(solution)/shard_map/pallas_call | solution.py:272
  114.5 0.0 collective-permute-done.11.oth
  114.5 2.1 %shard_map.73 = f32[1024,256]{1,0:T(8,128)} custom-call(s32[128]{0:T(128)S(1)} %copy-done.1, f32[1024,256]{1,0:T(8,128)S(1)} %get-tuple-element.39.cur, f32[16,96,128]{2,1,0:T(8,128)S(1)} %all_to_all.10.got.own, f32[16,64,128]{2,1,0:T(8,128)S(1)} %collective-permute-done.11.oth, f32[128,256]{1,0:T(8,128)S(1)} %get-tuple-element.40.kept), custom_call_target="tpu_custom_call" | custom-call | flops 500000000 | bytes 3145728 | tf_op jit(solution)/shard_map/pallas_call | solution.py:275
  (2 shorter events, 0.1 us)
Async XLA Ops:
  0.6 10.8 %copy-start = (f32[1024,256]{1,0:T(8,128)S(1)}, f32[1024,256]{1,0:T(8,128)}, u32[]{:S(2)}) copy-start(f32[1024,256]{1,0:T(8,128)} %a.1) | copy-start | bytes 3145732
  1.8 9.6 %collective-permute-start = (f32[8,8,8,256]{3,2,1,0:T(8,128)S(1)}, f32[8,8,8,256]{3,2,1,0:T(8,128)S(1)}, u32[]{:S(2)}, u32[]{:S(2)}) collective-permute-start(f32[8,8,8,256]{3,2,1,0:T(8,128)S(1)} %copy_bitcast_fusion), channel_id=1, source_target_pairs={{0,1},{2,3},{4,5},{6,7},{8,9},{10,11},{12,13},{14,15},{16,17},{18,... | collective-permute-start | bytes 1572872 | tf_op jit(solution)/shard_map/ppermute | solution.py:240
  11.5 17.7 %copy-start.1 = (s32[128]{0:T(128)S(1)}, s32[128]{0:T(128)}, u32[]{:S(2)}) copy-start(s32[128]{0:T(128)} %shard_map.68.meta) | copy-start | bytes 1540
  11.5 12.4 %collective-permute-start.1 = (f32[8,8,256]{2,1,0:T(8,128)S(1)}, f32[8,8,256]{2,1,0:T(8,128)S(1)}, u32[]{:S(2)}, u32[]{:S(2)}) collective-permute-start(f32[8,8,256]{2,1,0:T(8,128)S(1)} %get-tuple-element.24), channel_id=1, source_target_pairs={{1,30},{0,2},{33,62},{32,34},{65,94},{64,66},{97,126},{96,98},{129... | collective-permute-start | bytes 196616 | tf_op jit(solution)/shard_map/ppermute | solution.py:248
  18.2 7.0 %collective-permute-start.2 = (f32[8,8,256]{2,1,0:T(8,128)S(1)}, f32[8,8,256]{2,1,0:T(8,128)S(1)}, u32[]{:S(2)}, u32[]{:S(2)}) collective-permute-start(f32[8,8,256]{2,1,0:T(8,128)S(1)} %get-tuple-element.25), channel_id=1, source_target_pairs={{1,28},{0,4},{33,60},{32,36},{65,92},{64,68},{97,124},{96,100},{12... | collective-permute-start | bytes 196616 | tf_op jit(solution)/shard_map/ppermute | solution.py:248
  19.5 7.0 %collective-permute-start.3 = (f32[8,8,256]{2,1,0:T(8,128)S(1)}, f32[8,8,256]{2,1,0:T(8,128)S(1)}, u32[]{:S(2)}, u32[]{:S(2)}) collective-permute-start(f32[8,8,256]{2,1,0:T(8,128)S(1)} %get-tuple-element.26), channel_id=1, source_target_pairs={{1,26},{0,6},{33,58},{32,38},{65,90},{64,70},{97,122},{96,102},{12... | collective-permute-start | bytes 196616 | tf_op jit(solution)/shard_map/ppermute | solution.py:248
  20.8 7.0 %collective-permute-start.4 = (f32[8,8,256]{2,1,0:T(8,128)S(1)}, f32[8,8,256]{2,1,0:T(8,128)S(1)}, u32[]{:S(2)}, u32[]{:S(2)}) collective-permute-start(f32[8,8,256]{2,1,0:T(8,128)S(1)} %get-tuple-element.27), channel_id=1, source_target_pairs={{1,24},{0,8},{33,56},{32,40},{65,88},{64,72},{97,120},{96,104},{12... | collective-permute-start | bytes 196616 | tf_op jit(solution)/shard_map/ppermute | solution.py:248
  22.1 5.7 %collective-permute-start.5 = (f32[8,8,256]{2,1,0:T(8,128)S(1)}, f32[8,8,256]{2,1,0:T(8,128)S(1)}, u32[]{:S(2)}, u32[]{:S(2)}) collective-permute-start(f32[8,8,256]{2,1,0:T(8,128)S(1)} %get-tuple-element.28), channel_id=1, source_target_pairs={{1,22},{0,10},{33,54},{32,42},{65,86},{64,74},{97,118},{96,106},{1... | collective-permute-start | bytes 196616 | tf_op jit(solution)/shard_map/ppermute | solution.py:248
  23.9 4.0 %collective-permute-start.6 = (f32[8,8,256]{2,1,0:T(8,128)S(1)}, f32[8,8,256]{2,1,0:T(8,128)S(1)}, u32[]{:S(2)}, u32[]{:S(2)}) collective-permute-start(f32[8,8,256]{2,1,0:T(8,128)S(1)} %get-tuple-element.29), channel_id=1, source_target_pairs={{1,20},{0,12},{33,52},{32,44},{65,84},{64,76},{97,116},{96,108},{1... | collective-permute-start | bytes 196616 | tf_op jit(solution)/shard_map/ppermute | solution.py:248
  25.2 2.7 %collective-permute-start.7 = (f32[8,8,256]{2,1,0:T(8,128)S(1)}, f32[8,8,256]{2,1,0:T(8,128)S(1)}, u32[]{:S(2)}, u32[]{:S(2)}) collective-permute-start(f32[8,8,256]{2,1,0:T(8,128)S(1)} %get-tuple-element.30), channel_id=1, source_target_pairs={{1,18},{0,14},{33,50},{32,46},{65,82},{64,78},{97,114},{96,110},{1... | collective-permute-start | bytes 196616 | tf_op jit(solution)/shard_map/ppermute | solution.py:248
  26.5 2.6 %collective-permute-start.8 = (f32[8,8,256]{2,1,0:T(8,128)S(1)}, f32[8,8,256]{2,1,0:T(8,128)S(1)}, u32[]{:S(2)}, u32[]{:S(2)}) collective-permute-start(f32[8,8,256]{2,1,0:T(8,128)S(1)} %get-tuple-element.23.own), channel_id=1, source_target_pairs={{1,16},{33,48},{65,80},{97,112},{129,144},{161,176},{193,208},{225... | collective-permute-start | bytes 196616 | tf_op jit(solution)/shard_map/ppermute | solution.py:248
  30.6 17.1 %all-to-all-start = ((f32[16,9,8,128]{3,2,1,0:T(8,128)}), f32[16,9,8,128]{3,2,1,0:T(8,128)S(1)}, u32[]{:S(2)}, u32[]{:S(2)}) async-start(f32[16,9,8,128]{3,2,1,0:T(8,128)} %get-tuple-element.33), calls=%async_computation | async-start | bytes 1179648 | tf_op jit(solution)/shard_map/all_to_all | solution.py:254
  37.4 3.1 %collective-permute-start.9 = (f32[14,8,128]{2,1,0:T(8,128)S(1)}, f32[14,8,128]{2,1,0:T(8,128)S(1)}, u32[]{:S(2)}, u32[]{:S(2)}) collective-permute-start(f32[14,8,128]{2,1,0:T(8,128)S(1)} %get-tuple-element.31), channel_id=1, source_target_pairs={{0,1},{2,3},{4,5},{6,7},{8,9},{10,11},{12,13},{14,15},{16,17},{18,... | collective-permute-start | bytes 172040 | tf_op jit(solution)/shard_map/ppermute | solution.py:253
  73.6 12.9 %copy-start.2 = (s32[2,128]{1,0:T(2,128)S(1)}, s32[2,128]{1,0:T(2,128)}, u32[]{:S(2)}) copy-start(s32[2,128]{1,0:T(2,128)} %perms.1) | copy-start | bytes 3076
  73.6 12.9 %collective-permute-start.10 = (f32[16,14,8,128]{3,2,1,0:T(8,128)S(1)}, f32[16,14,8,128]{3,2,1,0:T(8,128)S(1)}, u32[]{:S(2)}, u32[]{:S(2)}) collective-permute-start(f32[16,14,8,128]{3,2,1,0:T(8,128)S(1)} %bitcast.86), channel_id=1, source_target_pairs={{0,1},{1,0},{2,3},{3,2},{4,5},{5,4},{6,7},{7,6},{8,9},{9,8},{10,11... | collective-permute-start | bytes 2752520 | tf_op jit(solution)/shard_map/ppermute | solution.py:260
  109.1 5.4 %collective-permute-start.11 = (f32[16,64,128]{2,1,0:T(8,128)S(1)}, f32[16,64,128]{2,1,0:T(8,128)S(1)}, u32[]{:S(2)}, u32[]{:S(2)}) collective-permute-start(f32[16,64,128]{2,1,0:T(8,128)S(1)} %slice.93), channel_id=1, source_target_pairs={{0,1},{1,0},{2,3},{3,2},{4,5},{5,4},{6,7},{7,6},{8,9},{9,8},{10,11... | collective-permute-start | bytes 1572872 | tf_op jit(solution)/shard_map/ppermute | solution.py:271

commit v4 on v3

--- a/solution.py
+++ b/solution.py
@@ -12,6 +12,7 @@
 NP = 16
 NZ = 16
 SLOTS = 8
+SENDS = ((8, 9), (7, 10), (6, 11), (5, 12), (4, 13), (3, 14), (2, 15), (1, 0))
 
 
 def split(x):
@@ -78,7 +79,7 @@
         meta[56 + slot] = lax.shift_right_logical(src[0, here], 3)
 
 
-def route_kernel(meta, a, own, *refs):
+def route_kernel(meta, own, *refs):
     got, (out, panel, last) = refs[:-3], refs[-3:]
     share = own[...] * meta[5].astype(jnp.float32)
     for ref in got:
@@ -96,14 +97,9 @@
         if slot < 2:
             out[:, 1 + 2 * slot] = jnp.broadcast_to(left[None], (NP, 8, W))
             out[:, 2 + 2 * slot] = jnp.broadcast_to(right[None], (NP, 8, W))
-    rows = a[: 2 * W].reshape(NP, 2, 8, 2 * W)
-    out[:, 5:7] = rows[..., :W]
-    out[:, 7:9] = rows[..., W:]
-
-
-def pack_kernel(meta, passed, last, got, out, chunk):
-    chunk[...] = got[0, 5:9]
-
+
+
+def pack_kernel(meta, passed, last, got, out):
     @pl.when(meta[0] == 1)
     def _():
         out[...] = passed[...]
@@ -134,7 +130,7 @@
     return approx
 
 
-def factor(meta, head, panel, chunk, perms, lpan, plow, send, lsrc):
+def factor(meta, head, panel, perms, lpan, plow, send, lsrc, kept):
     def tile(ref, t):
         return ref[:, t].reshape(W, W)
 
@@ -150,6 +146,7 @@
     kept01 = dot(order(perms, 0), tile(head, 11)) * flag(2)
     low_src = dot(tile(head, 12), inv0) * flag(3)
     lsrc[...] = low_src
+    kept[...] = kept01
     inv1 = refine(dot(order(perms, 1), tile(head, 13) - dot(low_src, kept01)))
     col0 = jnp.concatenate([tile(panel, s) for s in range(7)] + [tile(head, 0)], axis=0)
     lpan[:, :W] = flagged(dot(col0, inv0), 8)
@@ -160,8 +157,7 @@
     lpan[:, W:] = flagged(dot(col1 - dot(ext0, kept01), inv1), 16)
     for slot in range(SLOTS):
         half = pl.ds(pl.multiple_of(slot * W + meta[0] * H, H), H)
-        send[meta[32 + slot], :H] = lpan[half, W:]
-    send[:, H:] = jnp.broadcast_to(chunk[...].reshape(1, 32, W), (NP, 32, W))
+        send[meta[32 + slot]] = lpan[half, W:]
 
 
 def factor_kernel(meta, own, oth, *refs):
@@ -174,18 +170,17 @@
         factor(meta, oth, own, *refs)
 
 
-def first_kernel(meta, a, got, plow, lsrc, perms, cur, kept):
+def first_kernel(meta, a, rows, plow, lsrc, kept01, perms, cur, kept):
     def masked(block, k):
         return jnp.concatenate(
             [block[:, j * W : (j + 1) * W] * meta[64 + 2 * k + j].astype(jnp.float32) for j in range(2)],
             axis=1,
         )
 
-    rows = jnp.concatenate(
-        [got[:, H : H + 16].reshape(2 * W, W), got[:, H + 16 :].reshape(2 * W, W)], axis=1
-    )
     up0 = dot(order(perms, 0), rows[:W])
     kept0 = masked(up0, 0)
+    right = jnp.where(meta[5] == 1, kept01[...], kept0[:, W:])
+    kept0 = jnp.concatenate([kept0[:, :W], right], axis=1)
     up1 = dot(order(perms, 1), rows[W:] - dot(lsrc[...], kept0))
     kept[...] = masked(up1, 1)
     prod = dot(plow[...], kept0)
@@ -201,7 +196,7 @@
     core = meta[0]
     for slot in range(SLOTS):
         dev = meta[40 + slot]
-        low[pl.ds(pl.multiple_of(slot * W + core * H, H), H), :] = own[dev, :H]
+        low[pl.ds(pl.multiple_of(slot * W + core * H, H), H), :] = own[dev]
         low[pl.ds(pl.multiple_of(slot * W + (1 - core) * H, H), H), :] = oth[dev]
     out[...] = cur[...] - dot(low[...], kept[...])
 
@@ -220,58 +215,75 @@
         in_specs=[smem] + [vmem] * n_in,
         out_specs=[vmem] * len(out_shape) if multi else vmem,
         scratch_shapes=list(scratch),
-        compiler_params=pltpu.CompilerParams(vmem_limit_bytes=24 * 2**20),
+        compiler_params=pltpu.CompilerParams(vmem_limit_bytes=16 * 2**20),
         cost_estimate=pl.CostEstimate(flops=flops, bytes_accessed=moved, transcendentals=0),
     )
+
+
+def spread(block, axis):
+    names = (axis, "z", "core")
+    return [
+        lax.ppermute(block, names, [(r, k * 2 * NZ + r) for r in range(1, 2 * NZ)]) for k in range(1, 4)
+    ]
+
+
+def settle(block, copies, index):
+    for k in range(1, 4):
+        block = jnp.where(index == k, copies[k - 1], block)
+    return block
 
 
 def shards(a, row_perms, dest_rows, row_mask, col_mask):
     core = lax.axis_index("core")
     smem = pl.BlockSpec(memory_space=pltpu.SMEM)
+    cut = a.reshape(SLOTS, NZ, 8, 2 * W)
+    over = lax.ppermute(cut[:, 9:].transpose(1, 0, 2, 3), ("z", "core"), [(0, 1)])
+    got = []
+    for z0, z1 in SENDS:
+        pairs, piece = [(0, 2 * z0)], cut[:, z0]
+        if z1:
+            pairs.append((1, 2 * z1))
+            piece = jnp.where(core == 0, piece, over[z1 - 9])
+        got.append(lax.ppermute(piece, ("z", "core"), pairs))
+
+    got[0], maps = lax.optimization_barrier((got[0], (dest_rows, row_mask, col_mask)))
     meta = pl.pallas_call(
         index_kernel,
         out_shape=jax.ShapeDtypeStruct((W,), jnp.int32),
         in_specs=[smem] * 3,
         out_specs=smem,
         scratch_shapes=[pltpu.SMEM((2, W), jnp.int32)],
-    )(dest_rows, row_mask, col_mask)
-
-    cut = a.reshape(SLOTS, NZ, 8, 2 * W)
-    over = lax.ppermute(cut[:, 8:].transpose(1, 0, 2, 3), "core", [(0, 1)])
-    pieces = [jnp.where(core == 0, cut[:, step % 8], over[8 - step]) for step in range(1, 9)]
-    pieces, meta = lax.optimization_barrier((pieces, meta))
-    got = []
-    for step in range(1, 9):
-        pairs = [(1, 2 * (NZ - step))]
-        if step < 8:
-            pairs.append((0, 2 * step))
-        got.append(lax.ppermute(pieces[step - 1], ("z", "core"), pairs))
+    )(*maps)
 
     out0, panel, last = call(
-        route_kernel, (f32(NP, 9, 8, W), f32(14, 8, W), f32(2, 8, W)), 10, moved=2**20
-    )(meta, a[: 2 * W], pieces[7], *got)
+        route_kernel, (f32(NP, 5, 8, W), f32(14, 8, W), f32(2, 8, W)), 9, moved=2**20
+    )(meta, cut[:, 0], *got)
     passed = lax.ppermute(panel, "core", [(0, 1)])
+    out0, rows = lax.optimization_barrier((out0, a[: 2 * W]))
+    copies = spread(rows, "x")
     got0 = lax.all_to_all(out0, ("x", "y"), 0, 0, tiled=True)
-    payload, chunk = call(pack_kernel, (f32(14, 8, W), f32(4, 8, W)), 3, moved=2**19)(
-        meta, passed, last, got0
-    )
-
+    payload = call(pack_kernel, f32(14, 8, W), 3, moved=2**19)(meta, passed, last, got0)
+
+    payload, copies = lax.optimization_barrier((payload, copies))
     own = lax.all_gather(payload, "z", axis=0, tiled=False)
     oth = lax.ppermute(own, "core", [(0, 1), (1, 0)])
 
-    lpan, plow, send, lsrc = call(
+    lpan, plow, send, lsrc, kept01 = call(
         factor_kernel,
-        (f32(SLOTS * W, 2 * W), f32(SLOTS * W, W), f32(NP, H + 32, W), f32(W, W)),
-        4,
+        (f32(SLOTS * W, 2 * W), f32(SLOTS * W, W), f32(NP, H, W), f32(W, W), f32(W, W)),
+        3,
         flops=5 * 10**8,
         moved=4 * 2**20,
-    )(meta, own, oth, chunk, row_perms)
-
+    )(meta, own, oth, row_perms)
+
+    send, copies = lax.optimization_barrier((send, copies))
+    rows = settle(rows, copies, lax.axis_index("x"))
+    rows = settle(rows, spread(rows, "y"), lax.axis_index("y"))
     got1 = lax.all_to_all(send, ("x", "y"), 0, 0, tiled=True)
-    oth1 = lax.ppermute(got1[:, :H], "core", [(0, 1), (1, 0)])
+    oth1 = lax.ppermute(got1, "core", [(0, 1), (1, 0)])
     cur, kept = call(
-        first_kernel, (f32(SLOTS * W, 2 * W), f32(W, 2 * W)), 5, flops=5 * 10**8, moved=3 * 2**20
-    )(meta, a, got1, plow, lsrc, row_perms)
+        first_kernel, (f32(SLOTS * W, 2 * W), f32(W, 2 * W)), 6, flops=5 * 10**8, moved=3 * 2**20
+    )(meta, a, rows, plow, lsrc, kept01, row_perms)
     schur = call(
         second_kernel,
         f32(SLOTS * W, 2 * W),

time: 117 us -> 125 us (1.068)
  the two profiles are of different devices: /device:TPU:1 before, /device:TPU:41 now
where the time goes in v4:
time: 125 us; the launch traced here: 124 us
  starting transfers between devices  43.9 us (35%)
  blocking collectives  41.1 us (33%)
  waiting for transfers between devices  20.9 us (17%)
  Pallas kernels  13.6 us (11%)
  local copies, waits for them, and re-layouts  2.66 us (2%)
    all_gather x1, blocking collectives, shards(): own = lax.all_gather(payload, 'z', axis=0, tiled=False)  41.1 us
    ppermute x1, starting transfers between devices, shards(): oth = lax.ppermute(own, 'core', [(0, 1), (1, 0)])  9.5 us
    ppermute x6, starting transfers between devices, spread(): lax.ppermute(block, names, [(r, k * 2 * NZ + r) for r in range(1, 2 * NZ)])  9.23 us
    ppermute x6, waiting for transfers between devices, spread(): lax.ppermute(block, names, [(r, k * 2 * NZ + r) for r in range(1, 2 * NZ)])  7.21 us
    all_to_all x1, starting transfers between devices, shards(): got1 = lax.all_to_all(send, ('x', 'y'), 0, 0, tiled=True)  7.2 us
    all_to_all x1, starting transfers between devices, shards(): got0 = lax.all_to_all(out0, ('x', 'y'), 0, 0, tiled=True)  6.83 us
    all_to_all x1, waiting for transfers between devices, shards(): got1 = lax.all_to_all(send, ('x', 'y'), 0, 0, tiled=True)  6.64 us
    pallas_call x1, Pallas kernels, shards(): call(factor_kernel, (f32(SLOTS * W, 2 * W), f32(SLOTS * W, W), f32(NP, H,...  5.96 us
  transfers between devices with their start and end apart: 20, of which 5 were waited for; matrix products, arithmetic and copies ran while one was open for 2% of the time, Pallas kernels for 3%

profile of v4, /device:TPU:41, one launch (start us, length us, event | category | flops | bytes accessed | tf_op | source)
XLA Modules:
  0.0 124.3 jit_solution(11871774178610269711)
XLA Ops:
  0.6 0.0 copy-start
  0.6 1.1 copy_bitcast_fusion
  1.8 0.7 collective-permute-start
  2.5 0.9 slice_bitcast_fusion
  3.4 0.7 collective-permute-start.8
  4.1 0.1 fusion
  4.1 0.7 collective-permute-start.1
  4.8 0.7 collective-permute-start.2
  5.5 0.7 collective-permute-start.3
  6.2 0.7 collective-permute-start.4
  6.8 0.0 collective-permute-done.8.refs_7_
  6.8 0.7 collective-permute-start.5
  7.5 0.0 collective-permute-done.1.refs_0_
  7.5 0.7 collective-permute-start.6
  8.2 0.0 collective-permute-done.2.refs_1_
  8.2 0.7 collective-permute-start.7
  8.9 2.0 %shard_map.68.meta = s32[128]{0:T(128)} custom-call(s32[2,128]{1,0:T(2,128)} %dest, s32[2,128]{1,0:T(2,128)} %row_mask, s32[2,64]{1,0:T(2,128)} %col_mask), custom_call_target="tpu_custom_call" | custom-call | tf_op jit(solution)/shard_map/pallas_call | solution.py:250
  10.9 0.0 copy-start.1
  10.9 0.0 collective-permute-done.3.refs_2_
  10.9 0.0 collective-permute-done.5.refs_4_
  10.9 0.0 collective-permute-done.6.refs_5_
  11.0 0.6 copy-done.1
  11.6 1.3 %shard_map.69 = (f32[16,5,8,128]{3,2,1,0:T(8,128)}, f32[14,8,128]{2,1,0:T(8,128)S(1)}, f32[2,8,128]{2,1,0:T(8,128)S(1)}) custom-call(s32[128]{0:T(128)S(1)} %copy-done.1, f32[8,8,256]{2,1,0:T(8,128)S(1)} %get-tuple-element.58.own, f32[8,8,256]{2,1,0:T(8,128)S(1)} %collective-permute-done.1.refs_0_, f32[8,8,256]{2,1,0:T(8,128)S(1)} %collective-permute-done.2.refs_1_, ...), custom_call_target="tpu_custom_call" | custom-call | bytes 1048576 | tf_op jit(solution)/shard_map/pallas_call | solution.py:258
  12.9 6.8 %all-to-all-start = ((f32[16,5,8,128]{3,2,1,0:T(8,128)}), f32[16,5,8,128]{3,2,1,0:T(8,128)S(1)}, u32[]{:S(2)}, u32[]{:S(2)}) async-start(f32[16,5,8,128]{3,2,1,0:T(8,128)} %get-tuple-element.33), calls=%async_computation | async-start | bytes 655360 | tf_op jit(solution)/shard_map/all_to_all | solution.py:264
  19.7 3.1 %collective-permute-start.10 = (f32[256,256]{1,0:T(8,128)S(1)}, f32[256,256]{1,0:T(8,128)S(1)}, u32[]{:S(2)}, u32[]{:S(2)}) collective-permute-start(f32[256,256]{1,0:T(8,128)S(1)} %slice.71), channel_id=1, source_target_pairs={{1,129},{2,130},{3,131},{4,132},{5,133},{6,134},{7,135},{8,136},{9... | collective-permute-start | bytes 786440 | tf_op jit(solution)/shard_map/ppermute | solution.py:226
  22.8 2.2 %collective-permute-start.11 = (f32[256,256]{1,0:T(8,128)S(1)}, f32[256,256]{1,0:T(8,128)S(1)}, u32[]{:S(2)}, u32[]{:S(2)}) collective-permute-start(f32[256,256]{1,0:T(8,128)S(1)} %slice.71), channel_id=1, source_target_pairs={{1,257},{2,258},{3,259},{4,260},{5,261},{6,262},{7,263},{8,264},{9... | collective-permute-start | bytes 786440 | tf_op jit(solution)/shard_map/ppermute | solution.py:226
  25.0 1.3 %collective-permute-start.12 = (f32[256,256]{1,0:T(8,128)S(1)}, f32[256,256]{1,0:T(8,128)S(1)}, u32[]{:S(2)}, u32[]{:S(2)}) collective-permute-start(f32[256,256]{1,0:T(8,128)S(1)} %slice.71), channel_id=1, source_target_pairs={{1,385},{2,386},{3,387},{4,388},{5,389},{6,390},{7,391},{8,392},{9... | collective-permute-start | bytes 786440 | tf_op jit(solution)/shard_map/ppermute | solution.py:226
  26.3 1.3 %collective-permute-start.9 = (f32[14,8,128]{2,1,0:T(8,128)S(1)}, f32[14,8,128]{2,1,0:T(8,128)S(1)}, u32[]{:S(2)}, u32[]{:S(2)}) collective-permute-start(f32[14,8,128]{2,1,0:T(8,128)S(1)} %get-tuple-element.30), channel_id=1, source_target_pairs={{0,1},{2,3},{4,5},{6,7},{8,9},{10,11},{12,13},{14,15},{16,17},{18,... | collective-permute-start | bytes 172040 | tf_op jit(solution)/shard_map/ppermute | solution.py:261
  27.6 4.9 %collective-permute-done.9.passed = f32[14,8,128]{2,1,0:T(8,128)S(1)} collective-permute-done((f32[14,8,128]{2,1,0:T(8,128)S(1)}, f32[14,8,128]{2,1,0:T(8,128)S(1)}, u32[]{:S(2)}, u32[]{:S(2)}) %collective-permute-start.9) | collective-permute-done | bytes 57376 | tf_op jit(solution)/shard_map/ppermute | solution.py:261
  32.5 0.0 all-to-all-done.got
  32.5 0.6 shard_map.70
  33.1 0.0 collective-permute-done.10
  33.1 0.2 collective-permute-done.11
  33.3 41.1 %all-gather = f32[224,8,128]{2,1,0:T(8,128)S(1)} all-gather(f32[14,8,128]{2,1,0:T(8,128)S(1)} %shard_map.70), channel_id=2, replica_groups=mesh['x'=4,'y'=4,'z'=16,'core'=2] {'z'}, dimensions={0}, use_global_device_ids=true | all-gather | bytes 974848 | tf_op jit(solution)/shard_map/all_gather | solution.py:268
  74.4 9.5 %collective-permute-start.13 = (f32[16,14,8,128]{3,2,1,0:T(8,128)S(1)}, f32[16,14,8,128]{3,2,1,0:T(8,128)S(1)}, u32[]{:S(2)}, u32[]{:S(2)}) collective-permute-start(f32[16,14,8,128]{3,2,1,0:T(8,128)S(1)} %bitcast.85), channel_id=1, source_target_pairs={{0,1},{1,0},{2,3},{3,2},{4,5},{5,4},{6,7},{7,6},{8,9},{9,8},{10,11... | collective-permute-start | bytes 2752520 | tf_op jit(solution)/shard_map/ppermute | solution.py:269
  83.9 2.1 %collective-permute-done.13.oth = f32[16,14,8,128]{3,2,1,0:T(8,128)S(1)} collective-permute-done((f32[16,14,8,128]{3,2,1,0:T(8,128)S(1)}, f32[16,14,8,128]{3,2,1,0:T(8,128)S(1)}, u32[]{:S(2)}, u32[]{:S(2)}) %collective-permute-start.13) | collective-permute-done | bytes 917536 | tf_op jit(solution)/shard_map/ppermute | solution.py:269
  86.0 6.0 %shard_map.71 = (f32[1024,256]{1,0:T(8,128)}, f32[1024,128]{1,0:T(8,128)S(1)}, f32[16,64,128]{2,1,0:T(8,128)}, f32[128,128]{1,0:T(8,128)S(1)}, f32[128,128]{1,0:T(8,128)S(1)}) custom-call(s32[128]{0:T(128)S(1)} %copy-done.1, f32[16,14,8,128]{3,2,1,0:T(8,128)S(1)} %bitcast.86, f32[16,14,8,128]{3,2,1,0:T(8,128)S(1)} %collective-permute-done.13.oth, ...), custom_call_target="tpu_custom_call" | custom-call | flops 500000000 | bytes 4194304 | tf_op jit(solution)/shard_map/pallas_call | solution.py:271
  91.9 7.2 %all-to-all-start.1 = ((f32[16,64,128]{2,1,0:T(8,128)}), f32[16,64,128]{2,1,0:T(8,128)S(1)}, u32[]{:S(2)}, u32[]{:S(2)}) async-start(f32[16,64,128]{2,1,0:T(8,128)} %get-tuple-element.47), calls=%async_computation.1 | async-start | bytes 1048576 | tf_op jit(solution)/shard_map/all_to_all | solution.py:282
  99.1 0.1 select_select_fusion.1
  99.2 0.7 collective-permute-start.14
  99.9 0.7 collective-permute-start.15
  100.6 1.3 %collective-permute-start.16 = (f32[256,256]{1,0:T(8,128)S(1)}, f32[256,256]{1,0:T(8,128)}, u32[]{:S(2)}, u32[]{:S(2)}) collective-permute-start(f32[256,256]{1,0:T(8,128)S(1)} %select_select_fusion.1), channel_id=1, source_target_pairs={{1,33},{2,34},{3,35},{4,36},{5,37},{6,38},{7,39},{8,40},{9,41},{10... | collective-permute-start | bytes 786440 | tf_op jit(solution)/shard_map/ppermute | solution.py:226
  101.9 6.6 %all-to-all-done.1.own = f32[16,64,128]{2,1,0:T(8,128)S(1)} async-done(((f32[16,64,128]{2,1,0:T(8,128)}), f32[16,64,128]{2,1,0:T(8,128)S(1)}, u32[]{:S(2)}, u32[]{:S(2)}) %all-to-all-start.1) | async-done | bytes 524320 | tf_op jit(solution)/shard_map/all_to_all | solution.py:282
  108.5 3.9 %collective-permute-start.17 = (f32[16,64,128]{2,1,0:T(8,128)S(1)}, f32[16,64,128]{2,1,0:T(8,128)S(1)}, u32[]{:S(2)}, u32[]{:S(2)}) collective-permute-start(f32[16,64,128]{2,1,0:T(8,128)S(1)} %all-to-all-done.1.own), channel_id=1, source_target_pairs={{0,1},{1,0},{2,3},{3,2},{4,5},{5,4},{6,7},{7,6},{8,9},{9,8},{10,11... | collective-permute-start | bytes 1572872 | tf_op jit(solution)/shard_map/ppermute | solution.py:283
  112.4 7.0 %collective-permute-done.16 = f32[256,256]{1,0:T(8,128)} collective-permute-done((f32[256,256]{1,0:T(8,128)S(1)}, f32[256,256]{1,0:T(8,128)}, u32[]{:S(2)}, u32[]{:S(2)}) %collective-permute-start.16) | collective-permute-done | bytes 262176 | tf_op jit(solution)/shard_map/ppermute | solution.py:226
  119.5 1.0 select_select_fusion.rows
  120.5 1.7 %shard_map.72 = (f32[1024,256]{1,0:T(8,128)S(1)}, f32[128,256]{1,0:T(8,128)S(1)}) custom-call(s32[128]{0:T(128)S(1)} %copy-done.1, f32[1024,256]{1,0:T(8,128)S(1)} %copy-done, f32[256,256]{1,0:T(8,128)S(1)} %select_select_fusion.rows, f32[1024,128]{1,0:T(8,128)S(1)} %get-tuple-element.43.plow, f32[128,128]{1,0:T(8,128)S(1)} %get-tuple-element.44.lsrc, ...), custom_call_target="tpu_custom_call" | custom-call | flops 500000000 | bytes 3145728 | tf_op jit(solution)/shard_map/pallas_call | solution.py:284
  122.2 2.1 %shard_map.73 = f32[1024,256]{1,0:T(8,128)} custom-call(s32[128]{0:T(128)S(1)} %copy-done.1, f32[1024,256]{1,0:T(8,128)S(1)} %get-tuple-element.46.cur, f32[16,64,128]{2,1,0:T(8,128)S(1)} %all-to-all-done.1.own, f32[16,64,128]{2,1,0:T(8,128)S(1)} %collective-permute-done.17.oth, f32[128,256]{1,0:T(8,128)S(1)} %get-tuple-element.48.kept), custom_call_target="tpu_custom_call" | custom-call | flops 500000000 | bytes 3145728 | tf_op jit(solution)/shard_map/pallas_call | solution.py:287
  (11 shorter events, 0.0 us)
Async XLA Ops:
  0.6 3.4 %copy-start = (f32[1024,256]{1,0:T(8,128)S(1)}, f32[1024,256]{1,0:T(8,128)}, u32[]{:S(2)}) copy-start(f32[1024,256]{1,0:T(8,128)} %a.1) | copy-start | bytes 3145732
  1.8 2.3 %collective-permute-start = (f32[7,8,8,256]{3,2,1,0:T(8,128)S(1)}, f32[7,8,8,256]{3,2,1,0:T(8,128)S(1)}, u32[]{:S(2)}, u32[]{:S(2)}) collective-permute-start(f32[7,8,8,256]{3,2,1,0:T(8,128)S(1)} %copy_bitcast_fusion), channel_id=1, source_target_pairs={{0,1},{32,33},{64,65},{96,97},{128,129},{160,161},{192,193},{224,2... | collective-permute-start | bytes 1376264 | tf_op jit(solution)/shard_map/ppermute | solution.py:240
  3.4 3.5 %collective-permute-start.8 = (f32[8,8,256]{2,1,0:T(8,128)S(1)}, f32[8,8,256]{2,1,0:T(8,128)S(1)}, u32[]{:S(2)}, u32[]{:S(2)}) collective-permute-start(f32[8,8,256]{2,1,0:T(8,128)S(1)} %get-tuple-element.57), channel_id=1, source_target_pairs={{0,2},{32,34},{64,66},{96,98},{128,130},{160,162},{192,194},{224,2... | collective-permute-start | bytes 196616 | tf_op jit(solution)/shard_map/ppermute | solution.py:247
  4.1 3.4 %collective-permute-start.1 = (f32[8,8,256]{2,1,0:T(8,128)S(1)}, f32[8,8,256]{2,1,0:T(8,128)S(1)}, u32[]{:S(2)}, u32[]{:S(2)}) collective-permute-start(f32[8,8,256]{2,1,0:T(8,128)S(1)} %get-tuple-element.56), channel_id=1, source_target_pairs={{0,16},{1,18},{32,48},{33,50},{64,80},{65,82},{96,112},{97,114},{1... | collective-permute-start | bytes 196616 | tf_op jit(solution)/shard_map/ppermute | solution.py:247
  4.8 3.4 %collective-permute-start.2 = (f32[8,8,256]{2,1,0:T(8,128)S(1)}, f32[8,8,256]{2,1,0:T(8,128)S(1)}, u32[]{:S(2)}, u32[]{:S(2)}) collective-permute-start(f32[8,8,256]{2,1,0:T(8,128)S(1)} %get-tuple-element.55), channel_id=1, source_target_pairs={{0,14},{1,20},{32,46},{33,52},{64,78},{65,84},{96,110},{97,116},{1... | collective-permute-start | bytes 196616 | tf_op jit(solution)/shard_map/ppermute | solution.py:247
  5.5 5.4 %collective-permute-start.3 = (f32[8,8,256]{2,1,0:T(8,128)S(1)}, f32[8,8,256]{2,1,0:T(8,128)S(1)}, u32[]{:S(2)}, u32[]{:S(2)}) collective-permute-start(f32[8,8,256]{2,1,0:T(8,128)S(1)} %get-tuple-element.54), channel_id=1, source_target_pairs={{0,12},{1,22},{32,44},{33,54},{64,76},{65,86},{96,108},{97,118},{1... | collective-permute-start | bytes 196616 | tf_op jit(solution)/shard_map/ppermute | solution.py:247
  6.2 4.8 %collective-permute-start.4 = (f32[8,8,256]{2,1,0:T(8,128)S(1)}, f32[8,8,256]{2,1,0:T(8,128)S(1)}, u32[]{:S(2)}, u32[]{:S(2)}) collective-permute-start(f32[8,8,256]{2,1,0:T(8,128)S(1)} %get-tuple-element.53), channel_id=1, source_target_pairs={{0,10},{1,24},{32,42},{33,56},{64,74},{65,88},{96,106},{97,120},{1... | collective-permute-start | bytes 196616 | tf_op jit(solution)/shard_map/ppermute | solution.py:247
  6.8 4.1 %collective-permute-start.5 = (f32[8,8,256]{2,1,0:T(8,128)S(1)}, f32[8,8,256]{2,1,0:T(8,128)S(1)}, u32[]{:S(2)}, u32[]{:S(2)}) collective-permute-start(f32[8,8,256]{2,1,0:T(8,128)S(1)} %get-tuple-element.52), channel_id=1, source_target_pairs={{0,8},{1,26},{32,40},{33,58},{64,72},{65,90},{96,104},{97,122},{12... | collective-permute-start | bytes 196616 | tf_op jit(solution)/shard_map/ppermute | solution.py:247
  7.5 3.4 %collective-permute-start.6 = (f32[8,8,256]{2,1,0:T(8,128)S(1)}, f32[8,8,256]{2,1,0:T(8,128)S(1)}, u32[]{:S(2)}, u32[]{:S(2)}) collective-permute-start(f32[8,8,256]{2,1,0:T(8,128)S(1)} %get-tuple-element.51), channel_id=1, source_target_pairs={{0,6},{1,28},{32,38},{33,60},{64,70},{65,92},{96,102},{97,124},{12... | collective-permute-start | bytes 196616 | tf_op jit(solution)/shard_map/ppermute | solution.py:247
  8.2 2.7 %collective-permute-start.7 = (f32[8,8,256]{2,1,0:T(8,128)S(1)}, f32[8,8,256]{2,1,0:T(8,128)S(1)}, u32[]{:S(2)}, u32[]{:S(2)}) collective-permute-start(f32[8,8,256]{2,1,0:T(8,128)S(1)} %get-tuple-element.50), channel_id=1, source_target_pairs={{0,4},{1,30},{32,36},{33,62},{64,68},{65,94},{96,100},{97,126},{12... | collective-permute-start | bytes 196616 | tf_op jit(solution)/shard_map/ppermute | solution.py:247
  10.9 0.7 copy-start.1
  12.9 19.6 %all-to-all-start = ((f32[16,5,8,128]{3,2,1,0:T(8,128)}), f32[16,5,8,128]{3,2,1,0:T(8,128)S(1)}, u32[]{:S(2)}, u32[]{:S(2)}) async-start(f32[16,5,8,128]{3,2,1,0:T(8,128)} %get-tuple-element.33), calls=%async_computation | async-start | bytes 655360 | tf_op jit(solution)/shard_map/all_to_all | solution.py:264
  19.7 13.4 %collective-permute-start.10 = (f32[256,256]{1,0:T(8,128)S(1)}, f32[256,256]{1,0:T(8,128)S(1)}, u32[]{:S(2)}, u32[]{:S(2)}) collective-permute-start(f32[256,256]{1,0:T(8,128)S(1)} %slice.71), channel_id=1, source_target_pairs={{1,129},{2,130},{3,131},{4,132},{5,133},{6,134},{7,135},{8,136},{9... | collective-permute-start | bytes 786440 | tf_op jit(solution)/shard_map/ppermute | solution.py:226
  22.8 10.4 %collective-permute-start.11 = (f32[256,256]{1,0:T(8,128)S(1)}, f32[256,256]{1,0:T(8,128)S(1)}, u32[]{:S(2)}, u32[]{:S(2)}) collective-permute-start(f32[256,256]{1,0:T(8,128)S(1)} %slice.71), channel_id=1, source_target_pairs={{1,257},{2,258},{3,259},{4,260},{5,261},{6,262},{7,263},{8,264},{9... | collective-permute-start | bytes 786440 | tf_op jit(solution)/shard_map/ppermute | solution.py:226
  25.0 8.3 %collective-permute-start.12 = (f32[256,256]{1,0:T(8,128)S(1)}, f32[256,256]{1,0:T(8,128)S(1)}, u32[]{:S(2)}, u32[]{:S(2)}) collective-permute-start(f32[256,256]{1,0:T(8,128)S(1)} %slice.71), channel_id=1, source_target_pairs={{1,385},{2,386},{3,387},{4,388},{5,389},{6,390},{7,391},{8,392},{9... | collective-permute-start | bytes 786440 | tf_op jit(solution)/shard_map/ppermute | solution.py:226
  26.3 6.2 %collective-permute-start.9 = (f32[14,8,128]{2,1,0:T(8,128)S(1)}, f32[14,8,128]{2,1,0:T(8,128)S(1)}, u32[]{:S(2)}, u32[]{:S(2)}) collective-permute-start(f32[14,8,128]{2,1,0:T(8,128)S(1)} %get-tuple-element.30), channel_id=1, source_target_pairs={{0,1},{2,3},{4,5},{6,7},{8,9},{10,11},{12,13},{14,15},{16,17},{18,... | collective-permute-start | bytes 172040 | tf_op jit(solution)/shard_map/ppermute | solution.py:261
  74.4 11.6 %copy-start.2 = (s32[2,128]{1,0:T(2,128)S(1)}, s32[2,128]{1,0:T(2,128)}, u32[]{:S(2)}) copy-start(s32[2,128]{1,0:T(2,128)} %perms.1) | copy-start | bytes 3076
  74.4 11.6 %collective-permute-start.13 = (f32[16,14,8,128]{3,2,1,0:T(8,128)S(1)}, f32[16,14,8,128]{3,2,1,0:T(8,128)S(1)}, u32[]{:S(2)}, u32[]{:S(2)}) collective-permute-start(f32[16,14,8,128]{3,2,1,0:T(8,128)S(1)} %bitcast.85), channel_id=1, source_target_pairs={{0,1},{1,0},{2,3},{3,2},{4,5},{5,4},{6,7},{7,6},{8,9},{9,8},{10,11... | collective-permute-start | bytes 2752520 | tf_op jit(solution)/shard_map/ppermute | solution.py:269
  91.9 16.6 %all-to-all-start.1 = ((f32[16,64,128]{2,1,0:T(8,128)}), f32[16,64,128]{2,1,0:T(8,128)S(1)}, u32[]{:S(2)}, u32[]{:S(2)}) async-start(f32[16,64,128]{2,1,0:T(8,128)} %get-tuple-element.47), calls=%async_computation.1 | async-start | bytes 1048576 | tf_op jit(solution)/shard_map/all_to_all | solution.py:282
  99.2 13.2 %collective-permute-start.14 = (f32[256,256]{1,0:T(8,128)S(1)}, f32[256,256]{1,0:T(8,128)S(1)}, u32[]{:S(2)}, u32[]{:S(2)}) collective-permute-start(f32[256,256]{1,0:T(8,128)S(1)} %select_select_fusion.1), channel_id=1, source_target_pairs={{1,97},{2,98},{3,99},{4,100},{5,101},{6,102},{7,103},{8,104},{9,10... | collective-permute-start | bytes 786440 | tf_op jit(solution)/shard_map/ppermute | solution.py:226
  99.9 12.5 %collective-permute-start.15 = (f32[256,256]{1,0:T(8,128)S(1)}, f32[256,256]{1,0:T(8,128)S(1)}, u32[]{:S(2)}, u32[]{:S(2)}) collective-permute-start(f32[256,256]{1,0:T(8,128)S(1)} %select_select_fusion.1), channel_id=1, source_target_pairs={{1,65},{2,66},{3,67},{4,68},{5,69},{6,70},{7,71},{8,72},{9,73},{10... | collective-permute-start | bytes 786440 | tf_op jit(solution)/shard_map/ppermute | solution.py:226
  100.6 18.9 %collective-permute-start.16 = (f32[256,256]{1,0:T(8,128)S(1)}, f32[256,256]{1,0:T(8,128)}, u32[]{:S(2)}, u32[]{:S(2)}) collective-permute-start(f32[256,256]{1,0:T(8,128)S(1)} %select_select_fusion.1), channel_id=1, source_target_pairs={{1,33},{2,34},{3,35},{4,36},{5,37},{6,38},{7,39},{8,40},{9,41},{10... | collective-permute-start | bytes 786440 | tf_op jit(solution)/shard_map/ppermute | solution.py:226
  108.5 13.7 %collective-permute-start.17 = (f32[16,64,128]{2,1,0:T(8,128)S(1)}, f32[16,64,128]{2,1,0:T(8,128)S(1)}, u32[]{:S(2)}, u32[]{:S(2)}) collective-permute-start(f32[16,64,128]{2,1,0:T(8,128)S(1)} %all-to-all-done.1.own), channel_id=1, source_target_pairs={{0,1},{1,0},{2,3},{3,2},{4,5},{5,4},{6,7},{7,6},{8,9},{9,8},{10,11... | collective-permute-start | bytes 1572872 | tf_op jit(solution)/shard_map/ppermute | solution.py:283

commit v5 on v3

--- a/solution.py
+++ b/solution.py
@@ -12,30 +12,32 @@
 NP = 16
 NZ = 16
 SLOTS = 8
+SENDS = ((8, 9), (7, 10), (6, 11), (5, 12), (4, 13), (3, 14), (2, 15), (1, 0))
+
+
+def dot16(a, b):
+    return jnp.dot(a, b, preferred_element_type=jnp.float32)
 
 
 def split(x):
     high = x.astype(jnp.bfloat16)
-    rest = x - high.astype(jnp.float32)
-    mid = rest.astype(jnp.bfloat16)
-    low = (rest - mid.astype(jnp.float32)).astype(jnp.bfloat16)
-    return high, mid, low
-
-
-def dot16(a, b):
-    return jnp.dot(a, b, preferred_element_type=jnp.float32)
+    return high, (x - high.astype(jnp.float32)).astype(jnp.bfloat16)
 
 
 def dot(a, b):
-    ah, am, al = split(a)
-    bh, bm, bl = split(b)
-    lead = jnp.concatenate([ah, am], axis=1)
-    tail = jnp.concatenate([ah, al], axis=1)
-    right = jnp.concatenate([bh, bm], axis=1)
-    first = dot16(lead, jnp.concatenate([right, right], axis=0))
-    second = dot16(tail, jnp.concatenate([bl, bh], axis=0))
+    left = jnp.concatenate(split(a), axis=1)
+    right = jnp.concatenate(split(b), axis=1)
+    both = dot16(left, jnp.concatenate([right, right], axis=0))
     n = b.shape[1]
-    return first[:, :n] + (first[:, n:] + second)
+    return both[:, :n] + both[:, n:]
+
+
+def reorder(perms, k, x):
+    hit = lax.broadcasted_iota(jnp.int32, (W, W), 0) == perms[k : k + 1, :]
+    order = jnp.where(hit, 1.0, 0.0).astype(jnp.float32).T.astype(jnp.bfloat16)
+    high, mid = split(x)
+    low = (x - high.astype(jnp.float32) - mid.astype(jnp.float32)).astype(jnp.bfloat16)
+    return dot16(order, high) + (dot16(order, mid) + dot16(order, low))
 
 
 def index_kernel(dest, row_mask, col_mask, meta, src):
@@ -63,7 +65,6 @@
     meta[2] = col_ok(0, 1)
     meta[3] = row_ok(0, head)
     meta[4] = lax.shift_right_logical(head, 3)
-    meta[5] = ((z == 0) & (core == 0)).astype(jnp.int32)
     for k in range(2):
         for j in range(2):
             meta[64 + 2 * k + j] = col_ok(k, block + j)
@@ -74,19 +75,20 @@
         meta[24 + slot] = row_ok(0, src[0, here])
         meta[32 + slot] = lax.shift_right_logical(dest[1, here], 3)
         meta[40 + slot] = lax.shift_right_logical(src[1, here], 3)
-        meta[48 + slot] = lax.shift_right_logical(dest[0, here], 3)
         meta[56 + slot] = lax.shift_right_logical(src[0, here], 3)
 
 
-def route_kernel(meta, a, own, *refs):
+def route_kernel(dest, a, own, *refs):
     got, (out, panel, last) = refs[:-3], refs[-3:]
-    share = own[...] * meta[5].astype(jnp.float32)
+    me = lax.axis_index("x") * 4 + lax.axis_index("y")
+    root = (lax.axis_index("z") == 0) & (lax.axis_index("core") == 0)
+    share = own[...] * root.astype(jnp.float32)
     for ref in got:
         share = share + ref[...]
     out[...] = jnp.zeros_like(out)
     for slot in range(SLOTS):
         left, right = share[slot, :, :W], share[slot, :, W:]
-        out[meta[48 + slot], 0] = left
+        out[lax.shift_right_logical(dest[0, me * SLOTS + slot], 3), 0] = left
         if slot < 7:
             panel[slot] = left
             panel[7 + slot] = right
@@ -118,11 +120,6 @@
         out[13] = got[0, 4]
 
 
-def order(perms, k):
-    hit = lax.broadcasted_iota(jnp.int32, (W, W), 0) == perms[k : k + 1, :]
-    return jnp.where(hit, 1.0, 0.0).astype(jnp.float32).T
-
-
 def refine(pivot):
     row = lax.broadcasted_iota(jnp.int32, (W, W), 0)
     col = lax.broadcasted_iota(jnp.int32, (W, W), 1)
@@ -146,11 +143,11 @@
             [block[s * W : (s + 1) * W] * flag(base + s) for s in range(SLOTS)], axis=0
         )
 
-    inv0 = refine(dot(order(perms, 0), tile(head, 10)))
-    kept01 = dot(order(perms, 0), tile(head, 11)) * flag(2)
+    inv0 = refine(reorder(perms, 0, tile(head, 10)))
+    kept01 = reorder(perms, 0, tile(head, 11)) * flag(2)
     low_src = dot(tile(head, 12), inv0) * flag(3)
     lsrc[...] = low_src
-    inv1 = refine(dot(order(perms, 1), tile(head, 13) - dot(low_src, kept01)))
+    inv1 = refine(reorder(perms, 1, tile(head, 13) - dot(low_src, kept01)))
     col0 = jnp.concatenate([tile(panel, s) for s in range(7)] + [tile(head, 0)], axis=0)
     lpan[:, :W] = flagged(dot(col0, inv0), 8)
     ext0 = jnp.concatenate([tile(head, 2 + s) for s in range(SLOTS)], axis=0)
@@ -184,9 +181,9 @@
     rows = jnp.concatenate(
         [got[:, H : H + 16].reshape(2 * W, W), got[:, H + 16 :].reshape(2 * W, W)], axis=1
     )
-    up0 = dot(order(perms, 0), rows[:W])
+    up0 = reorder(perms, 0, rows[:W])
     kept0 = masked(up0, 0)
-    up1 = dot(order(perms, 1), rows[W:] - dot(lsrc[...], kept0))
+    up1 = reorder(perms, 1, rows[W:] - dot(lsrc[...], kept0))
     kept[...] = masked(up1, 1)
     prod = dot(plow[...], kept0)
     cur[...] = a[...] - prod
@@ -228,29 +225,28 @@
 def shards(a, row_perms, dest_rows, row_mask, col_mask):
     core = lax.axis_index("core")
     smem = pl.BlockSpec(memory_space=pltpu.SMEM)
+    over = lax.ppermute(a, ("z", "core"), [(0, 1)]).reshape(SLOTS, NZ, 8, 2 * W)
+    cut = a.reshape(SLOTS, NZ, 8, 2 * W)
+    got = []
+    for z0, z1 in reversed(SENDS):
+        pairs, piece = [(0, 2 * z0)], cut[:, z0]
+        if z1:
+            pairs.append((1, 2 * z1))
+            piece = jnp.where(core == 0, piece, over[:, z1])
+        got.append(lax.ppermute(piece, ("z", "core"), pairs))
+
+    out0, panel, last = call(
+        route_kernel, (f32(NP, 9, 8, W), f32(14, 8, W), f32(2, 8, W)), 10, moved=2**20
+    )(dest_rows, a[: 2 * W], cut[:, 0], *got)
+    out0, maps = lax.optimization_barrier((out0, (dest_rows, row_mask, col_mask)))
+    passed = lax.ppermute(panel, "core", [(0, 1)])
     meta = pl.pallas_call(
         index_kernel,
         out_shape=jax.ShapeDtypeStruct((W,), jnp.int32),
         in_specs=[smem] * 3,
         out_specs=smem,
         scratch_shapes=[pltpu.SMEM((2, W), jnp.int32)],
-    )(dest_rows, row_mask, col_mask)
-
-    cut = a.reshape(SLOTS, NZ, 8, 2 * W)
-    over = lax.ppermute(cut[:, 8:].transpose(1, 0, 2, 3), "core", [(0, 1)])
-    pieces = [jnp.where(core == 0, cut[:, step % 8], over[8 - step]) for step in range(1, 9)]
-    pieces, meta = lax.optimization_barrier((pieces, meta))
-    got = []
-    for step in range(1, 9):
-        pairs = [(1, 2 * (NZ - step))]
-        if step < 8:
-            pairs.append((0, 2 * step))
-        got.append(lax.ppermute(pieces[step - 1], ("z", "core"), pairs))
-
-    out0, panel, last = call(
-        route_kernel, (f32(NP, 9, 8, W), f32(14, 8, W), f32(2, 8, W)), 10, moved=2**20
-    )(meta, a[: 2 * W], pieces[7], *got)
-    passed = lax.ppermute(panel, "core", [(0, 1)])
+    )(*maps)
     got0 = lax.all_to_all(out0, ("x", "y"), 0, 0, tiled=True)
     payload, chunk = call(pack_kernel, (f32(14, 8, W), f32(4, 8, W)), 3, moved=2**19)(
         meta, passed, last, got0

time: 117 us -> 118 us (level)
  starting transfers between devices: 40.1 us -> 42.9 us
  waiting for transfers between devices: 18.7 us -> 17 us
    ppermute x1, starting transfers between devices: 10.8 us -> 13.1 us  [shards(): oth = lax.ppermute(own, 'core', [(0, 1), (1, 0)])]
    all_to_all x1, waiting for transfers between devices: 7.23 us -> 5.64 us  [shards(): got0 = lax.all_to_all(out0, ('x', 'y'), 0, 0, tiled=True)]
    ppermute x1, waiting for transfers between devices: 1.84 us -> 0.41 us  [shards(): passed = lax.ppermute(panel, 'core', [(0, 1)])]
    ppermute x9, waiting for transfers between devices: 7.52 us -> 8.89 us  [the longest x1 7.65 us: shards(): over = lax.ppermute(a, ('z', 'core'), [(0, 1)]).reshape(SLOTS, NZ, 8, 2 * W)]
  transfers between devices with their start and end apart: 13 -> 13, of which waited for: 5 -> 5; matrix products, arithmetic and copies ran while one was open for 0% -> 2% of each run, Pallas kernels for 3% -> 3%
where the time goes in v5:
time: 118 us
  starting transfers between devices  42.9 us (36%)
  blocking collectives  42.4 us (36%)
  waiting for transfers between devices  17 us (14%)
  Pallas kernels  12.6 us (11%)
    all_gather x1, blocking collectives, shards(): own = lax.all_gather(payload, 'z', axis=0, tiled=False)  25.4 us
    all_to_all x1, blocking collectives, shards(): got1 = lax.all_to_all(send, ('x', 'y'), 0, 0, tiled=True)  17 us
    ppermute x8, starting transfers between devices, shards(): got.append(lax.ppermute(piece, ('z', 'core'), pairs))  16.6 us
    ppermute x1, starting transfers between devices, shards(): oth = lax.ppermute(own, 'core', [(0, 1), (1, 0)])  13.1 us
    ppermute x1, waiting for transfers between devices, shards(): over = lax.ppermute(a, ('z', 'core'), [(0, 1)]).reshape(SLOTS, NZ, 8, 2 * W)  7.65 us
    all_to_all x1, starting transfers between devices, shards(): got0 = lax.all_to_all(out0, ('x', 'y'), 0, 0, tiled=True)  6.75 us
    all_to_all x1, waiting for transfers between devices, shards(): got0 = lax.all_to_all(out0, ('x', 'y'), 0, 0, tiled=True)  5.64 us
    pallas_call x1, Pallas kernels, shards(): call(factor_kernel, (f32(SLOTS * W, 2 * W), f32(SLOTS * W, W), f32(NP, H...  5.16 us
  transfers between devices with their start and end apart: 13, of which 5 were waited for; matrix products, arithmetic and copies ran while one was open for 2% of the time, Pallas kernels for 3%

profile of v5, /device:TPU:1, one launch (start us, length us, event | category | flops | bytes accessed | tf_op | source)
XLA Modules:
  0.0 117.9 jit_solution(13542443471712301180)
XLA Ops:
  0.6 0.0 copy-start
  0.6 1.4 %collective-permute-start.1 = (f32[1024,256]{1,0:T(8,128)}, f32[1024,256]{1,0:T(8,128)S(1)}, u32[]{:S(2)}, u32[]{:S(2)}) collective-permute-start(f32[1024,256]{1,0:T(8,128)} %a.1), channel_id=1, source_target_pairs={{0,1},{32,33},{64,65},{96,97},{128,129},{160,161},{192,193},{224,2... | collective-permute-start | bytes 3145736 | tf_op jit(solution)/shard_map/ppermute | solution.py:228
  2.1 0.9 slice_bitcast_fusion.14
  3.0 0.7 collective-permute-start
  3.6 7.7 %collective-permute-done.1 = f32[1024,256]{1,0:T(8,128)S(1)} collective-permute-done((f32[1024,256]{1,0:T(8,128)}, f32[1024,256]{1,0:T(8,128)S(1)}, u32[]{:S(2)}, u32[]{:S(2)}) %collective-permute-start.1) | collective-permute-done | bytes 1048608 | tf_op jit(solution)/shard_map/ppermute | solution.py:228
  11.3 1.1 fusion.1
  12.4 8.2 %collective-permute-start.8 = (f32[8,8,256]{2,1,0:T(8,128)S(1)}, f32[8,8,256]{2,1,0:T(8,128)S(1)}, u32[]{:S(2)}, u32[]{:S(2)}) collective-permute-start(f32[8,8,256]{2,1,0:T(8,128)S(1)} %get-tuple-element.32), channel_id=1, source_target_pairs={{0,16},{1,18},{32,48},{33,50},{64,80},{65,82},{96,112},{97,114},{1... | collective-permute-start | bytes 196616 | tf_op jit(solution)/shard_map/ppermute | solution.py:236
  20.6 1.3 %collective-permute-start.7 = (f32[8,8,256]{2,1,0:T(8,128)S(1)}, f32[8,8,256]{2,1,0:T(8,128)S(1)}, u32[]{:S(2)}, u32[]{:S(2)}) collective-permute-start(f32[8,8,256]{2,1,0:T(8,128)S(1)} %get-tuple-element.33), channel_id=1, source_target_pairs={{0,14},{1,20},{32,46},{33,52},{64,78},{65,84},{96,110},{97,116},{1... | collective-permute-start | bytes 196616 | tf_op jit(solution)/shard_map/ppermute | solution.py:236
  21.9 1.3 %collective-permute-start.6 = (f32[8,8,256]{2,1,0:T(8,128)S(1)}, f32[8,8,256]{2,1,0:T(8,128)S(1)}, u32[]{:S(2)}, u32[]{:S(2)}) collective-permute-start(f32[8,8,256]{2,1,0:T(8,128)S(1)} %get-tuple-element.34), channel_id=1, source_target_pairs={{0,12},{1,22},{32,44},{33,54},{64,76},{65,86},{96,108},{97,118},{1... | collective-permute-start | bytes 196616 | tf_op jit(solution)/shard_map/ppermute | solution.py:236
  23.2 1.3 %collective-permute-start.5 = (f32[8,8,256]{2,1,0:T(8,128)S(1)}, f32[8,8,256]{2,1,0:T(8,128)S(1)}, u32[]{:S(2)}, u32[]{:S(2)}) collective-permute-start(f32[8,8,256]{2,1,0:T(8,128)S(1)} %get-tuple-element.35), channel_id=1, source_target_pairs={{0,10},{1,24},{32,42},{33,56},{64,74},{65,88},{96,106},{97,120},{1... | collective-permute-start | bytes 196616 | tf_op jit(solution)/shard_map/ppermute | solution.py:236
  24.5 0.0 collective-permute-done.refs_0_
  24.5 1.3 %collective-permute-start.4 = (f32[8,8,256]{2,1,0:T(8,128)S(1)}, f32[8,8,256]{2,1,0:T(8,128)S(1)}, u32[]{:S(2)}, u32[]{:S(2)}) collective-permute-start(f32[8,8,256]{2,1,0:T(8,128)S(1)} %get-tuple-element.36), channel_id=1, source_target_pairs={{0,8},{1,26},{32,40},{33,58},{64,72},{65,90},{96,104},{97,122},{12... | collective-permute-start | bytes 196616 | tf_op jit(solution)/shard_map/ppermute | solution.py:236
  25.8 0.0 collective-permute-done.8.refs_7_
  25.8 1.3 %collective-permute-start.3 = (f32[8,8,256]{2,1,0:T(8,128)S(1)}, f32[8,8,256]{2,1,0:T(8,128)S(1)}, u32[]{:S(2)}, u32[]{:S(2)}) collective-permute-start(f32[8,8,256]{2,1,0:T(8,128)S(1)} %get-tuple-element.37), channel_id=1, source_target_pairs={{0,6},{1,28},{32,38},{33,60},{64,70},{65,92},{96,102},{97,124},{12... | collective-permute-start | bytes 196616 | tf_op jit(solution)/shard_map/ppermute | solution.py:236
  27.1 0.0 collective-permute-done.7.refs_6_
  27.1 1.3 %collective-permute-start.2 = (f32[8,8,256]{2,1,0:T(8,128)S(1)}, f32[8,8,256]{2,1,0:T(8,128)S(1)}, u32[]{:S(2)}, u32[]{:S(2)}) collective-permute-start(f32[8,8,256]{2,1,0:T(8,128)S(1)} %get-tuple-element.38), channel_id=1, source_target_pairs={{0,4},{1,30},{32,36},{33,62},{64,68},{65,94},{96,100},{97,126},{12... | collective-permute-start | bytes 196616 | tf_op jit(solution)/shard_map/ppermute | solution.py:236
  28.4 0.0 copy-done
  28.5 0.0 copy-start.3
  28.5 0.0 collective-permute-done.6.refs_5_
  28.5 0.0 collective-permute-done.5.refs_4_
  28.5 0.0 collective-permute-done.4.refs_3_
  28.5 0.0 collective-permute-done.3.refs_2_
  28.5 1.2 %collective-permute-done.2.refs_1_ = f32[8,8,256]{2,1,0:T(8,128)S(1)} collective-permute-done((f32[8,8,256]{2,1,0:T(8,128)S(1)}, f32[8,8,256]{2,1,0:T(8,128)S(1)}, u32[]{:S(2)}, u32[]{:S(2)}) %collective-permute-start.2) | collective-permute-done | bytes 65568 | tf_op jit(solution)/shard_map/ppermute | solution.py:236
  29.7 0.0 copy-done.3
  29.7 1.5 %shard_map.68 = (f32[16,9,8,128]{3,2,1,0:T(8,128)}, f32[14,8,128]{2,1,0:T(8,128)S(1)}, f32[2,8,128]{2,1,0:T(8,128)S(1)}) custom-call(s32[2,128]{1,0:T(2,128)S(1)} %copy-done.3, f32[256,256]{1,0:T(8,128)S(1)} %slice.54.a, f32[8,8,256]{2,1,0:T(8,128)S(1)} %get-tuple-element.40.own, f32[8,8,256]{2,1,0:T(8,128)S(1)} %collective-permute-done.refs_0_, ...), custom_call_target="tpu_custom_call" | custom-call | bytes 1048576 | tf_op jit(solution)/shard_map/pallas_call | solution.py:238
  31.2 6.8 %all-to-all-start = ((f32[16,9,8,128]{3,2,1,0:T(8,128)}), f32[16,9,8,128]{3,2,1,0:T(8,128)S(1)}, u32[]{:S(2)}, u32[]{:S(2)}) async-start(f32[16,9,8,128]{3,2,1,0:T(8,128)} %get-tuple-element.23), calls=%async_computation | async-start | bytes 1179648 | tf_op jit(solution)/shard_map/all_to_all | solution.py:250
  38.0 1.3 %collective-permute-start.9 = (f32[14,8,128]{2,1,0:T(8,128)S(1)}, f32[14,8,128]{2,1,0:T(8,128)S(1)}, u32[]{:S(2)}, u32[]{:S(2)}) collective-permute-start(f32[14,8,128]{2,1,0:T(8,128)S(1)} %get-tuple-element.21), channel_id=1, source_target_pairs={{0,1},{2,3},{4,5},{6,7},{8,9},{10,11},{12,13},{14,15},{16,17},{18,... | collective-permute-start | bytes 172040 | tf_op jit(solution)/shard_map/ppermute | solution.py:242
  39.3 2.0 %shard_map.69.meta = s32[128]{0:T(128)} custom-call(s32[2,128]{1,0:T(2,128)} %dest.2, s32[2,128]{1,0:T(2,128)} %row_mask, s32[2,64]{1,0:T(2,128)} %col_mask), custom_call_target="tpu_custom_call" | custom-call | tf_op jit(solution)/shard_map/pallas_call | solution.py:243
  41.2 0.0 copy-start.1
  41.2 0.4 collective-permute-done.9.passed
  41.7 5.6 %all-to-all-done.got = f32[16,9,8,128]{3,2,1,0:T(8,128)S(1)} async-done(((f32[16,9,8,128]{3,2,1,0:T(8,128)}), f32[16,9,8,128]{3,2,1,0:T(8,128)S(1)}, u32[]{:S(2)}, u32[]{:S(2)}) %all-to-all-start) | async-done | bytes 589856 | tf_op jit(solution)/shard_map/all_to_all | solution.py:250
  47.3 0.0 copy-done.1
  47.3 0.6 shard_map.70
  47.9 25.4 %all-gather = f32[224,8,128]{2,1,0:T(8,128)S(1)} all-gather(f32[14,8,128]{2,1,0:T(8,128)S(1)} %get-tuple-element.24), channel_id=2, replica_groups=mesh['x'=4,'y'=4,'z'=16,'core'=2] {'z'}, dimensions={0}, use_global_device_ids=true | all-gather | bytes 974848 | tf_op jit(solution)/shard_map/all_gather | solution.py:255
  73.3 0.0 copy-start.2
  73.3 13.1 %collective-permute-start.10 = (f32[16,14,8,128]{3,2,1,0:T(8,128)S(1)}, f32[16,14,8,128]{3,2,1,0:T(8,128)S(1)}, u32[]{:S(2)}, u32[]{:S(2)}) collective-permute-start(f32[16,14,8,128]{3,2,1,0:T(8,128)S(1)} %bitcast.95), channel_id=1, source_target_pairs={{0,1},{1,0},{2,3},{3,2},{4,5},{5,4},{6,7},{7,6},{8,9},{9,8},{10,11... | collective-permute-start | bytes 2752520 | tf_op jit(solution)/shard_map/ppermute | solution.py:256
  86.4 2.1 %collective-permute-done.10.oth = f32[16,14,8,128]{3,2,1,0:T(8,128)S(1)} collective-permute-done((f32[16,14,8,128]{3,2,1,0:T(8,128)S(1)}, f32[16,14,8,128]{3,2,1,0:T(8,128)S(1)}, u32[]{:S(2)}, u32[]{:S(2)}) %collective-permute-start.10) | collective-permute-done | bytes 917536 | tf_op jit(solution)/shard_map/ppermute | solution.py:256
  88.5 0.0 copy-done.2
  88.5 5.2 %shard_map.71 = (f32[1024,256]{1,0:T(8,128)}, f32[1024,128]{1,0:T(8,128)S(1)}, f32[16,96,128]{2,1,0:T(8,128)S(1)}, f32[128,128]{1,0:T(8,128)S(1)}) custom-call(s32[128]{0:T(128)S(1)} %copy-done.1, f32[16,14,8,128]{3,2,1,0:T(8,128)S(1)} %bitcast.96, f32[16,14,8,128]{3,2,1,0:T(8,128)S(1)} %collective-permute-done.10.oth, ...), custom_call_target="tpu_custom_call" | custom-call | flops 500000000 | bytes 4194304 | tf_op jit(solution)/shard_map/pallas_call | solution.py:258
  93.7 17.0 %all_to_all.10.got.own = f32[16,96,128]{2,1,0:T(8,128)S(1)} all-to-all(f32[16,96,128]{2,1,0:T(8,128)S(1)} %get-tuple-element.26), channel_id=1, replica_groups=mesh['x'=4,'y'=4,'z'=16,'core'=2] {'x','y'}, dimensions={0} | all-to-all | bytes 1572864 | tf_op jit(solution)/shard_map/all_to_all | solution.py:266
  110.7 3.7 %collective-permute-start.11 = (f32[16,64,128]{2,1,0:T(8,128)S(1)}, f32[16,64,128]{2,1,0:T(8,128)S(1)}, u32[]{:S(2)}, u32[]{:S(2)}) collective-permute-start(f32[16,64,128]{2,1,0:T(8,128)S(1)} %slice.88), channel_id=1, source_target_pairs={{0,1},{1,0},{2,3},{3,2},{4,5},{5,4},{6,7},{7,6},{8,9},{9,8},{10,11... | collective-permute-start | bytes 1572872 | tf_op jit(solution)/shard_map/ppermute | solution.py:267
  114.4 1.5 %shard_map.72 = (f32[1024,256]{1,0:T(8,128)S(1)}, f32[128,256]{1,0:T(8,128)S(1)}) custom-call(s32[128]{0:T(128)S(1)} %copy-done.1, f32[1024,256]{1,0:T(8,128)S(1)} %copy-done, f32[16,96,128]{2,1,0:T(8,128)S(1)} %all_to_all.10.got.own, f32[1024,128]{1,0:T(8,128)S(1)} %get-tuple-element.27.plow, f32[128,128]{1,0:T(8,128)S(1)} %get-tuple-element.28.lsrc, ...), custom_call_target="tpu_custom_call" | custom-call | flops 500000000 | bytes 3145728 | tf_op jit(solution)/shard_map/pallas_call | solution.py:268
  115.9 0.0 collective-permute-done.11.oth
  115.9 2.0 %shard_map.73 = f32[1024,256]{1,0:T(8,128)} custom-call(s32[128]{0:T(128)S(1)} %copy-done.1, f32[1024,256]{1,0:T(8,128)S(1)} %get-tuple-element.29.cur, f32[16,96,128]{2,1,0:T(8,128)S(1)} %all_to_all.10.got.own, f32[16,64,128]{2,1,0:T(8,128)S(1)} %collective-permute-done.11.oth, f32[128,256]{1,0:T(8,128)S(1)} %get-tuple-element.30.kept), custom_call_target="tpu_custom_call" | custom-call | flops 500000000 | bytes 3145728 | tf_op jit(solution)/shard_map/pallas_call | solution.py:271
  (2 shorter events, 0.1 us)
Async XLA Ops:
  0.6 27.8 %copy-start = (f32[1024,256]{1,0:T(8,128)S(1)}, f32[1024,256]{1,0:T(8,128)}, u32[]{:S(2)}) copy-start(f32[1024,256]{1,0:T(8,128)} %a.1) | copy-start | bytes 3145732
  0.6 10.7 %collective-permute-start.1 = (f32[1024,256]{1,0:T(8,128)}, f32[1024,256]{1,0:T(8,128)S(1)}, u32[]{:S(2)}, u32[]{:S(2)}) collective-permute-start(f32[1024,256]{1,0:T(8,128)} %a.1), channel_id=1, source_target_pairs={{0,1},{32,33},{64,65},{96,97},{128,129},{160,161},{192,193},{224,2... | collective-permute-start | bytes 3145736 | tf_op jit(solution)/shard_map/ppermute | solution.py:228
  3.0 21.5 %collective-permute-start = (f32[8,8,256]{2,1,0:T(8,128)S(1)}, f32[8,8,256]{2,1,0:T(8,128)S(1)}, u32[]{:S(2)}, u32[]{:S(2)}) collective-permute-start(f32[8,8,256]{2,1,0:T(8,128)S(1)} %get-tuple-element.39), channel_id=1, source_target_pairs={{0,2},{32,34},{64,66},{96,98},{128,130},{160,162},{192,194},{224,2... | collective-permute-start | bytes 196616 | tf_op jit(solution)/shard_map/ppermute | solution.py:236
  12.4 13.4 %collective-permute-start.8 = (f32[8,8,256]{2,1,0:T(8,128)S(1)}, f32[8,8,256]{2,1,0:T(8,128)S(1)}, u32[]{:S(2)}, u32[]{:S(2)}) collective-permute-start(f32[8,8,256]{2,1,0:T(8,128)S(1)} %get-tuple-element.32), channel_id=1, source_target_pairs={{0,16},{1,18},{32,48},{33,50},{64,80},{65,82},{96,112},{97,114},{1... | collective-permute-start | bytes 196616 | tf_op jit(solution)/shard_map/ppermute | solution.py:236
  20.6 6.5 %collective-permute-start.7 = (f32[8,8,256]{2,1,0:T(8,128)S(1)}, f32[8,8,256]{2,1,0:T(8,128)S(1)}, u32[]{:S(2)}, u32[]{:S(2)}) collective-permute-start(f32[8,8,256]{2,1,0:T(8,128)S(1)} %get-tuple-element.33), channel_id=1, source_target_pairs={{0,14},{1,20},{32,46},{33,52},{64,78},{65,84},{96,110},{97,116},{1... | collective-permute-start | bytes 196616 | tf_op jit(solution)/shard_map/ppermute | solution.py:236
  21.9 6.6 %collective-permute-start.6 = (f32[8,8,256]{2,1,0:T(8,128)S(1)}, f32[8,8,256]{2,1,0:T(8,128)S(1)}, u32[]{:S(2)}, u32[]{:S(2)}) collective-permute-start(f32[8,8,256]{2,1,0:T(8,128)S(1)} %get-tuple-element.34), channel_id=1, source_target_pairs={{0,12},{1,22},{32,44},{33,54},{64,76},{65,86},{96,108},{97,118},{1... | collective-permute-start | bytes 196616 | tf_op jit(solution)/shard_map/ppermute | solution.py:236
  23.2 5.3 %collective-permute-start.5 = (f32[8,8,256]{2,1,0:T(8,128)S(1)}, f32[8,8,256]{2,1,0:T(8,128)S(1)}, u32[]{:S(2)}, u32[]{:S(2)}) collective-permute-start(f32[8,8,256]{2,1,0:T(8,128)S(1)} %get-tuple-element.35), channel_id=1, source_target_pairs={{0,10},{1,24},{32,42},{33,56},{64,74},{65,88},{96,106},{97,120},{1... | collective-permute-start | bytes 196616 | tf_op jit(solution)/shard_map/ppermute | solution.py:236
  24.5 4.0 %collective-permute-start.4 = (f32[8,8,256]{2,1,0:T(8,128)S(1)}, f32[8,8,256]{2,1,0:T(8,128)S(1)}, u32[]{:S(2)}, u32[]{:S(2)}) collective-permute-start(f32[8,8,256]{2,1,0:T(8,128)S(1)} %get-tuple-element.36), channel_id=1, source_target_pairs={{0,8},{1,26},{32,40},{33,58},{64,72},{65,90},{96,104},{97,122},{12... | collective-permute-start | bytes 196616 | tf_op jit(solution)/shard_map/ppermute | solution.py:236
  25.8 2.7 %collective-permute-start.3 = (f32[8,8,256]{2,1,0:T(8,128)S(1)}, f32[8,8,256]{2,1,0:T(8,128)S(1)}, u32[]{:S(2)}, u32[]{:S(2)}) collective-permute-start(f32[8,8,256]{2,1,0:T(8,128)S(1)} %get-tuple-element.37), channel_id=1, source_target_pairs={{0,6},{1,28},{32,38},{33,60},{64,70},{65,92},{96,102},{97,124},{12... | collective-permute-start | bytes 196616 | tf_op jit(solution)/shard_map/ppermute | solution.py:236
  27.1 2.6 %collective-permute-start.2 = (f32[8,8,256]{2,1,0:T(8,128)S(1)}, f32[8,8,256]{2,1,0:T(8,128)S(1)}, u32[]{:S(2)}, u32[]{:S(2)}) collective-permute-start(f32[8,8,256]{2,1,0:T(8,128)S(1)} %get-tuple-element.38), channel_id=1, source_target_pairs={{0,4},{1,30},{32,36},{33,62},{64,68},{65,94},{96,100},{97,126},{12... | collective-permute-start | bytes 196616 | tf_op jit(solution)/shard_map/ppermute | solution.py:236
  28.5 1.3 %copy-start.3 = (s32[2,128]{1,0:T(2,128)S(1)}, s32[2,128]{1,0:T(2,128)}, u32[]{:S(2)}) copy-start(s32[2,128]{1,0:T(2,128)} %dest.2) | copy-start | bytes 3076
  31.2 16.1 %all-to-all-start = ((f32[16,9,8,128]{3,2,1,0:T(8,128)}), f32[16,9,8,128]{3,2,1,0:T(8,128)S(1)}, u32[]{:S(2)}, u32[]{:S(2)}) async-start(f32[16,9,8,128]{3,2,1,0:T(8,128)} %get-tuple-element.23), calls=%async_computation | async-start | bytes 1179648 | tf_op jit(solution)/shard_map/all_to_all | solution.py:250
  38.0 3.7 %collective-permute-start.9 = (f32[14,8,128]{2,1,0:T(8,128)S(1)}, f32[14,8,128]{2,1,0:T(8,128)S(1)}, u32[]{:S(2)}, u32[]{:S(2)}) collective-permute-start(f32[14,8,128]{2,1,0:T(8,128)S(1)} %get-tuple-element.21), channel_id=1, source_target_pairs={{0,1},{2,3},{4,5},{6,7},{8,9},{10,11},{12,13},{14,15},{16,17},{18,... | collective-permute-start | bytes 172040 | tf_op jit(solution)/shard_map/ppermute | solution.py:242
  41.2 6.1 %copy-start.1 = (s32[128]{0:T(128)S(1)}, s32[128]{0:T(128)}, u32[]{:S(2)}) copy-start(s32[128]{0:T(128)} %shard_map.69.meta) | copy-start | bytes 1540
  73.3 15.2 %copy-start.2 = (s32[2,128]{1,0:T(2,128)S(1)}, s32[2,128]{1,0:T(2,128)}, u32[]{:S(2)}) copy-start(s32[2,128]{1,0:T(2,128)} %perms.1) | copy-start | bytes 3076
  73.3 15.2 %collective-permute-start.10 = (f32[16,14,8,128]{3,2,1,0:T(8,128)S(1)}, f32[16,14,8,128]{3,2,1,0:T(8,128)S(1)}, u32[]{:S(2)}, u32[]{:S(2)}) collective-permute-start(f32[16,14,8,128]{3,2,1,0:T(8,128)S(1)} %bitcast.95), channel_id=1, source_target_pairs={{0,1},{1,0},{2,3},{3,2},{4,5},{5,4},{6,7},{7,6},{8,9},{9,8},{10,11... | collective-permute-start | bytes 2752520 | tf_op jit(solution)/shard_map/ppermute | solution.py:256
  110.7 5.2 %collective-permute-start.11 = (f32[16,64,128]{2,1,0:T(8,128)S(1)}, f32[16,64,128]{2,1,0:T(8,128)S(1)}, u32[]{:S(2)}, u32[]{:S(2)}) collective-permute-start(f32[16,64,128]{2,1,0:T(8,128)S(1)} %slice.88), channel_id=1, source_target_pairs={{0,1},{1,0},{2,3},{3,2},{4,5},{5,4},{6,7},{7,6},{8,9},{9,8},{10,11... | collective-permute-start | bytes 1572872 | tf_op jit(solution)/shard_map/ppermute | solution.py:267

commit v6 on v5

--- a/solution.py
+++ b/solution.py
@@ -12,7 +12,6 @@
 NP = 16
 NZ = 16
 SLOTS = 8
-SENDS = ((8, 9), (7, 10), (6, 11), (5, 12), (4, 13), (3, 14), (2, 15), (1, 0))
 
 
 def dot16(a, b):
@@ -223,20 +222,33 @@
 
 
 def shards(a, row_perms, dest_rows, row_mask, col_mask):
-    core = lax.axis_index("core")
+    z = lax.axis_index("z")
     smem = pl.BlockSpec(memory_space=pltpu.SMEM)
-    over = lax.ppermute(a, ("z", "core"), [(0, 1)]).reshape(SLOTS, NZ, 8, 2 * W)
     cut = a.reshape(SLOTS, NZ, 8, 2 * W)
-    got = []
-    for z0, z1 in reversed(SENDS):
-        pairs, piece = [(0, 2 * z0)], cut[:, z0]
-        if z1:
-            pairs.append((1, 2 * z1))
-            piece = jnp.where(core == 0, piece, over[:, z1])
-        got.append(lax.ppermute(piece, ("z", "core"), pairs))
+
+    def along(x, *pairs):
+        return lax.ppermute(x, ("z", "core"), [(2 * src, 2 * dst) for src, dst in pairs])
+
+    near = [along(cut[:, k], (0, k)) for k in (3, 2, 1)]
+    four = along(cut[:, 4:10].transpose(1, 0, 2, 3), (0, 4))
+    part, near, four = lax.optimization_barrier((cut[:, 10:13].transpose(1, 0, 2, 3), near, four))
+    twelve = along(part, (0, 12))
+
+    def held(k, up, down):
+        return jnp.where(z == 4, four[up - 4], jnp.where(z == 12, twelve[down - 10], cut[:, k]))
+
+    got = [
+        *near,
+        along(held(5, 6, 10), (0, 5), (4, 6)),
+        along(held(13, 7, 10), (0, 13), (4, 7)),
+        along(held(14, 9, 10), (0, 14), (4, 9), (12, 10)),
+        along(held(15, 8, 11), (0, 15), (4, 8), (12, 11)),
+        four[0],
+        twelve[2],
+    ]
 
     out0, panel, last = call(
-        route_kernel, (f32(NP, 9, 8, W), f32(14, 8, W), f32(2, 8, W)), 10, moved=2**20
+        route_kernel, (f32(NP, 9, 8, W), f32(14, 8, W), f32(2, 8, W)), 11, moved=2**20
     )(dest_rows, a[: 2 * W], cut[:, 0], *got)
     out0, maps = lax.optimization_barrier((out0, (dest_rows, row_mask, col_mask)))
     passed = lax.ppermute(panel, "core", [(0, 1)])

time: 118 us -> 119 us (level)
  starting transfers between devices: 42.9 us -> 35.1 us
  waiting for transfers between devices: 17 us -> 21.9 us
  blocking collectives: 42.4 us -> 44.8 us
  local copies, waits for them, and re-layouts: 0.96 us -> 2.81 us
    ppermute x1, waiting for transfers between devices: 0.41 us -> 19.8 us  [shards(): passed = lax.ppermute(panel, 'core', [(0, 1)])]
    ppermute x9, starting transfers between devices: 18 us -> 6.01 us  [along(): lax.ppermute(x, ('z', 'core'), [(2 * src, 2 * dst) for src, dst in pairs])]
    ppermute x9, waiting for transfers between devices: 8.89 us -> 0.02 us  [along(): lax.ppermute(x, ('z', 'core'), [(2 * src, 2 * dst) for src, dst in pairs])]
    all_to_all x1, waiting for transfers between devices: 5.64 us -> 0.01 us  [shards(): got0 = lax.all_to_all(out0, ('x', 'y'), 0, 0, tiled=True)]
    ppermute x1, starting transfers between devices: 13.1 us -> 16.5 us  [shards(): oth = lax.ppermute(own, 'core', [(0, 1), (1, 0)])]
    all_gather x1, blocking collectives: 25.4 us -> 27.7 us  [shards(): own = lax.all_gather(payload, 'z', axis=0, tiled=False)]
  transfers between devices with their start and end apart: 13 -> 13, of which waited for: 5 -> 2; matrix products, arithmetic and copies ran while one was open for 2% -> 1% of each run, Pallas kernels for 3% -> 3%
where the time goes in v6:
time: 119 us; the launch traced here: 118 us
  blocking collectives  44.8 us (38%)
  starting transfers between devices  35.1 us (29%)
  waiting for transfers between devices  21.9 us (18%)
  Pallas kernels  12.6 us (11%)
  local copies, waits for them, and re-layouts  2.81 us (2%)
    all_gather x1, blocking collectives, shards(): own = lax.all_gather(payload, 'z', axis=0, tiled=False)  27.7 us
    ppermute x1, waiting for transfers between devices, shards(): passed = lax.ppermute(panel, 'core', [(0, 1)])  19.8 us
    all_to_all x1, blocking collectives, shards(): got1 = lax.all_to_all(send, ('x', 'y'), 0, 0, tiled=True)  17.1 us
    ppermute x1, starting transfers between devices, shards(): oth = lax.ppermute(own, 'core', [(0, 1), (1, 0)])  16.5 us
    all_to_all x1, starting transfers between devices, shards(): got0 = lax.all_to_all(out0, ('x', 'y'), 0, 0, tiled=True)  7.58 us
    ppermute x9, starting transfers between devices, along(): lax.ppermute(x, ('z', 'core'), [(2 * src, 2 * dst) for src, dst in pairs])  6.01 us
    pallas_call x1, Pallas kernels, shards(): call(factor_kernel, (f32(SLOTS * W, 2 * W), f32(SLOTS * W, W), f32(NP, H...  5.17 us
    ppermute x1, starting transfers between devices, shards(): oth1 = lax.ppermute(got1[:, :H], 'core', [(0, 1), (1, 0)])  3.68 us
  transfers between devices with their start and end apart: 13, of which 2 were waited for; matrix products, arithmetic and copies ran while one was open for 1% of the time, Pallas kernels for 3%

profile of v6, /device:TPU:1, one launch (start us, length us, event | category | flops | bytes accessed | tf_op | source)
XLA Modules:
  0.0 118.3 jit_solution(6618961063369512673)
XLA Ops:
  0.6 0.0 copy-start
  0.6 1.1 copy_bitcast_fusion
  1.8 0.7 collective-permute-start.3
  2.5 1.0 slice_bitcast_fusion.7
  3.4 0.7 collective-permute-start.2
  4.1 0.7 collective-permute-start.1
  4.8 0.7 collective-permute-start
  5.4 0.0 copy-done
  5.5 0.0 collective-permute-done.2.refs_2_
  5.5 0.0 collective-permute-done.1.refs_1_
  5.5 0.0 collective-permute-done.refs_0_
  5.5 0.0 collective-permute-done.3
  5.6 0.7 collective-permute-start.4
  6.2 0.0 collective-permute-done.4
  6.3 0.7 collective-permute-start.8
  7.0 0.7 collective-permute-start.7
  7.7 0.7 collective-permute-start.6
  8.3 0.7 collective-permute-start.5
  9.0 0.0 copy-start.3
  9.0 0.0 collective-permute-done.8.refs_6_
  9.0 0.0 collective-permute-done.7.refs_5_
  9.1 0.0 collective-permute-done.6.refs_4_
  9.1 0.0 collective-permute-done.5.refs_3_
  9.1 0.6 copy-done.3
  9.7 1.5 %shard_map.68 = (f32[16,9,8,128]{3,2,1,0:T(8,128)}, f32[14,8,128]{2,1,0:T(8,128)S(1)}, f32[2,8,128]{2,1,0:T(8,128)S(1)}) custom-call(s32[2,128]{1,0:T(2,128)S(1)} %copy-done.3, f32[256,256]{1,0:T(8,128)S(1)} %slice.62.a, f32[8,8,256]{2,1,0:T(8,128)S(1)} %get-tuple-element.49.own, f32[8,8,256]{2,1,0:T(8,128)S(1)} %collective-permute-done.refs_0_, ...), custom_call_target="tpu_custom_call" | custom-call | bytes 1048576 | tf_op jit(solution)/shard_map/pallas_call | solution.py:250
  11.2 7.6 %all-to-all-start = ((f32[16,9,8,128]{3,2,1,0:T(8,128)}), f32[16,9,8,128]{3,2,1,0:T(8,128)S(1)}, u32[]{:S(2)}, u32[]{:S(2)}) async-start(f32[16,9,8,128]{3,2,1,0:T(8,128)} %get-tuple-element.33), calls=%async_computation | async-start | bytes 1179648 | tf_op jit(solution)/shard_map/all_to_all | solution.py:262
  18.8 1.3 %collective-permute-start.9 = (f32[14,8,128]{2,1,0:T(8,128)S(1)}, f32[14,8,128]{2,1,0:T(8,128)S(1)}, u32[]{:S(2)}, u32[]{:S(2)}) collective-permute-start(f32[14,8,128]{2,1,0:T(8,128)S(1)} %get-tuple-element.31), channel_id=1, source_target_pairs={{0,1},{2,3},{4,5},{6,7},{8,9},{10,11},{12,13},{14,15},{16,17},{18,... | collective-permute-start | bytes 172040 | tf_op jit(solution)/shard_map/ppermute | solution.py:254
  20.1 2.0 %shard_map.69.meta = s32[128]{0:T(128)} custom-call(s32[2,128]{1,0:T(2,128)} %dest.2, s32[2,128]{1,0:T(2,128)} %row_mask, s32[2,64]{1,0:T(2,128)} %col_mask), custom_call_target="tpu_custom_call" | custom-call | tf_op jit(solution)/shard_map/pallas_call | solution.py:255
  22.0 0.0 copy-start.1
  22.0 19.8 %collective-permute-done.9.passed = f32[14,8,128]{2,1,0:T(8,128)S(1)} collective-permute-done((f32[14,8,128]{2,1,0:T(8,128)S(1)}, f32[14,8,128]{2,1,0:T(8,128)S(1)}, u32[]{:S(2)}, u32[]{:S(2)}) %collective-permute-start.9) | collective-permute-done | bytes 57376 | tf_op jit(solution)/shard_map/ppermute | solution.py:254
  41.9 0.0 all-to-all-done.got
  41.9 0.0 copy-done.1
  41.9 0.6 shard_map.70
  42.4 27.7 %all-gather = f32[224,8,128]{2,1,0:T(8,128)S(1)} all-gather(f32[14,8,128]{2,1,0:T(8,128)S(1)} %get-tuple-element.34), channel_id=2, replica_groups=mesh['x'=4,'y'=4,'z'=16,'core'=2] {'z'}, dimensions={0}, use_global_device_ids=true | all-gather | bytes 974848 | tf_op jit(solution)/shard_map/all_gather | solution.py:267
  70.1 0.0 copy-start.2
  70.1 16.5 %collective-permute-start.10 = (f32[16,14,8,128]{3,2,1,0:T(8,128)S(1)}, f32[16,14,8,128]{3,2,1,0:T(8,128)S(1)}, u32[]{:S(2)}, u32[]{:S(2)}) collective-permute-start(f32[16,14,8,128]{3,2,1,0:T(8,128)S(1)} %bitcast.82), channel_id=1, source_target_pairs={{0,1},{1,0},{2,3},{3,2},{4,5},{5,4},{6,7},{7,6},{8,9},{9,8},{10,11... | collective-permute-start | bytes 2752520 | tf_op jit(solution)/shard_map/ppermute | solution.py:268
  86.7 2.1 %collective-permute-done.10.oth = f32[16,14,8,128]{3,2,1,0:T(8,128)S(1)} collective-permute-done((f32[16,14,8,128]{3,2,1,0:T(8,128)S(1)}, f32[16,14,8,128]{3,2,1,0:T(8,128)S(1)}, u32[]{:S(2)}, u32[]{:S(2)}) %collective-permute-start.10) | collective-permute-done | bytes 917536 | tf_op jit(solution)/shard_map/ppermute | solution.py:268
  88.8 0.0 copy-done.2
  88.8 5.2 %shard_map.71 = (f32[1024,256]{1,0:T(8,128)}, f32[1024,128]{1,0:T(8,128)S(1)}, f32[16,96,128]{2,1,0:T(8,128)S(1)}, f32[128,128]{1,0:T(8,128)S(1)}) custom-call(s32[128]{0:T(128)S(1)} %copy-done.1, f32[16,14,8,128]{3,2,1,0:T(8,128)S(1)} %bitcast.83, f32[16,14,8,128]{3,2,1,0:T(8,128)S(1)} %collective-permute-done.10.oth, ...), custom_call_target="tpu_custom_call" | custom-call | flops 500000000 | bytes 4194304 | tf_op jit(solution)/shard_map/pallas_call | solution.py:270
  93.9 17.1 %all_to_all.10.got.own = f32[16,96,128]{2,1,0:T(8,128)S(1)} all-to-all(f32[16,96,128]{2,1,0:T(8,128)S(1)} %get-tuple-element.36), channel_id=1, replica_groups=mesh['x'=4,'y'=4,'z'=16,'core'=2] {'x','y'}, dimensions={0} | all-to-all | bytes 1572864 | tf_op jit(solution)/shard_map/all_to_all | solution.py:278
  111.1 3.7 %collective-permute-start.11 = (f32[16,64,128]{2,1,0:T(8,128)S(1)}, f32[16,64,128]{2,1,0:T(8,128)S(1)}, u32[]{:S(2)}, u32[]{:S(2)}) collective-permute-start(f32[16,64,128]{2,1,0:T(8,128)S(1)} %slice.95), channel_id=1, source_target_pairs={{0,1},{1,0},{2,3},{3,2},{4,5},{5,4},{6,7},{7,6},{8,9},{9,8},{10,11... | collective-permute-start | bytes 1572872 | tf_op jit(solution)/shard_map/ppermute | solution.py:279
  114.8 1.5 %shard_map.72 = (f32[1024,256]{1,0:T(8,128)S(1)}, f32[128,256]{1,0:T(8,128)S(1)}) custom-call(s32[128]{0:T(128)S(1)} %copy-done.1, f32[1024,256]{1,0:T(8,128)S(1)} %copy-done, f32[16,96,128]{2,1,0:T(8,128)S(1)} %all_to_all.10.got.own, f32[1024,128]{1,0:T(8,128)S(1)} %get-tuple-element.37.plow, f32[128,128]{1,0:T(8,128)S(1)} %get-tuple-element.38.lsrc, ...), custom_call_target="tpu_custom_call" | custom-call | flops 500000000 | bytes 3145728 | tf_op jit(solution)/shard_map/pallas_call | solution.py:280
  116.3 0.0 collective-permute-done.11.oth
  116.3 2.0 %shard_map.73 = f32[1024,256]{1,0:T(8,128)} custom-call(s32[128]{0:T(128)S(1)} %copy-done.1, f32[1024,256]{1,0:T(8,128)S(1)} %get-tuple-element.39.cur, f32[16,96,128]{2,1,0:T(8,128)S(1)} %all_to_all.10.got.own, f32[16,64,128]{2,1,0:T(8,128)S(1)} %collective-permute-done.11.oth, f32[128,256]{1,0:T(8,128)S(1)} %get-tuple-element.40.kept), custom_call_target="tpu_custom_call" | custom-call | flops 500000000 | bytes 3145728 | tf_op jit(solution)/shard_map/pallas_call | solution.py:283
  (6 shorter events, 0.1 us)
Async XLA Ops:
  0.6 4.8 %copy-start = (f32[1024,256]{1,0:T(8,128)S(1)}, f32[1024,256]{1,0:T(8,128)}, u32[]{:S(2)}) copy-start(f32[1024,256]{1,0:T(8,128)} %a.1) | copy-start | bytes 3145732
  1.8 3.8 %collective-permute-start.3 = (f32[6,8,8,256]{3,2,1,0:T(8,128)S(1)}, f32[6,8,8,256]{3,2,1,0:T(8,128)S(1)}, u32[]{:S(2)}, u32[]{:S(2)}) collective-permute-start(f32[6,8,8,256]{3,2,1,0:T(8,128)S(1)} %copy_bitcast_fusion), channel_id=1, source_target_pairs={{0,8},{32,40},{64,72},{96,104},{128,136},{160,168},{192,200},{224,... | collective-permute-start | bytes 1179656 | tf_op jit(solution)/shard_map/ppermute | solution.py:230
  3.4 2.1 %collective-permute-start.2 = (f32[8,8,256]{2,1,0:T(8,128)S(1)}, f32[8,8,256]{2,1,0:T(8,128)S(1)}, u32[]{:S(2)}, u32[]{:S(2)}) collective-permute-start(f32[8,8,256]{2,1,0:T(8,128)S(1)} %get-tuple-element.46), channel_id=1, source_target_pairs={{0,2},{32,34},{64,66},{96,98},{128,130},{160,162},{192,194},{224,2... | collective-permute-start | bytes 196616 | tf_op jit(solution)/shard_map/ppermute | solution.py:230
  4.1 1.4 %collective-permute-start.1 = (f32[8,8,256]{2,1,0:T(8,128)S(1)}, f32[8,8,256]{2,1,0:T(8,128)S(1)}, u32[]{:S(2)}, u32[]{:S(2)}) collective-permute-start(f32[8,8,256]{2,1,0:T(8,128)S(1)} %get-tuple-element.47), channel_id=1, source_target_pairs={{0,4},{32,36},{64,68},{96,100},{128,132},{160,164},{192,196},{224,... | collective-permute-start | bytes 196616 | tf_op jit(solution)/shard_map/ppermute | solution.py:230
  4.8 0.8 collective-permute-start
  5.6 0.7 collective-permute-start.4
  6.3 2.7 %collective-permute-start.8 = (f32[8,8,256]{2,1,0:T(8,128)S(1)}, f32[8,8,256]{2,1,0:T(8,128)S(1)}, u32[]{:S(2)}, u32[]{:S(2)}) collective-permute-start(f32[8,8,256]{2,1,0:T(8,128)S(1)} %get-tuple-element.42), channel_id=1, source_target_pairs={{0,30},{8,16},{24,22},{32,62},{40,48},{56,54},{64,94},{72,80},{88,... | collective-permute-start | bytes 196616 | tf_op jit(solution)/shard_map/ppermute | solution.py:230
  7.0 2.1 %collective-permute-start.7 = (f32[8,8,256]{2,1,0:T(8,128)S(1)}, f32[8,8,256]{2,1,0:T(8,128)S(1)}, u32[]{:S(2)}, u32[]{:S(2)}) collective-permute-start(f32[8,8,256]{2,1,0:T(8,128)S(1)} %get-tuple-element.43), channel_id=1, source_target_pairs={{0,28},{8,18},{24,20},{32,60},{40,50},{56,52},{64,92},{72,82},{88,... | collective-permute-start | bytes 196616 | tf_op jit(solution)/shard_map/ppermute | solution.py:230
  7.7 1.4 %collective-permute-start.6 = (f32[8,8,256]{2,1,0:T(8,128)S(1)}, f32[8,8,256]{2,1,0:T(8,128)S(1)}, u32[]{:S(2)}, u32[]{:S(2)}) collective-permute-start(f32[8,8,256]{2,1,0:T(8,128)S(1)} %get-tuple-element.44), channel_id=1, source_target_pairs={{0,26},{8,14},{32,58},{40,46},{64,90},{72,78},{96,122},{104,110},{... | collective-permute-start | bytes 196616 | tf_op jit(solution)/shard_map/ppermute | solution.py:230
  8.3 0.7 collective-permute-start.5
  9.0 0.7 copy-start.3
  11.2 30.7 %all-to-all-start = ((f32[16,9,8,128]{3,2,1,0:T(8,128)}), f32[16,9,8,128]{3,2,1,0:T(8,128)S(1)}, u32[]{:S(2)}, u32[]{:S(2)}) async-start(f32[16,9,8,128]{3,2,1,0:T(8,128)} %get-tuple-element.33), calls=%async_computation | async-start | bytes 1179648 | tf_op jit(solution)/shard_map/all_to_all | solution.py:262
  18.8 23.1 %collective-permute-start.9 = (f32[14,8,128]{2,1,0:T(8,128)S(1)}, f32[14,8,128]{2,1,0:T(8,128)S(1)}, u32[]{:S(2)}, u32[]{:S(2)}) collective-permute-start(f32[14,8,128]{2,1,0:T(8,128)S(1)} %get-tuple-element.31), channel_id=1, source_target_pairs={{0,1},{2,3},{4,5},{6,7},{8,9},{10,11},{12,13},{14,15},{16,17},{18,... | collective-permute-start | bytes 172040 | tf_op jit(solution)/shard_map/ppermute | solution.py:254
  22.0 19.8 %copy-start.1 = (s32[128]{0:T(128)S(1)}, s32[128]{0:T(128)}, u32[]{:S(2)}) copy-start(s32[128]{0:T(128)} %shard_map.69.meta) | copy-start | bytes 1540
  70.1 18.6 %copy-start.2 = (s32[2,128]{1,0:T(2,128)S(1)}, s32[2,128]{1,0:T(2,128)}, u32[]{:S(2)}) copy-start(s32[2,128]{1,0:T(2,128)} %perms.1) | copy-start | bytes 3076
  70.1 18.6 %collective-permute-start.10 = (f32[16,14,8,128]{3,2,1,0:T(8,128)S(1)}, f32[16,14,8,128]{3,2,1,0:T(8,128)S(1)}, u32[]{:S(2)}, u32[]{:S(2)}) collective-permute-start(f32[16,14,8,128]{3,2,1,0:T(8,128)S(1)} %bitcast.82), channel_id=1, source_target_pairs={{0,1},{1,0},{2,3},{3,2},{4,5},{5,4},{6,7},{7,6},{8,9},{9,8},{10,11... | collective-permute-start | bytes 2752520 | tf_op jit(solution)/shard_map/ppermute | solution.py:268
  111.1 5.2 %collective-permute-start.11 = (f32[16,64,128]{2,1,0:T(8,128)S(1)}, f32[16,64,128]{2,1,0:T(8,128)S(1)}, u32[]{:S(2)}, u32[]{:S(2)}) collective-permute-start(f32[16,64,128]{2,1,0:T(8,128)S(1)} %slice.95), channel_id=1, source_target_pairs={{0,1},{1,0},{2,3},{3,2},{4,5},{5,4},{6,7},{7,6},{8,9},{9,8},{10,11... | collective-permute-start | bytes 1572872 | tf_op jit(solution)/shard_map/ppermute | solution.py:279

commit v7 on v5

--- a/solution.py
+++ b/solution.py
@@ -12,7 +12,6 @@
 NP = 16
 NZ = 16
 SLOTS = 8
-SENDS = ((8, 9), (7, 10), (6, 11), (5, 12), (4, 13), (3, 14), (2, 15), (1, 0))
 
 
 def dot16(a, b):
@@ -32,12 +31,26 @@
     return both[:, :n] + both[:, n:]
 
 
-def reorder(perms, k, x):
+def exact(x):
+    high, mid = split(x)
+    return high, mid, (x - high.astype(jnp.float32) - mid.astype(jnp.float32)).astype(jnp.bfloat16)
+
+
+def order(perms, k):
     hit = lax.broadcasted_iota(jnp.int32, (W, W), 0) == perms[k : k + 1, :]
-    order = jnp.where(hit, 1.0, 0.0).astype(jnp.float32).T.astype(jnp.bfloat16)
-    high, mid = split(x)
-    low = (x - high.astype(jnp.float32) - mid.astype(jnp.float32)).astype(jnp.bfloat16)
-    return dot16(order, high) + (dot16(order, mid) + dot16(order, low))
+    return jnp.where(hit, 1.0, 0.0).astype(jnp.float32)
+
+
+def reorder_rows(perms, k, x):
+    move = order(perms, k).T.astype(jnp.bfloat16)
+    high, mid, low = exact(x)
+    return dot16(move, high) + (dot16(move, mid) + dot16(move, low))
+
+
+def reorder_columns(perms, k, x):
+    move = order(perms, k).astype(jnp.bfloat16)
+    high, mid, low = exact(x)
+    return dot16(high, move) + (dot16(mid, move) + dot16(low, move))
 
 
 def index_kernel(dest, row_mask, col_mask, meta, src):
@@ -85,7 +98,6 @@
     share = own[...] * root.astype(jnp.float32)
     for ref in got:
         share = share + ref[...]
-    out[...] = jnp.zeros_like(out)
     for slot in range(SLOTS):
         left, right = share[slot, :, :W], share[slot, :, W:]
         out[lax.shift_right_logical(dest[0, me * SLOTS + slot], 3), 0] = left
@@ -120,55 +132,73 @@
         out[13] = got[0, 4]
 
 
-def refine(pivot):
+def refine(block):
     row = lax.broadcasted_iota(jnp.int32, (W, W), 0)
     col = lax.broadcasted_iota(jnp.int32, (W, W), 1)
-    two = jnp.where(row == col, 2.0, 0.0).astype(jnp.float32)
-    scale = W * (jnp.mean(pivot * pivot) + 1e-6)
-    approx = pivot.T / scale
-    for _ in range(SWEEPS):
-        approx = dot(approx, two - dot(pivot, approx))
+    one = jnp.where(row == col, 1.0, 0.0).astype(jnp.float32)
+    scale = W * (jnp.mean(block * block) + 1e-6)
+    approx = block.T / scale
+    rest = one - dot(block, approx)
+    for sweep in range(SWEEPS):
+        approx = approx + dot(approx, rest)
+        if sweep + 1 < SWEEPS:
+            rest = dot(rest, rest)
     return approx
 
 
-def factor(meta, head, panel, chunk, perms, lpan, plow, send, lsrc):
-    def tile(ref, t):
-        return ref[:, t].reshape(W, W)
-
-    def flag(i):
-        return meta[i].astype(jnp.float32)
-
-    def flagged(block, base):
-        return jnp.concatenate(
-            [block[s * W : (s + 1) * W] * flag(base + s) for s in range(SLOTS)], axis=0
-        )
-
-    inv0 = refine(reorder(perms, 0, tile(head, 10)))
-    kept01 = reorder(perms, 0, tile(head, 11)) * flag(2)
-    low_src = dot(tile(head, 12), inv0) * flag(3)
+def tile(ref, t):
+    return ref[:, t].reshape(W, W)
+
+
+def flagged(meta, block, base):
+    return jnp.concatenate(
+        [block[s * W : (s + 1) * W] * meta[base + s].astype(jnp.float32) for s in range(SLOTS)], axis=0
+    )
+
+
+def factor(meta, head, panel, send, plow, low1, inv0, lsrc):
+    inv = refine(tile(head, 10))
+    inv0[...] = inv
+    kept01 = tile(head, 11) * meta[2].astype(jnp.float32)
+    low_src = dot(tile(head, 12), inv) * meta[3].astype(jnp.float32)
     lsrc[...] = low_src
-    inv1 = refine(reorder(perms, 1, tile(head, 13) - dot(low_src, kept01)))
-    col0 = jnp.concatenate([tile(panel, s) for s in range(7)] + [tile(head, 0)], axis=0)
-    lpan[:, :W] = flagged(dot(col0, inv0), 8)
+    inv1 = refine(tile(head, 13) - dot(low_src, kept01))
     ext0 = jnp.concatenate([tile(head, 2 + s) for s in range(SLOTS)], axis=0)
-    ext0 = flagged(dot(ext0, inv0), 24)
+    ext0 = flagged(meta, dot(ext0, inv), 24)
     plow[...] = ext0
     col1 = jnp.concatenate([tile(panel, 7 + s) for s in range(7)] + [tile(head, 1)], axis=0)
-    lpan[:, W:] = flagged(dot(col1 - dot(ext0, kept01), inv1), 16)
+    low1[...] = flagged(meta, dot(col1 - dot(ext0, kept01), inv1), 16)
     for slot in range(SLOTS):
         half = pl.ds(pl.multiple_of(slot * W + meta[0] * H, H), H)
-        send[meta[32 + slot], :H] = lpan[half, W:]
+        send[meta[32 + slot], :H] = low1[half, :]
+
+
+def factor_kernel(meta, own, oth, chunk, send, *refs):
+    @pl.when(meta[0] == 0)
+    def _():
+        factor(meta, own, oth, send, *refs)
+
+    @pl.when(meta[0] == 1)
+    def _():
+        factor(meta, oth, own, send, *refs)
+
     send[:, H:] = jnp.broadcast_to(chunk[...].reshape(1, 32, W), (NP, 32, W))
 
 
-def factor_kernel(meta, own, oth, *refs):
+def panels_kernel(meta, own, oth, low1, inv0, perms, lpan):
+    def write(head, panel):
+        col0 = jnp.concatenate([tile(panel, s) for s in range(7)] + [tile(head, 0)], axis=0)
+        lpan[:, :W] = flagged(meta, dot(col0, reorder_columns(perms, 0, inv0[...])), 8)
+
     @pl.when(meta[0] == 0)
     def _():
-        factor(meta, own, oth, *refs)
+        write(own, oth)
 
     @pl.when(meta[0] == 1)
     def _():
-        factor(meta, oth, own, *refs)
+        write(oth, own)
+
+    lpan[:, W:] = reorder_columns(perms, 1, low1[...])
 
 
 def first_kernel(meta, a, got, plow, lsrc, perms, cur, kept):
@@ -181,17 +211,16 @@
     rows = jnp.concatenate(
         [got[:, H : H + 16].reshape(2 * W, W), got[:, H + 16 :].reshape(2 * W, W)], axis=1
     )
-    up0 = reorder(perms, 0, rows[:W])
-    kept0 = masked(up0, 0)
-    up1 = reorder(perms, 1, rows[W:] - dot(lsrc[...], kept0))
-    kept[...] = masked(up1, 1)
+    kept0 = masked(rows[:W], 0)
+    next1 = rows[W:] - dot(lsrc[...], kept0)
+    kept[...] = masked(next1, 1)
     prod = dot(plow[...], kept0)
     cur[...] = a[...] - prod
 
     @pl.when(meta[1] == 1)
     def _():
-        cur[:W] = up0 - prod[:W]
-        cur[W : 2 * W] = up1
+        cur[:W] = reorder_rows(perms, 0, rows[:W]) - prod[:W]
+        cur[W : 2 * W] = reorder_rows(perms, 1, next1)
 
 
 def second_kernel(meta, cur, own, oth, kept, out, low):
@@ -225,19 +254,20 @@
 def shards(a, row_perms, dest_rows, row_mask, col_mask):
     core = lax.axis_index("core")
     smem = pl.BlockSpec(memory_space=pltpu.SMEM)
-    over = lax.ppermute(a, ("z", "core"), [(0, 1)]).reshape(SLOTS, NZ, 8, 2 * W)
     cut = a.reshape(SLOTS, NZ, 8, 2 * W)
+    over = lax.ppermute(cut[:, 8:].transpose(1, 0, 2, 3), ("z", "core"), [(0, 1)])
+    pieces = [jnp.where(core == 0, cut[:, step % 8], over[8 - step]) for step in range(1, 9)]
+    pieces = lax.optimization_barrier(pieces)
     got = []
-    for z0, z1 in reversed(SENDS):
-        pairs, piece = [(0, 2 * z0)], cut[:, z0]
-        if z1:
-            pairs.append((1, 2 * z1))
-            piece = jnp.where(core == 0, piece, over[:, z1])
-        got.append(lax.ppermute(piece, ("z", "core"), pairs))
+    for step in range(1, 9):
+        pairs = [(1, 2 * (NZ - step))]
+        if step < 8:
+            pairs.append((0, 2 * step))
+        got.append(lax.ppermute(pieces[step - 1], ("z", "core"), pairs))
 
     out0, panel, last = call(
         route_kernel, (f32(NP, 9, 8, W), f32(14, 8, W), f32(2, 8, W)), 10, moved=2**20
-    )(dest_rows, a[: 2 * W], cut[:, 0], *got)
+    )(dest_rows, a[: 2 * W], pieces[7], *got)
     out0, maps = lax.optimization_barrier((out0, (dest_rows, row_mask, col_mask)))
     passed = lax.ppermute(panel, "core", [(0, 1)])
     meta = pl.pallas_call(
@@ -255,15 +285,19 @@
     own = lax.all_gather(payload, "z", axis=0, tiled=False)
     oth = lax.ppermute(own, "core", [(0, 1), (1, 0)])
 
-    lpan, plow, send, lsrc = call(
+    send, plow, low1, inv0, lsrc = call(
         factor_kernel,
-        (f32(SLOTS * W, 2 * W), f32(SLOTS * W, W), f32(NP, H + 32, W), f32(W, W)),
-        4,
+        (f32(NP, H + 32, W), f32(SLOTS * W, W), f32(SLOTS * W, W), f32(W, W), f32(W, W)),
+        3,
         flops=5 * 10**8,
         moved=4 * 2**20,
-    )(meta, own, oth, chunk, row_perms)
+    )(meta, own, oth, chunk)
 
     got1 = lax.all_to_all(send, ("x", "y"), 0, 0, tiled=True)
+    lpan = call(panels_kernel, f32(SLOTS * W, 2 * W), 5, flops=5 * 10**8, moved=4 * 2**20)(
+        meta, own, oth, low1, inv0, row_perms
+    )
+    got1, lpan = lax.optimization_barrier((got1, lpan))
     oth1 = lax.ppermute(got1[:, :H], "core", [(0, 1), (1, 0)])
     cur, kept = call(
         first_kernel, (f32(SLOTS * W, 2 * W), f32(W, 2 * W)), 5, flops=5 * 10**8, moved=3 * 2**20

time: 118 us -> 114 us (0.966)
  blocking collectives: 42.4 us -> 25.3 us
  waiting for transfers between devices: 17 us -> 26.2 us
  local copies, waits for them, and re-layouts: 0.96 us -> 4.95 us
  starting transfers between devices: 42.9 us -> 41.6 us
    all_to_all x1 -> x0, blocking collectives: 17 us -> none  [shards(): got1 = lax.all_to_all(send, ('x', 'y'), 0, 0, tiled=True)]
    all_to_all x0 -> x1, waiting for transfers between devices: none -> 7.42 us  [shards(): got1 = lax.all_to_all(send, ('x', 'y'), 0, 0, tiled=True)]
    all_to_all x0 -> x1, starting transfers between devices: none -> 3.71 us  [shards(): got1 = lax.all_to_all(send, ('x', 'y'), 0, 0, tiled=True)]
    unnamed x8 -> x16, local copies, waits for them, and re-layouts: 0.02 us -> 3.72 us
    ppermute x9, starting transfers between devices: 18 us -> 14.5 us  [the longest x8 13.2 us: shards(): got.append(lax.ppermute(pieces[step - 1], ('z', 'core'), pairs))]
    ppermute x1, starting transfers between devices: 13.1 us -> 10.7 us  [shards(): oth = lax.ppermute(own, 'core', [(0, 1), (1, 0)])]
    all_to_all x1, waiting for transfers between devices: 5.64 us -> 7.07 us  [shards(): got0 = lax.all_to_all(out0, ('x', 'y'), 0, 0, tiled=True)]
    pallas_call x1 -> x2, Pallas kernels: 5.16 us -> 6.44 us  [the longest x1 4.03 us: shards(): call(factor_kernel, (f32(NP, H + 32, W), f32(SLOTS * W, W), f32(SLOTS * W...]
  transfers between devices with their start and end apart: 13 -> 14, of which waited for: 5 -> 6; matrix products, arithmetic and copies ran while one was open for 2% -> 0% of each run, Pallas kernels for 3% -> 5%
where the time goes in v7:
time: 114 us; the launch traced here: 113 us
  starting transfers between devices  41.6 us (36%)
  waiting for transfers between devices  26.2 us (23%)
  blocking collectives  25.3 us (22%)
  Pallas kernels  13.7 us (12%)
  local copies, waits for them, and re-layouts  4.95 us (4%)
    all_gather x1, blocking collectives, shards(): own = lax.all_gather(payload, 'z', axis=0, tiled=False)  25.3 us
    ppermute x8, starting transfers between devices, shards(): got.append(lax.ppermute(pieces[step - 1], ('z', 'core'), pairs))  13.2 us
    ppermute x1, starting transfers between devices, shards(): oth = lax.ppermute(own, 'core', [(0, 1), (1, 0)])  10.7 us
    ppermute x1, waiting for transfers between devices, shards(): lax.ppermute(cut[:, 8:].transpose(1, 0, 2, 3), ('z', 'core'), [(0, 1)])  8.25 us
    all_to_all x1, waiting for transfers between devices, shards(): got1 = lax.all_to_all(send, ('x', 'y'), 0, 0, tiled=True)  7.42 us
    all_to_all x1, waiting for transfers between devices, shards(): got0 = lax.all_to_all(out0, ('x', 'y'), 0, 0, tiled=True)  7.07 us
    all_to_all x1, starting transfers between devices, shards(): got0 = lax.all_to_all(out0, ('x', 'y'), 0, 0, tiled=True)  6.75 us
    ppermute x1, starting transfers between devices, shards(): oth1 = lax.ppermute(got1[:, :H], 'core', [(0, 1), (1, 0)])  4.69 us
  transfers between devices with their start and end apart: 14, of which 6 were waited for; matrix products, arithmetic and copies ran while one was open for 0% of the time, Pallas kernels for 5%

profile of v7, /device:TPU:1, one launch (start us, length us, event | category | flops | bytes accessed | tf_op | source)
XLA Modules:
  0.0 112.8 jit_solution(14576678087679188147)
XLA Ops:
  0.6 0.0 copy-start
  0.6 1.2 %copy_bitcast_fusion = f32[8,8,8,256]{3,2,1,0:T(8,128)S(1)} fusion(f32[8,16,8,256]{3,2,1,0:T(8,128)} %bitcast.87), kind=kLoop, calls=%fused_computation | loop fusion | bytes 1048576 | tf_op jit(solution)/shard_map/transpose | solution.py:258
  1.8 1.3 %collective-permute-start = (f32[8,8,8,256]{3,2,1,0:T(8,128)S(1)}, f32[8,8,8,256]{3,2,1,0:T(8,128)S(1)}, u32[]{:S(2)}, u32[]{:S(2)}) collective-permute-start(f32[8,8,8,256]{3,2,1,0:T(8,128)S(1)} %copy_bitcast_fusion), channel_id=1, source_target_pairs={{0,1},{32,33},{64,65},{96,97},{128,129},{160,161},{192,193},{224,2... | collective-permute-start | bytes 1572872 | tf_op jit(solution)/shard_map/ppermute | solution.py:258
  3.1 8.3 %collective-permute-done = f32[8,8,8,256]{3,2,1,0:T(8,128)S(1)} collective-permute-done((f32[8,8,8,256]{3,2,1,0:T(8,128)S(1)}, f32[8,8,8,256]{3,2,1,0:T(8,128)S(1)}, u32[]{:S(2)}, u32[]{:S(2)}) %collective-permute-start) | collective-permute-done | bytes 524320 | tf_op jit(solution)/shard_map/ppermute | solution.py:258
  11.4 0.0 copy-done
  11.4 0.1 fusion
  11.5 0.0 copy-start.7
  11.5 3.7 %collective-permute-start.1 = (f32[8,8,256]{2,1,0:T(8,128)S(1)}, f32[8,8,256]{2,1,0:T(8,128)S(1)}, u32[]{:S(2)}, u32[]{:S(2)}) collective-permute-start(f32[8,8,256]{2,1,0:T(8,128)S(1)} %get-tuple-element.29), channel_id=1, source_target_pairs={{1,30},{0,2},{33,62},{32,34},{65,94},{64,66},{97,126},{96,98},{129... | collective-permute-start | bytes 196616 | tf_op jit(solution)/shard_map/ppermute | solution.py:266
  15.2 1.3 %collective-permute-start.2 = (f32[8,8,256]{2,1,0:T(8,128)S(1)}, f32[8,8,256]{2,1,0:T(8,128)S(1)}, u32[]{:S(2)}, u32[]{:S(2)}) collective-permute-start(f32[8,8,256]{2,1,0:T(8,128)S(1)} %get-tuple-element.30), channel_id=1, source_target_pairs={{1,28},{0,4},{33,60},{32,36},{65,92},{64,68},{97,124},{96,100},{12... | collective-permute-start | bytes 196616 | tf_op jit(solution)/shard_map/ppermute | solution.py:266
  16.5 1.3 %collective-permute-start.3 = (f32[8,8,256]{2,1,0:T(8,128)S(1)}, f32[8,8,256]{2,1,0:T(8,128)S(1)}, u32[]{:S(2)}, u32[]{:S(2)}) collective-permute-start(f32[8,8,256]{2,1,0:T(8,128)S(1)} %get-tuple-element.31), channel_id=1, source_target_pairs={{1,26},{0,6},{33,58},{32,38},{65,90},{64,70},{97,122},{96,102},{12... | collective-permute-start | bytes 196616 | tf_op jit(solution)/shard_map/ppermute | solution.py:266
  17.8 1.3 %collective-permute-start.4 = (f32[8,8,256]{2,1,0:T(8,128)S(1)}, f32[8,8,256]{2,1,0:T(8,128)S(1)}, u32[]{:S(2)}, u32[]{:S(2)}) collective-permute-start(f32[8,8,256]{2,1,0:T(8,128)S(1)} %get-tuple-element.32), channel_id=1, source_target_pairs={{1,24},{0,8},{33,56},{32,40},{65,88},{64,72},{97,120},{96,104},{12... | collective-permute-start | bytes 196616 | tf_op jit(solution)/shard_map/ppermute | solution.py:266
  19.1 1.8 %collective-permute-start.5 = (f32[8,8,256]{2,1,0:T(8,128)S(1)}, f32[8,8,256]{2,1,0:T(8,128)S(1)}, u32[]{:S(2)}, u32[]{:S(2)}) collective-permute-start(f32[8,8,256]{2,1,0:T(8,128)S(1)} %get-tuple-element.33), channel_id=1, source_target_pairs={{1,22},{0,10},{33,54},{32,42},{65,86},{64,74},{97,118},{96,106},{1... | collective-permute-start | bytes 196616 | tf_op jit(solution)/shard_map/ppermute | solution.py:266
  20.8 0.0 collective-permute-done.1.refs_0_
  20.8 1.3 %collective-permute-start.6 = (f32[8,8,256]{2,1,0:T(8,128)S(1)}, f32[8,8,256]{2,1,0:T(8,128)S(1)}, u32[]{:S(2)}, u32[]{:S(2)}) collective-permute-start(f32[8,8,256]{2,1,0:T(8,128)S(1)} %get-tuple-element.34), channel_id=1, source_target_pairs={{1,20},{0,12},{33,52},{32,44},{65,84},{64,76},{97,116},{96,108},{1... | collective-permute-start | bytes 196616 | tf_op jit(solution)/shard_map/ppermute | solution.py:266
  22.1 0.0 collective-permute-done.2.refs_1_
  22.2 1.3 %collective-permute-start.7 = (f32[8,8,256]{2,1,0:T(8,128)S(1)}, f32[8,8,256]{2,1,0:T(8,128)S(1)}, u32[]{:S(2)}, u32[]{:S(2)}) collective-permute-start(f32[8,8,256]{2,1,0:T(8,128)S(1)} %get-tuple-element.35), channel_id=1, source_target_pairs={{1,18},{0,14},{33,50},{32,46},{65,82},{64,78},{97,114},{96,110},{1... | collective-permute-start | bytes 196616 | tf_op jit(solution)/shard_map/ppermute | solution.py:266
  23.5 0.0 collective-permute-done.3.refs_2_
  23.5 1.3 %collective-permute-start.8 = (f32[8,8,256]{2,1,0:T(8,128)S(1)}, f32[8,8,256]{2,1,0:T(8,128)S(1)}, u32[]{:S(2)}, u32[]{:S(2)}) collective-permute-start(f32[8,8,256]{2,1,0:T(8,128)S(1)} %get-tuple-element.28.own), channel_id=1, source_target_pairs={{1,16},{33,48},{65,80},{97,112},{129,144},{161,176},{193,208},{225... | collective-permute-start | bytes 196616 | tf_op jit(solution)/shard_map/ppermute | solution.py:266
  24.8 0.0 collective-permute-done.4.refs_3_
  24.8 0.0 collective-permute-done.5.refs_4_
  24.8 0.0 collective-permute-done.6.refs_5_
  24.8 0.0 collective-permute-done.7.refs_6_
  24.8 1.2 %collective-permute-done.8.refs_7_ = f32[8,8,256]{2,1,0:T(8,128)S(1)} collective-permute-done((f32[8,8,256]{2,1,0:T(8,128)S(1)}, f32[8,8,256]{2,1,0:T(8,128)S(1)}, u32[]{:S(2)}, u32[]{:S(2)}) %collective-permute-start.8) | collective-permute-done | bytes 65568 | tf_op jit(solution)/shard_map/ppermute | solution.py:266
  26.1 0.0 copy-done.7
  26.1 1.4 %shard_map.68 = (f32[16,9,8,128]{3,2,1,0:T(8,128)}, f32[14,8,128]{2,1,0:T(8,128)S(1)}, f32[2,8,128]{2,1,0:T(8,128)S(1)}) custom-call(s32[2,128]{1,0:T(2,128)S(1)} %copy-done.7, f32[256,256]{1,0:T(8,128)S(1)} %slice.57.a, f32[8,8,256]{2,1,0:T(8,128)S(1)} %get-tuple-element.28.own, f32[8,8,256]{2,1,0:T(8,128)S(1)} %collective-permute-done.1.refs_0_, ...), custom_call_target="tpu_custom_call" | custom-call | bytes 1048576 | tf_op jit(solution)/shard_map/pallas_call | solution.py:268
  27.5 6.8 %all-to-all-start = ((f32[16,9,8,128]{3,2,1,0:T(8,128)}), f32[16,9,8,128]{3,2,1,0:T(8,128)S(1)}, u32[]{:S(2)}, u32[]{:S(2)}) async-start(f32[16,9,8,128]{3,2,1,0:T(8,128)} %get-tuple-element.42), calls=%async_computation | async-start | bytes 1179648 | tf_op jit(solution)/shard_map/all_to_all | solution.py:280
  34.3 1.3 %collective-permute-start.9 = (f32[14,8,128]{2,1,0:T(8,128)S(1)}, f32[14,8,128]{2,1,0:T(8,128)S(1)}, u32[]{:S(2)}, u32[]{:S(2)}) collective-permute-start(f32[14,8,128]{2,1,0:T(8,128)S(1)} %get-tuple-element.40), channel_id=1, source_target_pairs={{0,1},{2,3},{4,5},{6,7},{8,9},{10,11},{12,13},{14,15},{16,17},{18,... | collective-permute-start | bytes 172040 | tf_op jit(solution)/shard_map/ppermute | solution.py:272
  35.6 2.0 %shard_map.69.meta = s32[128]{0:T(128)} custom-call(s32[2,128]{1,0:T(2,128)} %dest.2, s32[2,128]{1,0:T(2,128)} %row_mask, s32[2,64]{1,0:T(2,128)} %col_mask), custom_call_target="tpu_custom_call" | custom-call | tf_op jit(solution)/shard_map/pallas_call | solution.py:273
  37.6 0.0 copy-start.5
  37.6 0.0 collective-permute-done.9.passed
  37.6 7.1 %all-to-all-done.got = f32[16,9,8,128]{3,2,1,0:T(8,128)S(1)} async-done(((f32[16,9,8,128]{3,2,1,0:T(8,128)}), f32[16,9,8,128]{3,2,1,0:T(8,128)S(1)}, u32[]{:S(2)}, u32[]{:S(2)}) %all-to-all-start) | async-done | bytes 589856 | tf_op jit(solution)/shard_map/all_to_all | solution.py:280
  44.7 0.6 shard_map.70
  45.2 25.3 %all-gather = f32[224,8,128]{2,1,0:T(8,128)S(1)} all-gather(f32[14,8,128]{2,1,0:T(8,128)S(1)} %get-tuple-element.43), channel_id=2, replica_groups=mesh['x'=4,'y'=4,'z'=16,'core'=2] {'z'}, dimensions={0}, use_global_device_ids=true | all-gather | bytes 974848 | tf_op jit(solution)/shard_map/all_gather | solution.py:285
  70.6 10.7 %collective-permute-start.10 = (f32[16,14,8,128]{3,2,1,0:T(8,128)S(1)}, f32[16,14,8,128]{3,2,1,0:T(8,128)S(1)}, u32[]{:S(2)}, u32[]{:S(2)}) collective-permute-start(f32[16,14,8,128]{3,2,1,0:T(8,128)S(1)} %bitcast.84), channel_id=1, source_target_pairs={{0,1},{1,0},{2,3},{3,2},{4,5},{5,4},{6,7},{7,6},{8,9},{9,8},{10,11... | collective-permute-start | bytes 2752520 | tf_op jit(solution)/shard_map/ppermute | solution.py:286
  81.2 2.1 %collective-permute-done.10.oth = f32[16,14,8,128]{3,2,1,0:T(8,128)S(1)} collective-permute-done((f32[16,14,8,128]{3,2,1,0:T(8,128)S(1)}, f32[16,14,8,128]{3,2,1,0:T(8,128)S(1)}, u32[]{:S(2)}, u32[]{:S(2)}) %collective-permute-start.10) | collective-permute-done | bytes 917536 | tf_op jit(solution)/shard_map/ppermute | solution.py:286
  83.3 4.0 %shard_map.71 = (f32[16,96,128]{2,1,0:T(8,128)}, f32[1024,128]{1,0:T(8,128)S(1)}, f32[1024,128]{1,0:T(8,128)S(1)}, f32[128,128]{1,0:T(8,128)S(1)}, f32[128,128]{1,0:T(8,128)S(1)}) custom-call(s32[128]{0:T(128)S(1)} %copy-done.5, f32[16,14,8,128]{3,2,1,0:T(8,128)S(1)} %bitcast.85, f32[16,14,8,128]{3,2,1,0:T(8,128)S(1)} %collective-permute-done.10.oth, ...), custom_call_target="tpu_custom_call" | custom-call | flops 500000000 | bytes 4194304 | tf_op jit(solution)/shard_map/pallas_call | solution.py:288
  87.3 0.8 copy-done.3
  88.2 3.7 %all-to-all-start.1 = ((f32[16,96,128]{2,1,0:T(8,128)}), f32[16,96,128]{2,1,0:T(8,128)S(1)}, u32[]{:S(2)}, u32[]{:S(2)}) async-start(f32[16,96,128]{2,1,0:T(8,128)} %get-tuple-element.45), calls=%async_computation.1 | async-start | bytes 1572864 | tf_op jit(solution)/shard_map/all_to_all | solution.py:296
  91.9 0.0 copy-start.6
  91.9 0.7 copy-done.6
  92.6 1.2 %copy-done.2 = f32[16,14,8,128]{3,2,1,0:T(8,128)S(1)} copy-done((f32[16,14,8,128]{3,2,1,0:T(8,128)S(1)}, f32[16,14,8,128]{3,2,1,0:T(8,128)}, u32[]{:S(2)}) %copy-start.2) | copy-done | bytes 917528
  93.7 1.0 copy-done.4
  94.8 2.4 %shard_map.72 = f32[1024,256]{1,0:T(8,128)} custom-call(s32[128]{0:T(128)S(1)} %copy-done.5, f32[16,14,8,128]{3,2,1,0:T(8,128)S(1)} %bitcast.86, f32[16,14,8,128]{3,2,1,0:T(8,128)S(1)} %copy-done.2, f32[1024,128]{1,0:T(8,128)S(1)} %copy-done.4, f32[128,128]{1,0:T(8,128)S(1)} %get-tuple-element.47.inv0, s32[2,128]{1,0:T(2,128)S(1)} %copy-done.6), custom_call_target="tpu_custom_call" | custom-call | flops 500000000 | bytes 4194304 | tf_op jit(solution)/shard_map/pallas_call | solution.py:297
  97.2 7.4 %all-to-all-done.1.got.own = f32[16,96,128]{2,1,0:T(8,128)S(1)} async-done(((f32[16,96,128]{2,1,0:T(8,128)}), f32[16,96,128]{2,1,0:T(8,128)S(1)}, u32[]{:S(2)}, u32[]{:S(2)}) %all-to-all-start.1) | async-done | bytes 786464 | tf_op jit(solution)/shard_map/all_to_all | solution.py:296
  104.6 4.7 %collective-permute-start.11 = (f32[16,64,128]{2,1,0:T(8,128)S(1)}, f32[16,64,128]{2,1,0:T(8,128)S(1)}, u32[]{:S(2)}, u32[]{:S(2)}) collective-permute-start(f32[16,64,128]{2,1,0:T(8,128)S(1)} %slice.75), channel_id=1, source_target_pairs={{0,1},{1,0},{2,3},{3,2},{4,5},{5,4},{6,7},{7,6},{8,9},{9,8},{10,11... | collective-permute-start | bytes 1572872 | tf_op jit(solution)/shard_map/ppermute | solution.py:301
  109.3 1.3 %shard_map.73 = (f32[1024,256]{1,0:T(8,128)S(1)}, f32[128,256]{1,0:T(8,128)S(1)}) custom-call(s32[128]{0:T(128)S(1)} %copy-done.5, f32[1024,256]{1,0:T(8,128)S(1)} %copy-done, f32[16,96,128]{2,1,0:T(8,128)S(1)} %all-to-all-done.1.got.own, f32[1024,128]{1,0:T(8,128)S(1)} %get-tuple-element.49.plow, f32[128,128]{1,0:T(8,128)S(1)} %get-tuple-element.50.lsrc, ...), custom_call_target="tpu_custom_call" | custom-call | flops 500000000 | bytes 3145728 | tf_op jit(solution)/shard_map/pallas_call | solution.py:302
  110.7 0.2 collective-permute-done.11.oth
  110.9 2.0 %shard_map.74 = f32[1024,256]{1,0:T(8,128)} custom-call(s32[128]{0:T(128)S(1)} %copy-done.5, f32[1024,256]{1,0:T(8,128)S(1)} %get-tuple-element.51.cur, f32[16,96,128]{2,1,0:T(8,128)S(1)} %all-to-all-done.1.got.own, f32[16,64,128]{2,1,0:T(8,128)S(1)} %collective-permute-done.11.oth, f32[128,256]{1,0:T(8,128)S(1)} %get-tuple-element.52.kept), custom_call_target="tpu_custom_call" | custom-call | flops 500000000 | bytes 3145728 | tf_op jit(solution)/shard_map/pallas_call | solution.py:305
  (8 shorter events, 0.1 us)
Async XLA Ops:
  0.6 10.8 %copy-start = (f32[1024,256]{1,0:T(8,128)S(1)}, f32[1024,256]{1,0:T(8,128)}, u32[]{:S(2)}) copy-start(f32[1024,256]{1,0:T(8,128)} %a.1) | copy-start | bytes 3145732
  1.8 9.6 %collective-permute-start = (f32[8,8,8,256]{3,2,1,0:T(8,128)S(1)}, f32[8,8,8,256]{3,2,1,0:T(8,128)S(1)}, u32[]{:S(2)}, u32[]{:S(2)}) collective-permute-start(f32[8,8,8,256]{3,2,1,0:T(8,128)S(1)} %copy_bitcast_fusion), channel_id=1, source_target_pairs={{0,1},{32,33},{64,65},{96,97},{128,129},{160,161},{192,193},{224,2... | collective-permute-start | bytes 1572872 | tf_op jit(solution)/shard_map/ppermute | solution.py:258
  11.5 14.6 %copy-start.7 = (s32[2,128]{1,0:T(2,128)S(1)}, s32[2,128]{1,0:T(2,128)}, u32[]{:S(2)}) copy-start(s32[2,128]{1,0:T(2,128)} %dest.2) | copy-start | bytes 3076
  11.5 9.4 %collective-permute-start.1 = (f32[8,8,256]{2,1,0:T(8,128)S(1)}, f32[8,8,256]{2,1,0:T(8,128)S(1)}, u32[]{:S(2)}, u32[]{:S(2)}) collective-permute-start(f32[8,8,256]{2,1,0:T(8,128)S(1)} %get-tuple-element.29), channel_id=1, source_target_pairs={{1,30},{0,2},{33,62},{32,34},{65,94},{64,66},{97,126},{96,98},{129... | collective-permute-start | bytes 196616 | tf_op jit(solution)/shard_map/ppermute | solution.py:266
  15.2 7.0 %collective-permute-start.2 = (f32[8,8,256]{2,1,0:T(8,128)S(1)}, f32[8,8,256]{2,1,0:T(8,128)S(1)}, u32[]{:S(2)}, u32[]{:S(2)}) collective-permute-start(f32[8,8,256]{2,1,0:T(8,128)S(1)} %get-tuple-element.30), channel_id=1, source_target_pairs={{1,28},{0,4},{33,60},{32,36},{65,92},{64,68},{97,124},{96,100},{12... | collective-permute-start | bytes 196616 | tf_op jit(solution)/shard_map/ppermute | solution.py:266
  16.5 7.0 %collective-permute-start.3 = (f32[8,8,256]{2,1,0:T(8,128)S(1)}, f32[8,8,256]{2,1,0:T(8,128)S(1)}, u32[]{:S(2)}, u32[]{:S(2)}) collective-permute-start(f32[8,8,256]{2,1,0:T(8,128)S(1)} %get-tuple-element.31), channel_id=1, source_target_pairs={{1,26},{0,6},{33,58},{32,38},{65,90},{64,70},{97,122},{96,102},{12... | collective-permute-start | bytes 196616 | tf_op jit(solution)/shard_map/ppermute | solution.py:266
  17.8 7.0 %collective-permute-start.4 = (f32[8,8,256]{2,1,0:T(8,128)S(1)}, f32[8,8,256]{2,1,0:T(8,128)S(1)}, u32[]{:S(2)}, u32[]{:S(2)}) collective-permute-start(f32[8,8,256]{2,1,0:T(8,128)S(1)} %get-tuple-element.32), channel_id=1, source_target_pairs={{1,24},{0,8},{33,56},{32,40},{65,88},{64,72},{97,120},{96,104},{12... | collective-permute-start | bytes 196616 | tf_op jit(solution)/shard_map/ppermute | solution.py:266
  19.1 5.7 %collective-permute-start.5 = (f32[8,8,256]{2,1,0:T(8,128)S(1)}, f32[8,8,256]{2,1,0:T(8,128)S(1)}, u32[]{:S(2)}, u32[]{:S(2)}) collective-permute-start(f32[8,8,256]{2,1,0:T(8,128)S(1)} %get-tuple-element.33), channel_id=1, source_target_pairs={{1,22},{0,10},{33,54},{32,42},{65,86},{64,74},{97,118},{96,106},{1... | collective-permute-start | bytes 196616 | tf_op jit(solution)/shard_map/ppermute | solution.py:266
  20.8 4.0 %collective-permute-start.6 = (f32[8,8,256]{2,1,0:T(8,128)S(1)}, f32[8,8,256]{2,1,0:T(8,128)S(1)}, u32[]{:S(2)}, u32[]{:S(2)}) collective-permute-start(f32[8,8,256]{2,1,0:T(8,128)S(1)} %get-tuple-element.34), channel_id=1, source_target_pairs={{1,20},{0,12},{33,52},{32,44},{65,84},{64,76},{97,116},{96,108},{1... | collective-permute-start | bytes 196616 | tf_op jit(solution)/shard_map/ppermute | solution.py:266
  22.2 2.7 %collective-permute-start.7 = (f32[8,8,256]{2,1,0:T(8,128)S(1)}, f32[8,8,256]{2,1,0:T(8,128)S(1)}, u32[]{:S(2)}, u32[]{:S(2)}) collective-permute-start(f32[8,8,256]{2,1,0:T(8,128)S(1)} %get-tuple-element.35), channel_id=1, source_target_pairs={{1,18},{0,14},{33,50},{32,46},{65,82},{64,78},{97,114},{96,110},{1... | collective-permute-start | bytes 196616 | tf_op jit(solution)/shard_map/ppermute | solution.py:266
  23.5 2.6 %collective-permute-start.8 = (f32[8,8,256]{2,1,0:T(8,128)S(1)}, f32[8,8,256]{2,1,0:T(8,128)S(1)}, u32[]{:S(2)}, u32[]{:S(2)}) collective-permute-start(f32[8,8,256]{2,1,0:T(8,128)S(1)} %get-tuple-element.28.own), channel_id=1, source_target_pairs={{1,16},{33,48},{65,80},{97,112},{129,144},{161,176},{193,208},{225... | collective-permute-start | bytes 196616 | tf_op jit(solution)/shard_map/ppermute | solution.py:266
  27.5 17.1 %all-to-all-start = ((f32[16,9,8,128]{3,2,1,0:T(8,128)}), f32[16,9,8,128]{3,2,1,0:T(8,128)S(1)}, u32[]{:S(2)}, u32[]{:S(2)}) async-start(f32[16,9,8,128]{3,2,1,0:T(8,128)} %get-tuple-element.42), calls=%async_computation | async-start | bytes 1179648 | tf_op jit(solution)/shard_map/all_to_all | solution.py:280
  34.3 3.3 %collective-permute-start.9 = (f32[14,8,128]{2,1,0:T(8,128)S(1)}, f32[14,8,128]{2,1,0:T(8,128)S(1)}, u32[]{:S(2)}, u32[]{:S(2)}) collective-permute-start(f32[14,8,128]{2,1,0:T(8,128)S(1)} %get-tuple-element.40), channel_id=1, source_target_pairs={{0,1},{2,3},{4,5},{6,7},{8,9},{10,11},{12,13},{14,15},{16,17},{18,... | collective-permute-start | bytes 172040 | tf_op jit(solution)/shard_map/ppermute | solution.py:272
  37.6 7.1 %copy-start.5 = (s32[128]{0:T(128)S(1)}, s32[128]{0:T(128)}, u32[]{:S(2)}) copy-start(s32[128]{0:T(128)} %shard_map.69.meta) | copy-start | bytes 1540
  70.6 12.7 %collective-permute-start.10 = (f32[16,14,8,128]{3,2,1,0:T(8,128)S(1)}, f32[16,14,8,128]{3,2,1,0:T(8,128)S(1)}, u32[]{:S(2)}, u32[]{:S(2)}) collective-permute-start(f32[16,14,8,128]{3,2,1,0:T(8,128)S(1)} %bitcast.84), channel_id=1, source_target_pairs={{0,1},{1,0},{2,3},{3,2},{4,5},{5,4},{6,7},{7,6},{8,9},{9,8},{10,11... | collective-permute-start | bytes 2752520 | tf_op jit(solution)/shard_map/ppermute | solution.py:286
  83.3 4.0 %copy-start.1 = (f32[16,14,8,128]{3,2,1,0:T(8,128)}, f32[16,14,8,128]{3,2,1,0:T(8,128)S(1)}, u32[]{:S(2)}) copy-start(f32[16,14,8,128]{3,2,1,0:T(8,128)S(1)} %collective-permute-done.10.oth) | copy-start | bytes 2752516
  87.3 0.8 copy-start.3
  88.2 16.5 %all-to-all-start.1 = ((f32[16,96,128]{2,1,0:T(8,128)}), f32[16,96,128]{2,1,0:T(8,128)S(1)}, u32[]{:S(2)}, u32[]{:S(2)}) async-start(f32[16,96,128]{2,1,0:T(8,128)} %get-tuple-element.45), calls=%async_computation.1 | async-start | bytes 1572864 | tf_op jit(solution)/shard_map/all_to_all | solution.py:296
  91.9 0.7 copy-start.6
  92.6 1.2 %copy-start.2 = (f32[16,14,8,128]{3,2,1,0:T(8,128)S(1)}, f32[16,14,8,128]{3,2,1,0:T(8,128)}, u32[]{:S(2)}) copy-start(f32[16,14,8,128]{3,2,1,0:T(8,128)} %copy-done.1) | copy-start | bytes 2752516
  93.7 1.0 copy-start.4
  104.6 6.2 %collective-permute-start.11 = (f32[16,64,128]{2,1,0:T(8,128)S(1)}, f32[16,64,128]{2,1,0:T(8,128)S(1)}, u32[]{:S(2)}, u32[]{:S(2)}) collective-permute-start(f32[16,64,128]{2,1,0:T(8,128)S(1)} %slice.75), channel_id=1, source_target_pairs={{0,1},{1,0},{2,3},{3,2},{4,5},{5,4},{6,7},{7,6},{8,9},{9,8},{10,11... | collective-permute-start | bytes 1572872 | tf_op jit(solution)/shard_map/ppermute | solution.py:301

commit v8 on v7

--- a/solution.py
+++ b/solution.py
@@ -12,6 +12,7 @@
 NP = 16
 NZ = 16
 SLOTS = 8
+SENDS = ((1, 15), (2, 14), (3, 13), (4, 12), (5, 11), (6, 10), (7, 8), (9, 0))
 
 
 def dot16(a, b):
@@ -91,11 +92,33 @@
         meta[56 + slot] = lax.shift_right_logical(src[0, here], 3)
 
 
+def cut_kernel(a, over, *refs):
+    outs, sem = refs[:9], refs[9]
+    z, core = lax.axis_index("z"), lax.axis_index("core")
+
+    def bring(source, places):
+        copies = [
+            pltpu.make_async_copy(source.at[:, place], outs[i], sem.at[i]) for i, place in places
+        ]
+        for copy in copies:
+            copy.start()
+        for copy in copies:
+            copy.wait()
+
+    @pl.when((z == 0) & (core == 0))
+    def _():
+        bring(a, [(i, z0) for i, (z0, _) in enumerate(SENDS)] + [(8, 0)])
+
+    @pl.when((z == 0) & (core == 1))
+    def _():
+        bring(over, [(i, z1) for i, (_, z1) in enumerate(SENDS) if z1])
+
+
 def route_kernel(dest, a, own, *refs):
     got, (out, panel, last) = refs[:-3], refs[-3:]
     me = lax.axis_index("x") * 4 + lax.axis_index("y")
     root = (lax.axis_index("z") == 0) & (lax.axis_index("core") == 0)
-    share = own[...] * root.astype(jnp.float32)
+    share = jnp.where(root, own[...], 0.0)
     for ref in got:
         share = share + ref[...]
     for slot in range(SLOTS):
@@ -252,22 +275,27 @@
 
 
 def shards(a, row_perms, dest_rows, row_mask, col_mask):
-    core = lax.axis_index("core")
     smem = pl.BlockSpec(memory_space=pltpu.SMEM)
     cut = a.reshape(SLOTS, NZ, 8, 2 * W)
-    over = lax.ppermute(cut[:, 8:].transpose(1, 0, 2, 3), ("z", "core"), [(0, 1)])
-    pieces = [jnp.where(core == 0, cut[:, step % 8], over[8 - step]) for step in range(1, 9)]
-    pieces = lax.optimization_barrier(pieces)
+    over = lax.ppermute(a, ("z", "core"), [(0, 1)]).reshape(SLOTS, NZ, 8, 2 * W)
+    block = f32(SLOTS, 8, 2 * W)
+    hbm, vmem = pl.BlockSpec(memory_space=pltpu.HBM), pl.BlockSpec(memory_space=pltpu.VMEM)
+    *pieces, own0 = pl.pallas_call(
+        cut_kernel,
+        out_shape=[block] * 9,
+        in_specs=[hbm, vmem],
+        out_specs=[vmem] * 9,
+        scratch_shapes=[pltpu.SemaphoreType.DMA((9,))],
+        compiler_params=pltpu.CompilerParams(vmem_limit_bytes=8 * 2**20),
+    )(cut, over)
     got = []
-    for step in range(1, 9):
-        pairs = [(1, 2 * (NZ - step))]
-        if step < 8:
-            pairs.append((0, 2 * step))
-        got.append(lax.ppermute(pieces[step - 1], ("z", "core"), pairs))
+    for (z0, z1), piece in zip(SENDS, pieces):
+        pairs = ([(1, 2 * z1)] if z1 else []) + [(0, 2 * z0)]
+        got.append(lax.ppermute(piece, ("z", "core"), pairs))
 
     out0, panel, last = call(
         route_kernel, (f32(NP, 9, 8, W), f32(14, 8, W), f32(2, 8, W)), 10, moved=2**20
-    )(dest_rows, a[: 2 * W], pieces[7], *got)
+    )(dest_rows, a[: 2 * W], own0, *got)
     out0, maps = lax.optimization_barrier((out0, (dest_rows, row_mask, col_mask)))
     passed = lax.ppermute(panel, "core", [(0, 1)])
     meta = pl.pallas_call(
@@ -276,6 +304,7 @@
         in_specs=[smem] * 3,
         out_specs=smem,
         scratch_shapes=[pltpu.SMEM((2, W), jnp.int32)],
+        compiler_params=pltpu.CompilerParams(vmem_limit_bytes=8 * 2**20),
     )(*maps)
     got0 = lax.all_to_all(out0, ("x", "y"), 0, 0, tiled=True)
     payload, chunk = call(pack_kernel, (f32(14, 8, W), f32(4, 8, W)), 3, moved=2**19)(

time: 114 us -> 116 us (1.018)
  starting transfers between devices: 41.6 us -> 44.4 us
    ppermute x1, starting transfers between devices: 10.7 us -> 14.9 us  [shards(): oth = lax.ppermute(own, 'core', [(0, 1), (1, 0)])]
    ppermute x9, starting transfers between devices: 14.5 us -> 13 us  [the longest x8 11.8 us: shards(): got.append(lax.ppermute(piece, ('z', 'core'), pairs))]
    unnamed x16 -> x20, local copies, waits for them, and re-layouts: 3.72 us -> 5.05 us
    transpose x1 -> x0, local copies, waits for them, and re-layouts: 1.17 us -> none  [shards(): cut[:, 8:].transpose(1, 0, 2, 3)]
  transfers between devices with their start and end apart: 14 -> 14, of which waited for: 6 -> 7; matrix products, arithmetic and copies ran while one was open for 0% -> 0% of each run, Pallas kernels for 5% -> 5%
where the time goes in v8:
time: 116 us
  starting transfers between devices  44.4 us (38%)
  waiting for transfers between devices  26.7 us (23%)
  blocking collectives  24.8 us (21%)
  Pallas kernels  13.8 us (12%)
  local copies, waits for them, and re-layouts  5.1 us (4%)
    all_gather x1, blocking collectives, shards(): own = lax.all_gather(payload, 'z', axis=0, tiled=False)  24.8 us
    ppermute x1, starting transfers between devices, shards(): oth = lax.ppermute(own, 'core', [(0, 1), (1, 0)])  14.9 us
    ppermute x8, starting transfers between devices, shards(): got.append(lax.ppermute(piece, ('z', 'core'), pairs))  11.8 us
    ppermute x1, waiting for transfers between devices, shards(): over = lax.ppermute(a, ('z', 'core'), [(0, 1)]).reshape(SLOTS, NZ, 8, 2 * W)  9.22 us
    all_to_all x1, waiting for transfers between devices, shards(): got1 = lax.all_to_all(send, ('x', 'y'), 0, 0, tiled=True)  7.46 us
    all_to_all x1, waiting for transfers between devices, shards(): got0 = lax.all_to_all(out0, ('x', 'y'), 0, 0, tiled=True)  7.07 us
    all_to_all x1, starting transfers between devices, shards(): got0 = lax.all_to_all(out0, ('x', 'y'), 0, 0, tiled=True)  6.89 us
    unnamed x20, local copies, waits for them, and re-layouts  5.05 us
  transfers between devices with their start and end apart: 14, of which 7 were waited for; matrix products, arithmetic and copies ran while one was open for 0% of the time, Pallas kernels for 5%

profile of v8, /device:TPU:1, one launch (start us, length us, event | category | flops | bytes accessed | tf_op | source)
XLA Modules:
  0.0 115.8 jit_solution(10561954439224700273)
XLA Ops:
  0.6 1.3 %collective-permute-start = (f32[1024,256]{1,0:T(8,128)}, f32[1024,256]{1,0:T(8,128)S(1)}, u32[]{:S(2)}, u32[]{:S(2)}) collective-permute-start(f32[1024,256]{1,0:T(8,128)} %a.1), channel_id=1, source_target_pairs={{0,1},{32,33},{64,65},{96,97},{128,129},{160,161},{192,193},{224,2... | collective-permute-start | bytes 3145736 | tf_op jit(solution)/shard_map/ppermute | solution.py:280
  1.9 9.2 %collective-permute-done = f32[1024,256]{1,0:T(8,128)S(1)} collective-permute-done((f32[1024,256]{1,0:T(8,128)}, f32[1024,256]{1,0:T(8,128)S(1)}, u32[]{:S(2)}, u32[]{:S(2)}) %collective-permute-start) | collective-permute-done | bytes 1048608 | tf_op jit(solution)/shard_map/ppermute | solution.py:280
  11.1 1.2 %copy-done = f32[1024,256]{1,0:T(8,128)S(1)} copy-done((f32[1024,256]{1,0:T(8,128)S(1)}, f32[1024,256]{1,0:T(8,128)}, u32[]{:S(2)}) %copy-start) | copy-done | bytes 1048600
  12.4 0.2 shard_map.68
  12.6 2.8 %collective-permute-start.1 = (f32[8,8,256]{2,1,0:T(8,128)S(1)}, f32[8,8,256]{2,1,0:T(8,128)S(1)}, u32[]{:S(2)}, u32[]{:S(2)}) collective-permute-start(f32[8,8,256]{2,1,0:T(8,128)S(1)} %get-tuple-element.30), channel_id=1, source_target_pairs={{1,30},{0,2},{33,62},{32,34},{65,94},{64,66},{97,126},{96,98},{129... | collective-permute-start | bytes 196616 | tf_op jit(solution)/shard_map/ppermute | solution.py:294
  15.3 1.3 %collective-permute-start.2 = (f32[8,8,256]{2,1,0:T(8,128)S(1)}, f32[8,8,256]{2,1,0:T(8,128)S(1)}, u32[]{:S(2)}, u32[]{:S(2)}) collective-permute-start(f32[8,8,256]{2,1,0:T(8,128)S(1)} %get-tuple-element.31), channel_id=1, source_target_pairs={{1,28},{0,4},{33,60},{32,36},{65,92},{64,68},{97,124},{96,100},{12... | collective-permute-start | bytes 196616 | tf_op jit(solution)/shard_map/ppermute | solution.py:294
  16.6 1.3 %collective-permute-start.3 = (f32[8,8,256]{2,1,0:T(8,128)S(1)}, f32[8,8,256]{2,1,0:T(8,128)S(1)}, u32[]{:S(2)}, u32[]{:S(2)}) collective-permute-start(f32[8,8,256]{2,1,0:T(8,128)S(1)} %get-tuple-element.32), channel_id=1, source_target_pairs={{1,26},{0,6},{33,58},{32,38},{65,90},{64,70},{97,122},{96,102},{12... | collective-permute-start | bytes 196616 | tf_op jit(solution)/shard_map/ppermute | solution.py:294
  17.9 1.3 %collective-permute-start.4 = (f32[8,8,256]{2,1,0:T(8,128)S(1)}, f32[8,8,256]{2,1,0:T(8,128)S(1)}, u32[]{:S(2)}, u32[]{:S(2)}) collective-permute-start(f32[8,8,256]{2,1,0:T(8,128)S(1)} %get-tuple-element.33), channel_id=1, source_target_pairs={{1,24},{0,8},{33,56},{32,40},{65,88},{64,72},{97,120},{96,104},{12... | collective-permute-start | bytes 196616 | tf_op jit(solution)/shard_map/ppermute | solution.py:294
  19.2 1.8 %collective-permute-start.5 = (f32[8,8,256]{2,1,0:T(8,128)S(1)}, f32[8,8,256]{2,1,0:T(8,128)S(1)}, u32[]{:S(2)}, u32[]{:S(2)}) collective-permute-start(f32[8,8,256]{2,1,0:T(8,128)S(1)} %get-tuple-element.34), channel_id=1, source_target_pairs={{1,22},{0,10},{33,54},{32,42},{65,86},{64,74},{97,118},{96,106},{1... | collective-permute-start | bytes 196616 | tf_op jit(solution)/shard_map/ppermute | solution.py:294
  21.0 0.0 collective-permute-done.1.refs_0_
  21.0 1.3 %collective-permute-start.6 = (f32[8,8,256]{2,1,0:T(8,128)S(1)}, f32[8,8,256]{2,1,0:T(8,128)S(1)}, u32[]{:S(2)}, u32[]{:S(2)}) collective-permute-start(f32[8,8,256]{2,1,0:T(8,128)S(1)} %get-tuple-element.35), channel_id=1, source_target_pairs={{1,20},{0,12},{33,52},{32,44},{65,84},{64,76},{97,116},{96,108},{1... | collective-permute-start | bytes 196616 | tf_op jit(solution)/shard_map/ppermute | solution.py:294
  22.3 0.0 collective-permute-done.2.refs_1_
  22.3 1.4 %collective-permute-start.7 = (f32[8,8,256]{2,1,0:T(8,128)S(1)}, f32[8,8,256]{2,1,0:T(8,128)S(1)}, u32[]{:S(2)}, u32[]{:S(2)}) collective-permute-start(f32[8,8,256]{2,1,0:T(8,128)S(1)} %get-tuple-element.36), channel_id=1, source_target_pairs={{1,16},{0,14},{33,48},{32,46},{65,80},{64,78},{97,112},{96,110},{1... | collective-permute-start | bytes 196616 | tf_op jit(solution)/shard_map/ppermute | solution.py:294
  23.7 0.0 collective-permute-done.3.refs_2_
  23.7 0.7 collective-permute-start.8
  24.4 0.0 copy-done.1
  24.4 0.0 copy-start.7
  24.5 0.0 collective-permute-done.4.refs_3_
  24.5 0.0 collective-permute-done.5.refs_4_
  24.5 0.0 collective-permute-done.6.refs_5_
  24.5 0.5 collective-permute-done.7.refs_6_
  25.0 0.0 collective-permute-done.8.refs_7_
  25.0 0.1 copy-done.7
  25.1 1.4 %shard_map.69 = (f32[16,9,8,128]{3,2,1,0:T(8,128)}, f32[14,8,128]{2,1,0:T(8,128)S(1)}, f32[2,8,128]{2,1,0:T(8,128)S(1)}) custom-call(s32[2,128]{1,0:T(2,128)S(1)} %copy-done.7, f32[256,256]{1,0:T(8,128)S(1)} %slice.6.a, f32[8,8,256]{2,1,0:T(8,128)S(1)} %get-tuple-element.29.own, f32[8,8,256]{2,1,0:T(8,128)S(1)} %collective-permute-done.1.refs_0_, ...), custom_call_target="tpu_custom_call" | custom-call | bytes 1048576 | tf_op jit(solution)/shard_map/pallas_call | solution.py:296
  26.6 6.9 %all-to-all-start = ((f32[16,9,8,128]{3,2,1,0:T(8,128)}), f32[16,9,8,128]{3,2,1,0:T(8,128)S(1)}, u32[]{:S(2)}, u32[]{:S(2)}) async-start(f32[16,9,8,128]{3,2,1,0:T(8,128)} %get-tuple-element.44), calls=%async_computation | async-start | bytes 1179648 | tf_op jit(solution)/shard_map/all_to_all | solution.py:309
  33.5 0.0 copy-start.8
  33.5 1.3 %collective-permute-start.9 = (f32[14,8,128]{2,1,0:T(8,128)S(1)}, f32[14,8,128]{2,1,0:T(8,128)S(1)}, u32[]{:S(2)}, u32[]{:S(2)}) collective-permute-start(f32[14,8,128]{2,1,0:T(8,128)S(1)} %get-tuple-element.42), channel_id=1, source_target_pairs={{0,1},{2,3},{4,5},{6,7},{8,9},{10,11},{12,13},{14,15},{16,17},{18,... | collective-permute-start | bytes 172040 | tf_op jit(solution)/shard_map/ppermute | solution.py:300
  34.8 1.9 %shard_map.70.meta = s32[128]{0:T(128)S(1)} custom-call(s32[2,128]{1,0:T(2,128)S(1)} %copy-done.7, s32[2,128]{1,0:T(2,128)S(1)} %copy-done.8, s32[2,64]{1,0:T(2,128)S(1)} %copy-done.9), custom_call_target="tpu_custom_call" | custom-call | tf_op jit(solution)/shard_map/pallas_call | solution.py:301
  36.7 0.2 collective-permute-done.9.passed
  36.9 7.1 %all-to-all-done.got = f32[16,9,8,128]{3,2,1,0:T(8,128)S(1)} async-done(((f32[16,9,8,128]{3,2,1,0:T(8,128)}), f32[16,9,8,128]{3,2,1,0:T(8,128)S(1)}, u32[]{:S(2)}, u32[]{:S(2)}) %all-to-all-start) | async-done | bytes 589856 | tf_op jit(solution)/shard_map/all_to_all | solution.py:309
  43.9 0.6 shard_map.71
  44.5 24.8 %all-gather = f32[224,8,128]{2,1,0:T(8,128)S(1)} all-gather(f32[14,8,128]{2,1,0:T(8,128)S(1)} %get-tuple-element.45), channel_id=2, replica_groups=mesh['x'=4,'y'=4,'z'=16,'core'=2] {'z'}, dimensions={0}, use_global_device_ids=true | all-gather | bytes 974848 | tf_op jit(solution)/shard_map/all_gather | solution.py:314
  69.4 14.9 %collective-permute-start.10 = (f32[16,14,8,128]{3,2,1,0:T(8,128)S(1)}, f32[16,14,8,128]{3,2,1,0:T(8,128)S(1)}, u32[]{:S(2)}, u32[]{:S(2)}) collective-permute-start(f32[16,14,8,128]{3,2,1,0:T(8,128)S(1)} %bitcast.3), channel_id=1, source_target_pairs={{0,1},{1,0},{2,3},{3,2},{4,5},{5,4},{6,7},{7,6},{8,9},{9,8},{10,11... | collective-permute-start | bytes 2752520 | tf_op jit(solution)/shard_map/ppermute | solution.py:315
  84.2 2.1 %collective-permute-done.10.oth = f32[16,14,8,128]{3,2,1,0:T(8,128)S(1)} collective-permute-done((f32[16,14,8,128]{3,2,1,0:T(8,128)S(1)}, f32[16,14,8,128]{3,2,1,0:T(8,128)S(1)}, u32[]{:S(2)}, u32[]{:S(2)}) %collective-permute-start.10) | collective-permute-done | bytes 917536 | tf_op jit(solution)/shard_map/ppermute | solution.py:315
  86.3 4.0 %shard_map.72 = (f32[16,96,128]{2,1,0:T(8,128)}, f32[1024,128]{1,0:T(8,128)S(1)}, f32[1024,128]{1,0:T(8,128)S(1)}, f32[128,128]{1,0:T(8,128)S(1)}, f32[128,128]{1,0:T(8,128)S(1)}) custom-call(s32[128]{0:T(128)S(1)} %shard_map.70.meta, f32[16,14,8,128]{3,2,1,0:T(8,128)S(1)} %bitcast.4, f32[16,14,8,128]{3,2,1,0:T(8,128)S(1)} %collective-permute-done.10.oth, ...), custom_call_target="tpu_custom_call" | custom-call | flops 500000000 | bytes 4194304 | tf_op jit(solution)/shard_map/pallas_call | solution.py:317
  90.4 0.0 copy-done.2
  90.4 0.8 copy-done.4
  91.2 3.6 %all-to-all-start.1 = ((f32[16,96,128]{2,1,0:T(8,128)}), f32[16,96,128]{2,1,0:T(8,128)S(1)}, u32[]{:S(2)}, u32[]{:S(2)}) async-start(f32[16,96,128]{2,1,0:T(8,128)} %get-tuple-element.47), calls=%async_computation.1 | async-start | bytes 1572864 | tf_op jit(solution)/shard_map/all_to_all | solution.py:325
  94.8 0.0 copy-start.6
  94.8 0.7 copy-done.6
  95.5 1.2 %copy-done.3 = f32[16,14,8,128]{3,2,1,0:T(8,128)S(1)} copy-done((f32[16,14,8,128]{3,2,1,0:T(8,128)S(1)}, f32[16,14,8,128]{3,2,1,0:T(8,128)}, u32[]{:S(2)}) %copy-start.3) | copy-done | bytes 917528
  96.7 1.0 copy-done.5
  97.7 2.4 %shard_map.73 = f32[1024,256]{1,0:T(8,128)} custom-call(s32[128]{0:T(128)S(1)} %shard_map.70.meta, f32[16,14,8,128]{3,2,1,0:T(8,128)S(1)} %bitcast.5, f32[16,14,8,128]{3,2,1,0:T(8,128)S(1)} %copy-done.3, f32[1024,128]{1,0:T(8,128)S(1)} %copy-done.5, f32[128,128]{1,0:T(8,128)S(1)} %get-tuple-element.49.inv0, s32[2,128]{1,0:T(2,128)S(1)} %copy-done.6), custom_call_target="tpu_custom_call" | custom-call | flops 500000000 | bytes 4194304 | tf_op jit(solution)/shard_map/pallas_call | solution.py:326
  100.1 7.5 %all-to-all-done.1.got.own = f32[16,96,128]{2,1,0:T(8,128)S(1)} async-done(((f32[16,96,128]{2,1,0:T(8,128)}), f32[16,96,128]{2,1,0:T(8,128)S(1)}, u32[]{:S(2)}, u32[]{:S(2)}) %all-to-all-start.1) | async-done | bytes 786464 | tf_op jit(solution)/shard_map/all_to_all | solution.py:325
  107.6 4.7 %collective-permute-start.11 = (f32[16,64,128]{2,1,0:T(8,128)S(1)}, f32[16,64,128]{2,1,0:T(8,128)S(1)}, u32[]{:S(2)}, u32[]{:S(2)}) collective-permute-start(f32[16,64,128]{2,1,0:T(8,128)S(1)} %slice.7), channel_id=1, source_target_pairs={{0,1},{1,0},{2,3},{3,2},{4,5},{5,4},{6,7},{7,6},{8,9},{9,8},{10,11... | collective-permute-start | bytes 1572872 | tf_op jit(solution)/shard_map/ppermute | solution.py:330
  112.3 1.3 %shard_map.74 = (f32[1024,256]{1,0:T(8,128)S(1)}, f32[128,256]{1,0:T(8,128)S(1)}) custom-call(s32[128]{0:T(128)S(1)} %shard_map.70.meta, f32[1024,256]{1,0:T(8,128)S(1)} %copy-done.1, f32[16,96,128]{2,1,0:T(8,128)S(1)} %all-to-all-done.1.got.own, f32[1024,128]{1,0:T(8,128)S(1)} %get-tuple-element.51.plow, f32[128,128]{1,0:T(8,128)S(1)} %get-tuple-element.52.lsrc, ...), custom_call_target="tpu_custom_call" | custom-call | flops 500000000 | bytes 3145728 | tf_op jit(solution)/shard_map/pallas_call | solution.py:331
  113.6 0.2 collective-permute-done.11.oth
  113.8 2.0 %shard_map.75 = f32[1024,256]{1,0:T(8,128)} custom-call(s32[128]{0:T(128)S(1)} %shard_map.70.meta, f32[1024,256]{1,0:T(8,128)S(1)} %get-tuple-element.53.cur, f32[16,96,128]{2,1,0:T(8,128)S(1)} %all-to-all-done.1.got.own, f32[16,64,128]{2,1,0:T(8,128)S(1)} %collective-permute-done.11.oth, f32[128,256]{1,0:T(8,128)S(1)} %get-tuple-element.54.kept), custom_call_target="tpu_custom_call" | custom-call | flops 500000000 | bytes 3145728 | tf_op jit(solution)/shard_map/pallas_call | solution.py:334
  (11 shorter events, 0.1 us)
Async XLA Ops:
  0.6 10.5 %collective-permute-start = (f32[1024,256]{1,0:T(8,128)}, f32[1024,256]{1,0:T(8,128)S(1)}, u32[]{:S(2)}, u32[]{:S(2)}) collective-permute-start(f32[1024,256]{1,0:T(8,128)} %a.1), channel_id=1, source_target_pairs={{0,1},{32,33},{64,65},{96,97},{128,129},{160,161},{192,193},{224,2... | collective-permute-start | bytes 3145736 | tf_op jit(solution)/shard_map/ppermute | solution.py:280
  11.1 1.2 %copy-start = (f32[1024,256]{1,0:T(8,128)S(1)}, f32[1024,256]{1,0:T(8,128)}, u32[]{:S(2)}) copy-start(f32[1024,256]{1,0:T(8,128)} %a.1) | copy-start | bytes 3145732
  12.4 12.0 %copy-start.1 = (f32[1024,256]{1,0:T(8,128)S(1)}, f32[1024,256]{1,0:T(8,128)}, u32[]{:S(2)}) copy-start(f32[1024,256]{1,0:T(8,128)} %a.1) | copy-start | bytes 3145732
  12.6 8.5 %collective-permute-start.1 = (f32[8,8,256]{2,1,0:T(8,128)S(1)}, f32[8,8,256]{2,1,0:T(8,128)S(1)}, u32[]{:S(2)}, u32[]{:S(2)}) collective-permute-start(f32[8,8,256]{2,1,0:T(8,128)S(1)} %get-tuple-element.30), channel_id=1, source_target_pairs={{1,30},{0,2},{33,62},{32,34},{65,94},{64,66},{97,126},{96,98},{129... | collective-permute-start | bytes 196616 | tf_op jit(solution)/shard_map/ppermute | solution.py:294
  15.3 7.0 %collective-permute-start.2 = (f32[8,8,256]{2,1,0:T(8,128)S(1)}, f32[8,8,256]{2,1,0:T(8,128)S(1)}, u32[]{:S(2)}, u32[]{:S(2)}) collective-permute-start(f32[8,8,256]{2,1,0:T(8,128)S(1)} %get-tuple-element.31), channel_id=1, source_target_pairs={{1,28},{0,4},{33,60},{32,36},{65,92},{64,68},{97,124},{96,100},{12... | collective-permute-start | bytes 196616 | tf_op jit(solution)/shard_map/ppermute | solution.py:294
  16.6 7.1 %collective-permute-start.3 = (f32[8,8,256]{2,1,0:T(8,128)S(1)}, f32[8,8,256]{2,1,0:T(8,128)S(1)}, u32[]{:S(2)}, u32[]{:S(2)}) collective-permute-start(f32[8,8,256]{2,1,0:T(8,128)S(1)} %get-tuple-element.32), channel_id=1, source_target_pairs={{1,26},{0,6},{33,58},{32,38},{65,90},{64,70},{97,122},{96,102},{12... | collective-permute-start | bytes 196616 | tf_op jit(solution)/shard_map/ppermute | solution.py:294
  17.9 6.5 %collective-permute-start.4 = (f32[8,8,256]{2,1,0:T(8,128)S(1)}, f32[8,8,256]{2,1,0:T(8,128)S(1)}, u32[]{:S(2)}, u32[]{:S(2)}) collective-permute-start(f32[8,8,256]{2,1,0:T(8,128)S(1)} %get-tuple-element.33), channel_id=1, source_target_pairs={{1,24},{0,8},{33,56},{32,40},{65,88},{64,72},{97,120},{96,104},{12... | collective-permute-start | bytes 196616 | tf_op jit(solution)/shard_map/ppermute | solution.py:294
  19.2 5.2 %collective-permute-start.5 = (f32[8,8,256]{2,1,0:T(8,128)S(1)}, f32[8,8,256]{2,1,0:T(8,128)S(1)}, u32[]{:S(2)}, u32[]{:S(2)}) collective-permute-start(f32[8,8,256]{2,1,0:T(8,128)S(1)} %get-tuple-element.34), channel_id=1, source_target_pairs={{1,22},{0,10},{33,54},{32,42},{65,86},{64,74},{97,118},{96,106},{1... | collective-permute-start | bytes 196616 | tf_op jit(solution)/shard_map/ppermute | solution.py:294
  21.0 3.4 %collective-permute-start.6 = (f32[8,8,256]{2,1,0:T(8,128)S(1)}, f32[8,8,256]{2,1,0:T(8,128)S(1)}, u32[]{:S(2)}, u32[]{:S(2)}) collective-permute-start(f32[8,8,256]{2,1,0:T(8,128)S(1)} %get-tuple-element.35), channel_id=1, source_target_pairs={{1,20},{0,12},{33,52},{32,44},{65,84},{64,76},{97,116},{96,108},{1... | collective-permute-start | bytes 196616 | tf_op jit(solution)/shard_map/ppermute | solution.py:294
  22.3 2.7 %collective-permute-start.7 = (f32[8,8,256]{2,1,0:T(8,128)S(1)}, f32[8,8,256]{2,1,0:T(8,128)S(1)}, u32[]{:S(2)}, u32[]{:S(2)}) collective-permute-start(f32[8,8,256]{2,1,0:T(8,128)S(1)} %get-tuple-element.36), channel_id=1, source_target_pairs={{1,16},{0,14},{33,48},{32,46},{65,80},{64,78},{97,112},{96,110},{1... | collective-permute-start | bytes 196616 | tf_op jit(solution)/shard_map/ppermute | solution.py:294
  23.7 1.3 %collective-permute-start.8 = (f32[8,8,256]{2,1,0:T(8,128)S(1)}, f32[8,8,256]{2,1,0:T(8,128)S(1)}, u32[]{:S(2)}, u32[]{:S(2)}) collective-permute-start(f32[8,8,256]{2,1,0:T(8,128)S(1)} %get-tuple-element.37), channel_id=1, source_target_pairs={{0,18},{32,50},{64,82},{96,114},{128,146},{160,178},{192,210},{224... | collective-permute-start | bytes 196616 | tf_op jit(solution)/shard_map/ppermute | solution.py:294
  24.4 0.7 copy-start.7
  26.6 8.2 %copy-start.9 = (s32[2,64]{1,0:T(2,128)S(1)}, s32[2,64]{1,0:T(2,128)}, u32[]{:S(2)}) copy-start(s32[2,64]{1,0:T(2,128)} %col_mask) | copy-start | bytes 1540
  26.6 17.4 %all-to-all-start = ((f32[16,9,8,128]{3,2,1,0:T(8,128)}), f32[16,9,8,128]{3,2,1,0:T(8,128)S(1)}, u32[]{:S(2)}, u32[]{:S(2)}) async-start(f32[16,9,8,128]{3,2,1,0:T(8,128)} %get-tuple-element.44), calls=%async_computation | async-start | bytes 1179648 | tf_op jit(solution)/shard_map/all_to_all | solution.py:309
  33.5 1.3 %copy-start.8 = (s32[2,128]{1,0:T(2,128)S(1)}, s32[2,128]{1,0:T(2,128)}, u32[]{:S(2)}) copy-start(s32[2,128]{1,0:T(2,128)} %row_mask) | copy-start | bytes 3076
  33.5 3.4 %collective-permute-start.9 = (f32[14,8,128]{2,1,0:T(8,128)S(1)}, f32[14,8,128]{2,1,0:T(8,128)S(1)}, u32[]{:S(2)}, u32[]{:S(2)}) collective-permute-start(f32[14,8,128]{2,1,0:T(8,128)S(1)} %get-tuple-element.42), channel_id=1, source_target_pairs={{0,1},{2,3},{4,5},{6,7},{8,9},{10,11},{12,13},{14,15},{16,17},{18,... | collective-permute-start | bytes 172040 | tf_op jit(solution)/shard_map/ppermute | solution.py:300
  69.4 17.0 %collective-permute-start.10 = (f32[16,14,8,128]{3,2,1,0:T(8,128)S(1)}, f32[16,14,8,128]{3,2,1,0:T(8,128)S(1)}, u32[]{:S(2)}, u32[]{:S(2)}) collective-permute-start(f32[16,14,8,128]{3,2,1,0:T(8,128)S(1)} %bitcast.3), channel_id=1, source_target_pairs={{0,1},{1,0},{2,3},{3,2},{4,5},{5,4},{6,7},{7,6},{8,9},{9,8},{10,11... | collective-permute-start | bytes 2752520 | tf_op jit(solution)/shard_map/ppermute | solution.py:315
  86.3 4.0 %copy-start.2 = (f32[16,14,8,128]{3,2,1,0:T(8,128)}, f32[16,14,8,128]{3,2,1,0:T(8,128)S(1)}, u32[]{:S(2)}) copy-start(f32[16,14,8,128]{3,2,1,0:T(8,128)S(1)} %collective-permute-done.10.oth) | copy-start | bytes 2752516
  90.4 0.8 copy-start.4
  91.2 16.4 %all-to-all-start.1 = ((f32[16,96,128]{2,1,0:T(8,128)}), f32[16,96,128]{2,1,0:T(8,128)S(1)}, u32[]{:S(2)}, u32[]{:S(2)}) async-start(f32[16,96,128]{2,1,0:T(8,128)} %get-tuple-element.47), calls=%async_computation.1 | async-start | bytes 1572864 | tf_op jit(solution)/shard_map/all_to_all | solution.py:325
  94.8 0.7 copy-start.6
  95.5 1.2 %copy-start.3 = (f32[16,14,8,128]{3,2,1,0:T(8,128)S(1)}, f32[16,14,8,128]{3,2,1,0:T(8,128)}, u32[]{:S(2)}) copy-start(f32[16,14,8,128]{3,2,1,0:T(8,128)} %copy-done.2) | copy-start | bytes 2752516
  96.7 1.0 copy-start.5
  107.6 6.2 %collective-permute-start.11 = (f32[16,64,128]{2,1,0:T(8,128)S(1)}, f32[16,64,128]{2,1,0:T(8,128)S(1)}, u32[]{:S(2)}, u32[]{:S(2)}) collective-permute-start(f32[16,64,128]{2,1,0:T(8,128)S(1)} %slice.7), channel_id=1, source_target_pairs={{0,1},{1,0},{2,3},{3,2},{4,5},{5,4},{6,7},{7,6},{8,9},{9,8},{10,11... | collective-permute-start | bytes 1572872 | tf_op jit(solution)/shard_map/ppermute | solution.py:330

commit v9 on v7

--- a/solution.py
+++ b/solution.py
@@ -12,6 +12,7 @@
 NP = 16
 NZ = 16
 SLOTS = 8
+SENDS = ((1, 15), (2, 14), (7, 9), (8, 10), (6, 11), (5, 12), (4, 13), (3, 0))
 
 
 def dot16(a, b):
@@ -156,18 +157,23 @@
     )
 
 
-def factor(meta, head, panel, send, plow, low1, inv0, lsrc):
+def lower1(meta, head, panel, ext0, inv1):
+    kept01 = tile(head, 11) * meta[2].astype(jnp.float32)
+    col1 = jnp.concatenate([tile(panel, 7 + s) for s in range(7)] + [tile(head, 1)], axis=0)
+    return flagged(meta, dot(col1 - dot(ext0, kept01), inv1[...]), 16)
+
+
+def factor(meta, head, panel, send, plow, inv0, inv1, lsrc, low1):
     inv = refine(tile(head, 10))
     inv0[...] = inv
     kept01 = tile(head, 11) * meta[2].astype(jnp.float32)
     low_src = dot(tile(head, 12), inv) * meta[3].astype(jnp.float32)
     lsrc[...] = low_src
-    inv1 = refine(tile(head, 13) - dot(low_src, kept01))
+    inv1[...] = refine(tile(head, 13) - dot(low_src, kept01))
     ext0 = jnp.concatenate([tile(head, 2 + s) for s in range(SLOTS)], axis=0)
     ext0 = flagged(meta, dot(ext0, inv), 24)
     plow[...] = ext0
-    col1 = jnp.concatenate([tile(panel, 7 + s) for s in range(7)] + [tile(head, 1)], axis=0)
-    low1[...] = flagged(meta, dot(col1 - dot(ext0, kept01), inv1), 16)
+    low1[...] = lower1(meta, head, panel, ext0, inv1)
     for slot in range(SLOTS):
         half = pl.ds(pl.multiple_of(slot * W + meta[0] * H, H), H)
         send[meta[32 + slot], :H] = low1[half, :]
@@ -185,10 +191,12 @@
     send[:, H:] = jnp.broadcast_to(chunk[...].reshape(1, 32, W), (NP, 32, W))
 
 
-def panels_kernel(meta, own, oth, low1, inv0, perms, lpan):
+def panels_kernel(meta, own, oth, plow, inv0, inv1, perms, lpan):
     def write(head, panel):
         col0 = jnp.concatenate([tile(panel, s) for s in range(7)] + [tile(head, 0)], axis=0)
         lpan[:, :W] = flagged(meta, dot(col0, reorder_columns(perms, 0, inv0[...])), 8)
+        low = lower1(meta, head, panel, plow[...], inv1)
+        lpan[:, W:] = reorder_columns(perms, 1, low)
 
     @pl.when(meta[0] == 0)
     def _():
@@ -198,7 +206,13 @@
     def _():
         write(oth, own)
 
-    lpan[:, W:] = reorder_columns(perms, 1, low1[...])
+
+def subtract(meta, half_of, kept, out, half):
+    low = jnp.concatenate([half_of(meta[40 + slot]) for slot in range(SLOTS)], axis=0)
+    prod = dot(low, kept[...])
+    for slot in range(SLOTS):
+        here = pl.ds(pl.multiple_of(slot * W + half * H, H), H)
+        out[here, :] = out[here, :] - prod[slot * H : (slot + 1) * H]
 
 
 def first_kernel(meta, a, got, plow, lsrc, perms, cur, kept):
@@ -222,14 +236,12 @@
         cur[:W] = reorder_rows(perms, 0, rows[:W]) - prod[:W]
         cur[W : 2 * W] = reorder_rows(perms, 1, next1)
 
-
-def second_kernel(meta, cur, own, oth, kept, out, low):
-    core = meta[0]
-    for slot in range(SLOTS):
-        dev = meta[40 + slot]
-        low[pl.ds(pl.multiple_of(slot * W + core * H, H), H), :] = own[dev, :H]
-        low[pl.ds(pl.multiple_of(slot * W + (1 - core) * H, H), H), :] = oth[dev]
-    out[...] = cur[...] - dot(low[...], kept[...])
+    subtract(meta, lambda dev: got[dev, :H], kept, cur, meta[0])
+
+
+def second_kernel(meta, cur, oth, kept, out):
+    out[...] = cur[...]
+    subtract(meta, lambda dev: oth[dev], kept, out, 1 - meta[0])
 
 
 def f32(*shape):
@@ -239,12 +251,12 @@
 def call(kernel, out_shape, n_in, scratch=(), flops=0, moved=0):
     smem = pl.BlockSpec(memory_space=pltpu.SMEM)
     vmem = pl.BlockSpec(memory_space=pltpu.VMEM)
-    multi = isinstance(out_shape, (tuple, list))
+    out_specs = [vmem] * len(out_shape) if isinstance(out_shape, tuple) else vmem
     return pl.pallas_call(
         kernel,
         out_shape=out_shape,
         in_specs=[smem] + [vmem] * n_in,
-        out_specs=[vmem] * len(out_shape) if multi else vmem,
+        out_specs=out_specs,
         scratch_shapes=list(scratch),
         compiler_params=pltpu.CompilerParams(vmem_limit_bytes=24 * 2**20),
         cost_estimate=pl.CostEstimate(flops=flops, bytes_accessed=moved, transcendentals=0),
@@ -255,19 +267,18 @@
     core = lax.axis_index("core")
     smem = pl.BlockSpec(memory_space=pltpu.SMEM)
     cut = a.reshape(SLOTS, NZ, 8, 2 * W)
-    over = lax.ppermute(cut[:, 8:].transpose(1, 0, 2, 3), ("z", "core"), [(0, 1)])
-    pieces = [jnp.where(core == 0, cut[:, step % 8], over[8 - step]) for step in range(1, 9)]
-    pieces = lax.optimization_barrier(pieces)
+    over = lax.ppermute(cut[:, 9:].transpose(1, 0, 2, 3), ("z", "core"), [(0, 1)])
+    *pieces, own0 = lax.optimization_barrier(
+        [jnp.where(core == 0, cut[:, z0], over[max(z1 - 9, 0)]) for z0, z1 in (*SENDS, (0, 0))]
+    )
     got = []
-    for step in range(1, 9):
-        pairs = [(1, 2 * (NZ - step))]
-        if step < 8:
-            pairs.append((0, 2 * step))
-        got.append(lax.ppermute(pieces[step - 1], ("z", "core"), pairs))
+    for (z0, z1), piece in zip(SENDS, pieces):
+        pairs = ([(1, 2 * z1)] if z1 else []) + [(0, 2 * z0)]
+        got.append(lax.ppermute(piece, ("z", "core"), pairs))
 
     out0, panel, last = call(
         route_kernel, (f32(NP, 9, 8, W), f32(14, 8, W), f32(2, 8, W)), 10, moved=2**20
-    )(dest_rows, a[: 2 * W], pieces[7], *got)
+    )(dest_rows, a[: 2 * W], own0, *got)
     out0, maps = lax.optimization_barrier((out0, (dest_rows, row_mask, col_mask)))
     passed = lax.ppermute(panel, "core", [(0, 1)])
     meta = pl.pallas_call(
@@ -285,31 +296,27 @@
     own = lax.all_gather(payload, "z", axis=0, tiled=False)
     oth = lax.ppermute(own, "core", [(0, 1), (1, 0)])
 
-    send, plow, low1, inv0, lsrc = call(
+    send, plow, inv0, inv1, lsrc = call(
         factor_kernel,
-        (f32(NP, H + 32, W), f32(SLOTS * W, W), f32(SLOTS * W, W), f32(W, W), f32(W, W)),
+        (f32(NP, H + 32, W), f32(SLOTS * W, W), f32(W, W), f32(W, W), f32(W, W)),
         3,
+        scratch=(pltpu.VMEM((SLOTS * W, W), jnp.float32),),
         flops=5 * 10**8,
         moved=4 * 2**20,
     )(meta, own, oth, chunk)
 
     got1 = lax.all_to_all(send, ("x", "y"), 0, 0, tiled=True)
-    lpan = call(panels_kernel, f32(SLOTS * W, 2 * W), 5, flops=5 * 10**8, moved=4 * 2**20)(
-        meta, own, oth, low1, inv0, row_perms
+    lpan = call(panels_kernel, f32(SLOTS * W, 2 * W), 6, flops=5 * 10**8, moved=4 * 2**20)(
+        meta, own, oth, plow, inv0, inv1, row_perms
     )
     got1, lpan = lax.optimization_barrier((got1, lpan))
     oth1 = lax.ppermute(got1[:, :H], "core", [(0, 1), (1, 0)])
     cur, kept = call(
         first_kernel, (f32(SLOTS * W, 2 * W), f32(W, 2 * W)), 5, flops=5 * 10**8, moved=3 * 2**20
     )(meta, a, got1, plow, lsrc, row_perms)
-    schur = call(
-        second_kernel,
-        f32(SLOTS * W, 2 * W),
-        4,
-        scratch=(pltpu.VMEM((SLOTS * W, W), jnp.float32),),
-        flops=5 * 10**8,
-        moved=3 * 2**20,
-    )(meta, cur, got1, oth1, kept)
+    schur = call(second_kernel, f32(SLOTS * W, 2 * W), 3, flops=3 * 10**8, moved=3 * 2**20)(
+        meta, cur, oth1, kept
+    )
     return schur, lpan
 
 

time: 114 us -> 116 us (1.018)
  starting transfers between devices: 41.6 us -> 45.6 us
    ppermute x1, starting transfers between devices: 10.7 us -> 13 us  [shards(): oth = lax.ppermute(own, 'core', [(0, 1), (1, 0)])]
    ppermute x9, starting transfers between devices: 14.5 us -> 16.2 us  [the longest x8 14.8 us: shards(): got.append(lax.ppermute(piece, ('z', 'core'), pairs))]
    all_to_all x1, waiting for transfers between devices: 7.07 us -> 5.37 us  [shards(): got0 = lax.all_to_all(out0, ('x', 'y'), 0, 0, tiled=True)]
    unnamed x16 -> x14, local copies, waits for them, and re-layouts: 3.72 us -> 2.75 us
  transfers between devices with their start and end apart: 14 -> 14, of which waited for: 6 -> 6; matrix products, arithmetic and copies ran while one was open for 0% -> 0% of each run, Pallas kernels for 5% -> 6%
where the time goes in v9:
time: 116 us; the launch traced here: 115 us
  starting transfers between devices  45.6 us (39%)
  waiting for transfers between devices  25.3 us (22%)
  blocking collectives  25.2 us (22%)
  Pallas kernels  13.5 us (12%)
  local copies, waits for them, and re-layouts  3.86 us (3%)
  other arithmetic  1.17 us (1%)
    all_gather x1, blocking collectives, shards(): own = lax.all_gather(payload, 'z', axis=0, tiled=False)  25.2 us
    ppermute x8, starting transfers between devices, shards(): got.append(lax.ppermute(piece, ('z', 'core'), pairs))  14.8 us
    ppermute x1, starting transfers between devices, shards(): oth = lax.ppermute(own, 'core', [(0, 1), (1, 0)])  13 us
    ppermute x1, waiting for transfers between devices, shards(): lax.ppermute(cut[:, 9:].transpose(1, 0, 2, 3), ('z', 'core'), [(0, 1)])  8.16 us
    all_to_all x1, waiting for transfers between devices, shards(): got1 = lax.all_to_all(send, ('x', 'y'), 0, 0, tiled=True)  8.01 us
    all_to_all x1, starting transfers between devices, shards(): got0 = lax.all_to_all(out0, ('x', 'y'), 0, 0, tiled=True)  6.75 us
    all_to_all x1, waiting for transfers between devices, shards(): got0 = lax.all_to_all(out0, ('x', 'y'), 0, 0, tiled=True)  5.37 us
    ppermute x1, starting transfers between devices, shards(): oth1 = lax.ppermute(got1[:, :H], 'core', [(0, 1), (1, 0)])  4.67 us
  transfers between devices with their start and end apart: 14, of which 6 were waited for; matrix products, arithmetic and copies ran while one was open for 0% of the time, Pallas kernels for 6%

profile of v9, /device:TPU:1, one launch (start us, length us, event | category | flops | bytes accessed | tf_op | source)
XLA Modules:
  0.0 115.5 jit_solution(14143617786843375356)
XLA Ops:
  0.6 1.1 copy_bitcast_fusion
  1.7 0.0 copy-start
  1.7 1.4 %collective-permute-start = (f32[7,8,8,256]{3,2,1,0:T(8,128)S(1)}, f32[7,8,8,256]{3,2,1,0:T(8,128)S(1)}, u32[]{:S(2)}, u32[]{:S(2)}) collective-permute-start(f32[7,8,8,256]{3,2,1,0:T(8,128)S(1)} %copy_bitcast_fusion), channel_id=1, source_target_pairs={{0,1},{32,33},{64,65},{96,97},{128,129},{160,161},{192,193},{224,2... | collective-permute-start | bytes 1376264 | tf_op jit(solution)/shard_map/ppermute | solution.py:270
  3.1 8.2 %collective-permute-done = f32[7,8,8,256]{3,2,1,0:T(8,128)S(1)} collective-permute-done((f32[7,8,8,256]{3,2,1,0:T(8,128)S(1)}, f32[7,8,8,256]{3,2,1,0:T(8,128)S(1)}, u32[]{:S(2)}, u32[]{:S(2)}) %collective-permute-start) | collective-permute-done | bytes 458784 | tf_op jit(solution)/shard_map/ppermute | solution.py:270
  11.3 1.2 %fusion = (f32[8,8,256]{2,1,0:T(8,128)S(1)}, f32[8,8,256]{2,1,0:T(8,128)S(1)}, f32[8,8,256]{2,1,0:T(8,128)S(1)}, f32[8,8,256]{2,1,0:T(8,128)S(1)}, f32[8,8,256]{...) fusion(f32[8,16,8,256]{3,2,1,0:T(8,128)} %bitcast.94, ...), kind=kLoop, calls=%fused_computation.2 | loop fusion | flops 147456 | bytes 1638401 | tf_op jit(solution)/shard_map/jit(_where)/select_n | solution.py:272
  12.5 0.0 copy-start.6
  12.5 3.8 %collective-permute-start.1 = (f32[8,8,256]{2,1,0:T(8,128)S(1)}, f32[8,8,256]{2,1,0:T(8,128)S(1)}, u32[]{:S(2)}, u32[]{:S(2)}) collective-permute-start(f32[8,8,256]{2,1,0:T(8,128)S(1)} %get-tuple-element.30), channel_id=1, source_target_pairs={{1,30},{0,2},{33,62},{32,34},{65,94},{64,66},{97,126},{96,98},{129... | collective-permute-start | bytes 196616 | tf_op jit(solution)/shard_map/ppermute | solution.py:277
  16.3 1.3 %collective-permute-start.2 = (f32[8,8,256]{2,1,0:T(8,128)S(1)}, f32[8,8,256]{2,1,0:T(8,128)S(1)}, u32[]{:S(2)}, u32[]{:S(2)}) collective-permute-start(f32[8,8,256]{2,1,0:T(8,128)S(1)} %get-tuple-element.31), channel_id=1, source_target_pairs={{1,28},{0,4},{33,60},{32,36},{65,92},{64,68},{97,124},{96,100},{12... | collective-permute-start | bytes 196616 | tf_op jit(solution)/shard_map/ppermute | solution.py:277
  17.6 3.9 %collective-permute-start.3 = (f32[8,8,256]{2,1,0:T(8,128)S(1)}, f32[8,8,256]{2,1,0:T(8,128)S(1)}, u32[]{:S(2)}, u32[]{:S(2)}) collective-permute-start(f32[8,8,256]{2,1,0:T(8,128)S(1)} %get-tuple-element.32), channel_id=1, source_target_pairs={{1,18},{0,14},{33,50},{32,46},{65,82},{64,78},{97,114},{96,110},{1... | collective-permute-start | bytes 196616 | tf_op jit(solution)/shard_map/ppermute | solution.py:277
  21.5 1.3 %collective-permute-start.4 = (f32[8,8,256]{2,1,0:T(8,128)S(1)}, f32[8,8,256]{2,1,0:T(8,128)S(1)}, u32[]{:S(2)}, u32[]{:S(2)}) collective-permute-start(f32[8,8,256]{2,1,0:T(8,128)S(1)} %get-tuple-element.33), channel_id=1, source_target_pairs={{1,20},{0,16},{33,52},{32,48},{65,84},{64,80},{97,116},{96,112},{1... | collective-permute-start | bytes 196616 | tf_op jit(solution)/shard_map/ppermute | solution.py:277
  22.8 1.3 %collective-permute-start.5 = (f32[8,8,256]{2,1,0:T(8,128)S(1)}, f32[8,8,256]{2,1,0:T(8,128)S(1)}, u32[]{:S(2)}, u32[]{:S(2)}) collective-permute-start(f32[8,8,256]{2,1,0:T(8,128)S(1)} %get-tuple-element.34), channel_id=1, source_target_pairs={{1,22},{0,12},{33,54},{32,44},{65,86},{64,76},{97,118},{96,108},{1... | collective-permute-start | bytes 196616 | tf_op jit(solution)/shard_map/ppermute | solution.py:277
  24.1 0.0 collective-permute-done.1.refs_0_
  24.1 1.3 %collective-permute-start.6 = (f32[8,8,256]{2,1,0:T(8,128)S(1)}, f32[8,8,256]{2,1,0:T(8,128)S(1)}, u32[]{:S(2)}, u32[]{:S(2)}) collective-permute-start(f32[8,8,256]{2,1,0:T(8,128)S(1)} %get-tuple-element.35), channel_id=1, source_target_pairs={{1,24},{0,10},{33,56},{32,42},{65,88},{64,74},{97,120},{96,106},{1... | collective-permute-start | bytes 196616 | tf_op jit(solution)/shard_map/ppermute | solution.py:277
  25.4 0.0 collective-permute-done.2.refs_1_
  25.4 1.3 %collective-permute-start.7 = (f32[8,8,256]{2,1,0:T(8,128)S(1)}, f32[8,8,256]{2,1,0:T(8,128)S(1)}, u32[]{:S(2)}, u32[]{:S(2)}) collective-permute-start(f32[8,8,256]{2,1,0:T(8,128)S(1)} %get-tuple-element.36), channel_id=1, source_target_pairs={{1,26},{0,8},{33,58},{32,40},{65,90},{64,72},{97,122},{96,104},{12... | collective-permute-start | bytes 196616 | tf_op jit(solution)/shard_map/ppermute | solution.py:277
  26.7 0.0 collective-permute-done.3.refs_2_
  26.7 0.7 collective-permute-start.8
  27.4 0.0 copy-done
  27.4 0.0 collective-permute-done.4.refs_3_
  27.4 0.0 collective-permute-done.5.refs_4_
  27.5 0.0 collective-permute-done.6.refs_5_
  27.5 0.6 collective-permute-done.7.refs_6_
  28.0 0.0 collective-permute-done.8.refs_7_
  28.0 0.0 copy-done.6
  28.0 1.4 %shard_map.68 = (f32[16,9,8,128]{3,2,1,0:T(8,128)}, f32[14,8,128]{2,1,0:T(8,128)S(1)}, f32[2,8,128]{2,1,0:T(8,128)S(1)}) custom-call(s32[2,128]{1,0:T(2,128)S(1)} %copy-done.6, f32[256,256]{1,0:T(8,128)S(1)} %slice.59.a, f32[8,8,256]{2,1,0:T(8,128)S(1)} %get-tuple-element.29.own, f32[8,8,256]{2,1,0:T(8,128)S(1)} %collective-permute-done.1.refs_0_, ...), custom_call_target="tpu_custom_call" | custom-call | bytes 1048576 | tf_op jit(solution)/shard_map/pallas_call | solution.py:279
  29.5 6.8 %all-to-all-start = ((f32[16,9,8,128]{3,2,1,0:T(8,128)}), f32[16,9,8,128]{3,2,1,0:T(8,128)S(1)}, u32[]{:S(2)}, u32[]{:S(2)}) async-start(f32[16,9,8,128]{3,2,1,0:T(8,128)} %get-tuple-element.44), calls=%async_computation | async-start | bytes 1179648 | tf_op jit(solution)/shard_map/all_to_all | solution.py:291
  36.2 1.3 %collective-permute-start.9 = (f32[14,8,128]{2,1,0:T(8,128)S(1)}, f32[14,8,128]{2,1,0:T(8,128)S(1)}, u32[]{:S(2)}, u32[]{:S(2)}) collective-permute-start(f32[14,8,128]{2,1,0:T(8,128)S(1)} %get-tuple-element.42), channel_id=1, source_target_pairs={{0,1},{2,3},{4,5},{6,7},{8,9},{10,11},{12,13},{14,15},{16,17},{18,... | collective-permute-start | bytes 172040 | tf_op jit(solution)/shard_map/ppermute | solution.py:283
  37.5 2.0 %shard_map.69.meta = s32[128]{0:T(128)} custom-call(s32[2,128]{1,0:T(2,128)} %dest.2, s32[2,128]{1,0:T(2,128)} %row_mask, s32[2,64]{1,0:T(2,128)} %col_mask), custom_call_target="tpu_custom_call" | custom-call | tf_op jit(solution)/shard_map/pallas_call | solution.py:284
  39.5 0.0 copy-start.4
  39.5 1.1 collective-permute-done.9.passed
  40.6 5.4 %all-to-all-done.got = f32[16,9,8,128]{3,2,1,0:T(8,128)S(1)} async-done(((f32[16,9,8,128]{3,2,1,0:T(8,128)}), f32[16,9,8,128]{3,2,1,0:T(8,128)S(1)}, u32[]{:S(2)}, u32[]{:S(2)}) %all-to-all-start) | async-done | bytes 589856 | tf_op jit(solution)/shard_map/all_to_all | solution.py:291
  46.0 0.6 shard_map.70
  46.6 25.2 %all-gather = f32[224,8,128]{2,1,0:T(8,128)S(1)} all-gather(f32[14,8,128]{2,1,0:T(8,128)S(1)} %get-tuple-element.45), channel_id=2, replica_groups=mesh['x'=4,'y'=4,'z'=16,'core'=2] {'z'}, dimensions={0}, use_global_device_ids=true | all-gather | bytes 974848 | tf_op jit(solution)/shard_map/all_gather | solution.py:296
  71.7 13.0 %collective-permute-start.10 = (f32[16,14,8,128]{3,2,1,0:T(8,128)S(1)}, f32[16,14,8,128]{3,2,1,0:T(8,128)S(1)}, u32[]{:S(2)}, u32[]{:S(2)}) collective-permute-start(f32[16,14,8,128]{3,2,1,0:T(8,128)S(1)} %bitcast.90), channel_id=1, source_target_pairs={{0,1},{1,0},{2,3},{3,2},{4,5},{5,4},{6,7},{7,6},{8,9},{9,8},{10,11... | collective-permute-start | bytes 2752520 | tf_op jit(solution)/shard_map/ppermute | solution.py:297
  84.7 2.1 %collective-permute-done.10.oth = f32[16,14,8,128]{3,2,1,0:T(8,128)S(1)} collective-permute-done((f32[16,14,8,128]{3,2,1,0:T(8,128)S(1)}, f32[16,14,8,128]{3,2,1,0:T(8,128)S(1)}, u32[]{:S(2)}, u32[]{:S(2)}) %collective-permute-start.10) | collective-permute-done | bytes 917536 | tf_op jit(solution)/shard_map/ppermute | solution.py:297
  86.8 3.1 %shard_map.71 = (f32[16,96,128]{2,1,0:T(8,128)S(1)}, f32[1024,128]{1,0:T(8,128)S(1)}, f32[128,128]{1,0:T(8,128)S(1)}, f32[128,128]{1,0:T(8,128)S(1)}, f32[128,128]{1,0:T(8,128)S(1)}) custom-call(s32[128]{0:T(128)S(1)} %copy-done.4, f32[16,14,8,128]{3,2,1,0:T(8,128)S(1)} %bitcast.91, f32[16,14,8,128]{3,2,1,0:T(8,128)S(1)} %collective-permute-done.10.oth, ...), custom_call_target="tpu_custom_call" | custom-call | flops 500000000 | bytes 4194304 | tf_op jit(solution)/shard_map/pallas_call | solution.py:299
  90.0 0.0 copy-start.3
  90.0 0.9 copy-done.3
  90.9 3.6 %all-to-all-start.1 = ((f32[16,96,128]{2,1,0:T(8,128)}), f32[16,96,128]{2,1,0:T(8,128)S(1)}, u32[]{:S(2)}, u32[]{:S(2)}) async-start(f32[16,96,128]{2,1,0:T(8,128)} %copy-done.3), calls=%async_computation.1 | async-start | bytes 1572864 | tf_op jit(solution)/shard_map/all_to_all | solution.py:308
  94.5 0.0 copy-start.5
  94.5 0.7 copy-done.5
  95.2 1.2 %copy-done.2 = f32[16,14,8,128]{3,2,1,0:T(8,128)S(1)} copy-done((f32[16,14,8,128]{3,2,1,0:T(8,128)S(1)}, f32[16,14,8,128]{3,2,1,0:T(8,128)}, u32[]{:S(2)}) %copy-start.2) | copy-done | bytes 917528
  96.3 2.9 %shard_map.72 = f32[1024,256]{1,0:T(8,128)} custom-call(s32[128]{0:T(128)S(1)} %copy-done.4, f32[16,14,8,128]{3,2,1,0:T(8,128)S(1)} %bitcast.92, f32[16,14,8,128]{3,2,1,0:T(8,128)S(1)} %copy-done.2, f32[1024,128]{1,0:T(8,128)S(1)} %get-tuple-element.48.plow, f32[128,128]{1,0:T(8,128)S(1)} %get-tuple-element.49.inv0, f32[128,128]{1,0:T(8,128)S(1)} %get-tuple-element.50.inv1, ...), custom_call_target="tpu_custom_call" | custom-call | flops 500000000 | bytes 4194304 | tf_op jit(solution)/shard_map/pallas_call | solution.py:309
  99.2 8.0 %all-to-all-done.1.got = f32[16,96,128]{2,1,0:T(8,128)S(1)} async-done(((f32[16,96,128]{2,1,0:T(8,128)}), f32[16,96,128]{2,1,0:T(8,128)S(1)}, u32[]{:S(2)}, u32[]{:S(2)}) %all-to-all-start.1) | async-done | bytes 786464 | tf_op jit(solution)/shard_map/all_to_all | solution.py:308
  107.3 4.7 %collective-permute-start.11 = (f32[16,64,128]{2,1,0:T(8,128)S(1)}, f32[16,64,128]{2,1,0:T(8,128)S(1)}, u32[]{:S(2)}, u32[]{:S(2)}) collective-permute-start(f32[16,64,128]{2,1,0:T(8,128)S(1)} %slice.77), channel_id=1, source_target_pairs={{0,1},{1,0},{2,3},{3,2},{4,5},{5,4},{6,7},{7,6},{8,9},{9,8},{10,11... | collective-permute-start | bytes 1572872 | tf_op jit(solution)/shard_map/ppermute | solution.py:313
  112.0 1.7 %shard_map.73 = (f32[1024,256]{1,0:T(8,128)S(1)}, f32[128,256]{1,0:T(8,128)S(1)}) custom-call(s32[128]{0:T(128)S(1)} %copy-done.4, f32[1024,256]{1,0:T(8,128)S(1)} %copy-done, f32[16,96,128]{2,1,0:T(8,128)S(1)} %all-to-all-done.1.got, f32[1024,128]{1,0:T(8,128)S(1)} %get-tuple-element.48.plow, f32[128,128]{1,0:T(8,128)S(1)} %get-tuple-element.52.lsrc, ...), custom_call_target="tpu_custom_call" | custom-call | flops 500000000 | bytes 3145728 | tf_op jit(solution)/shard_map/pallas_call | solution.py:314
  113.6 0.0 collective-permute-done.11.oth
  113.6 1.8 %shard_map.74 = f32[1024,256]{1,0:T(8,128)} custom-call(s32[128]{0:T(128)S(1)} %copy-done.4, f32[1024,256]{1,0:T(8,128)S(1)} %get-tuple-element.53.cur, f32[16,64,128]{2,1,0:T(8,128)S(1)} %collective-permute-done.11.oth, f32[128,256]{1,0:T(8,128)S(1)} %get-tuple-element.54.kept), custom_call_target="tpu_custom_call" | custom-call | flops 300000000 | bytes 3145728 | tf_op jit(solution)/shard_map/pallas_call | solution.py:317
  (6 shorter events, 0.1 us)
Async XLA Ops:
  1.7 25.7 %copy-start = (f32[1024,256]{1,0:T(8,128)S(1)}, f32[1024,256]{1,0:T(8,128)}, u32[]{:S(2)}) copy-start(f32[1024,256]{1,0:T(8,128)} %a.1) | copy-start | bytes 3145732
  1.7 9.6 %collective-permute-start = (f32[7,8,8,256]{3,2,1,0:T(8,128)S(1)}, f32[7,8,8,256]{3,2,1,0:T(8,128)S(1)}, u32[]{:S(2)}, u32[]{:S(2)}) collective-permute-start(f32[7,8,8,256]{3,2,1,0:T(8,128)S(1)} %copy_bitcast_fusion), channel_id=1, source_target_pairs={{0,1},{32,33},{64,65},{96,97},{128,129},{160,161},{192,193},{224,2... | collective-permute-start | bytes 1376264 | tf_op jit(solution)/shard_map/ppermute | solution.py:270
  12.5 15.6 %copy-start.6 = (s32[2,128]{1,0:T(2,128)S(1)}, s32[2,128]{1,0:T(2,128)}, u32[]{:S(2)}) copy-start(s32[2,128]{1,0:T(2,128)} %dest.2) | copy-start | bytes 3076
  12.5 11.6 %collective-permute-start.1 = (f32[8,8,256]{2,1,0:T(8,128)S(1)}, f32[8,8,256]{2,1,0:T(8,128)S(1)}, u32[]{:S(2)}, u32[]{:S(2)}) collective-permute-start(f32[8,8,256]{2,1,0:T(8,128)S(1)} %get-tuple-element.30), channel_id=1, source_target_pairs={{1,30},{0,2},{33,62},{32,34},{65,94},{64,66},{97,126},{96,98},{129... | collective-permute-start | bytes 196616 | tf_op jit(solution)/shard_map/ppermute | solution.py:277
  16.3 9.1 %collective-permute-start.2 = (f32[8,8,256]{2,1,0:T(8,128)S(1)}, f32[8,8,256]{2,1,0:T(8,128)S(1)}, u32[]{:S(2)}, u32[]{:S(2)}) collective-permute-start(f32[8,8,256]{2,1,0:T(8,128)S(1)} %get-tuple-element.31), channel_id=1, source_target_pairs={{1,28},{0,4},{33,60},{32,36},{65,92},{64,68},{97,124},{96,100},{12... | collective-permute-start | bytes 196616 | tf_op jit(solution)/shard_map/ppermute | solution.py:277
  17.6 9.1 %collective-permute-start.3 = (f32[8,8,256]{2,1,0:T(8,128)S(1)}, f32[8,8,256]{2,1,0:T(8,128)S(1)}, u32[]{:S(2)}, u32[]{:S(2)}) collective-permute-start(f32[8,8,256]{2,1,0:T(8,128)S(1)} %get-tuple-element.32), channel_id=1, source_target_pairs={{1,18},{0,14},{33,50},{32,46},{65,82},{64,78},{97,114},{96,110},{1... | collective-permute-start | bytes 196616 | tf_op jit(solution)/shard_map/ppermute | solution.py:277
  21.5 5.9 %collective-permute-start.4 = (f32[8,8,256]{2,1,0:T(8,128)S(1)}, f32[8,8,256]{2,1,0:T(8,128)S(1)}, u32[]{:S(2)}, u32[]{:S(2)}) collective-permute-start(f32[8,8,256]{2,1,0:T(8,128)S(1)} %get-tuple-element.33), channel_id=1, source_target_pairs={{1,20},{0,16},{33,52},{32,48},{65,84},{64,80},{97,116},{96,112},{1... | collective-permute-start | bytes 196616 | tf_op jit(solution)/shard_map/ppermute | solution.py:277
  22.8 4.7 %collective-permute-start.5 = (f32[8,8,256]{2,1,0:T(8,128)S(1)}, f32[8,8,256]{2,1,0:T(8,128)S(1)}, u32[]{:S(2)}, u32[]{:S(2)}) collective-permute-start(f32[8,8,256]{2,1,0:T(8,128)S(1)} %get-tuple-element.34), channel_id=1, source_target_pairs={{1,22},{0,12},{33,54},{32,44},{65,86},{64,76},{97,118},{96,108},{1... | collective-permute-start | bytes 196616 | tf_op jit(solution)/shard_map/ppermute | solution.py:277
  24.1 3.4 %collective-permute-start.6 = (f32[8,8,256]{2,1,0:T(8,128)S(1)}, f32[8,8,256]{2,1,0:T(8,128)S(1)}, u32[]{:S(2)}, u32[]{:S(2)}) collective-permute-start(f32[8,8,256]{2,1,0:T(8,128)S(1)} %get-tuple-element.35), channel_id=1, source_target_pairs={{1,24},{0,10},{33,56},{32,42},{65,88},{64,74},{97,120},{96,106},{1... | collective-permute-start | bytes 196616 | tf_op jit(solution)/shard_map/ppermute | solution.py:277
  25.4 2.6 %collective-permute-start.7 = (f32[8,8,256]{2,1,0:T(8,128)S(1)}, f32[8,8,256]{2,1,0:T(8,128)S(1)}, u32[]{:S(2)}, u32[]{:S(2)}) collective-permute-start(f32[8,8,256]{2,1,0:T(8,128)S(1)} %get-tuple-element.36), channel_id=1, source_target_pairs={{1,26},{0,8},{33,58},{32,40},{65,90},{64,72},{97,122},{96,104},{12... | collective-permute-start | bytes 196616 | tf_op jit(solution)/shard_map/ppermute | solution.py:277
  26.7 1.3 %collective-permute-start.8 = (f32[8,8,256]{2,1,0:T(8,128)S(1)}, f32[8,8,256]{2,1,0:T(8,128)S(1)}, u32[]{:S(2)}, u32[]{:S(2)}) collective-permute-start(f32[8,8,256]{2,1,0:T(8,128)S(1)} %get-tuple-element.37), channel_id=1, source_target_pairs={{0,6},{32,38},{64,70},{96,102},{128,134},{160,166},{192,198},{224,... | collective-permute-start | bytes 196616 | tf_op jit(solution)/shard_map/ppermute | solution.py:277
  29.5 16.5 %all-to-all-start = ((f32[16,9,8,128]{3,2,1,0:T(8,128)}), f32[16,9,8,128]{3,2,1,0:T(8,128)S(1)}, u32[]{:S(2)}, u32[]{:S(2)}) async-start(f32[16,9,8,128]{3,2,1,0:T(8,128)} %get-tuple-element.44), calls=%async_computation | async-start | bytes 1179648 | tf_op jit(solution)/shard_map/all_to_all | solution.py:291
  36.2 4.4 %collective-permute-start.9 = (f32[14,8,128]{2,1,0:T(8,128)S(1)}, f32[14,8,128]{2,1,0:T(8,128)S(1)}, u32[]{:S(2)}, u32[]{:S(2)}) collective-permute-start(f32[14,8,128]{2,1,0:T(8,128)S(1)} %get-tuple-element.42), channel_id=1, source_target_pairs={{0,1},{2,3},{4,5},{6,7},{8,9},{10,11},{12,13},{14,15},{16,17},{18,... | collective-permute-start | bytes 172040 | tf_op jit(solution)/shard_map/ppermute | solution.py:283
  39.5 6.5 %copy-start.4 = (s32[128]{0:T(128)S(1)}, s32[128]{0:T(128)}, u32[]{:S(2)}) copy-start(s32[128]{0:T(128)} %shard_map.69.meta) | copy-start | bytes 1540
  71.7 15.1 %collective-permute-start.10 = (f32[16,14,8,128]{3,2,1,0:T(8,128)S(1)}, f32[16,14,8,128]{3,2,1,0:T(8,128)S(1)}, u32[]{:S(2)}, u32[]{:S(2)}) collective-permute-start(f32[16,14,8,128]{3,2,1,0:T(8,128)S(1)} %bitcast.90), channel_id=1, source_target_pairs={{0,1},{1,0},{2,3},{3,2},{4,5},{5,4},{6,7},{7,6},{8,9},{9,8},{10,11... | collective-permute-start | bytes 2752520 | tf_op jit(solution)/shard_map/ppermute | solution.py:297
  86.8 3.1 %copy-start.1 = (f32[16,14,8,128]{3,2,1,0:T(8,128)}, f32[16,14,8,128]{3,2,1,0:T(8,128)S(1)}, u32[]{:S(2)}) copy-start(f32[16,14,8,128]{3,2,1,0:T(8,128)S(1)} %collective-permute-done.10.oth) | copy-start | bytes 2752516
  90.0 0.9 copy-start.3
  90.9 16.4 %all-to-all-start.1 = ((f32[16,96,128]{2,1,0:T(8,128)}), f32[16,96,128]{2,1,0:T(8,128)S(1)}, u32[]{:S(2)}, u32[]{:S(2)}) async-start(f32[16,96,128]{2,1,0:T(8,128)} %copy-done.3), calls=%async_computation.1 | async-start | bytes 1572864 | tf_op jit(solution)/shard_map/all_to_all | solution.py:308
  94.5 0.7 copy-start.5
  95.2 1.2 %copy-start.2 = (f32[16,14,8,128]{3,2,1,0:T(8,128)S(1)}, f32[16,14,8,128]{3,2,1,0:T(8,128)}, u32[]{:S(2)}) copy-start(f32[16,14,8,128]{3,2,1,0:T(8,128)} %copy-done.1) | copy-start | bytes 2752516
  107.3 6.3 %collective-permute-start.11 = (f32[16,64,128]{2,1,0:T(8,128)S(1)}, f32[16,64,128]{2,1,0:T(8,128)S(1)}, u32[]{:S(2)}, u32[]{:S(2)}) collective-permute-start(f32[16,64,128]{2,1,0:T(8,128)S(1)} %slice.77), channel_id=1, source_target_pairs={{0,1},{1,0},{2,3},{3,2},{4,5},{5,4},{6,7},{7,6},{8,9},{9,8},{10,11... | collective-permute-start | bytes 1572872 | tf_op jit(solution)/shard_map/ppermute | solution.py:313

commit v10 on v9

--- a/solution.py
+++ b/solution.py
@@ -12,7 +12,6 @@
 NP = 16
 NZ = 16
 SLOTS = 8
-SENDS = ((1, 15), (2, 14), (7, 9), (8, 10), (6, 11), (5, 12), (4, 13), (3, 0))
 
 
 def dot16(a, b):
@@ -267,18 +266,19 @@
     core = lax.axis_index("core")
     smem = pl.BlockSpec(memory_space=pltpu.SMEM)
     cut = a.reshape(SLOTS, NZ, 8, 2 * W)
-    over = lax.ppermute(cut[:, 9:].transpose(1, 0, 2, 3), ("z", "core"), [(0, 1)])
-    *pieces, own0 = lax.optimization_barrier(
-        [jnp.where(core == 0, cut[:, z0], over[max(z1 - 9, 0)]) for z0, z1 in (*SENDS, (0, 0))]
-    )
+    over = lax.ppermute(cut[:, 8:].transpose(1, 0, 2, 3), ("z", "core"), [(0, 1)])
+    pieces = [jnp.where(core == 0, cut[:, step % 8], over[8 - step]) for step in range(1, 9)]
+    pieces = lax.optimization_barrier(pieces)
     got = []
-    for (z0, z1), piece in zip(SENDS, pieces):
-        pairs = ([(1, 2 * z1)] if z1 else []) + [(0, 2 * z0)]
-        got.append(lax.ppermute(piece, ("z", "core"), pairs))
+    for step in range(1, 9):
+        pairs = [(1, 2 * (NZ - step))]
+        if step < 8:
+            pairs.append((0, 2 * step))
+        got.append(lax.ppermute(pieces[step - 1], ("z", "core"), pairs))
 
     out0, panel, last = call(
         route_kernel, (f32(NP, 9, 8, W), f32(14, 8, W), f32(2, 8, W)), 10, moved=2**20
-    )(dest_rows, a[: 2 * W], own0, *got)
+    )(dest_rows, a[: 2 * W], pieces[7], *got)
     out0, maps = lax.optimization_barrier((out0, (dest_rows, row_mask, col_mask)))
     passed = lax.ppermute(panel, "core", [(0, 1)])
     meta = pl.pallas_call(

time: 116 us -> 113 us (0.974)
  starting transfers between devices: 45.6 us -> 41.6 us
  waiting for transfers between devices: 25.3 us -> 26.6 us
    ppermute x1, starting transfers between devices: 13 us -> 10.7 us  [shards(): oth = lax.ppermute(own, 'core', [(0, 1), (1, 0)])]
    ppermute x9, starting transfers between devices: 16.2 us -> 14.5 us  [the longest x8 13.2 us: shards(): got.append(lax.ppermute(pieces[step - 1], ('z', 'core'), pairs))]
    all_to_all x1, waiting for transfers between devices: 5.37 us -> 7.07 us  [shards(): got0 = lax.all_to_all(out0, ('x', 'y'), 0, 0, tiled=True)]
  transfers between devices with their start and end apart: 14 -> 14, of which waited for: 6 -> 5; matrix products, arithmetic and copies ran while one was open for 0% -> 0% of each run, Pallas kernels for 6% -> 6%
where the time goes in v10:
time: 113 us; the launch traced here: 112 us
  starting transfers between devices  41.6 us (37%)
  waiting for transfers between devices  26.6 us (24%)
  blocking collectives  25.3 us (22%)
  Pallas kernels  13.5 us (12%)
  local copies, waits for them, and re-layouts  3.97 us (4%)
    all_gather x1, blocking collectives, shards(): own = lax.all_gather(payload, 'z', axis=0, tiled=False)  25.3 us
    ppermute x8, starting transfers between devices, shards(): got.append(lax.ppermute(pieces[step - 1], ('z', 'core'), pairs))  13.2 us
    ppermute x1, starting transfers between devices, shards(): oth = lax.ppermute(own, 'core', [(0, 1), (1, 0)])  10.7 us
    ppermute x1, waiting for transfers between devices, shards(): lax.ppermute(cut[:, 8:].transpose(1, 0, 2, 3), ('z', 'core'), [(0, 1)])  8.25 us
    all_to_all x1, waiting for transfers between devices, shards(): got1 = lax.all_to_all(send, ('x', 'y'), 0, 0, tiled=True)  7.98 us
    all_to_all x1, waiting for transfers between devices, shards(): got0 = lax.all_to_all(out0, ('x', 'y'), 0, 0, tiled=True)  7.07 us
    all_to_all x1, starting transfers between devices, shards(): got0 = lax.all_to_all(out0, ('x', 'y'), 0, 0, tiled=True)  6.75 us
    ppermute x1, starting transfers between devices, shards(): oth1 = lax.ppermute(got1[:, :H], 'core', [(0, 1), (1, 0)])  4.69 us
  transfers between devices with their start and end apart: 14, of which 5 were waited for; matrix products, arithmetic and copies ran while one was open for 0% of the time, Pallas kernels for 6%

profile of v10, /device:TPU:1, one launch (start us, length us, event | category | flops | bytes accessed | tf_op | source)
XLA Modules:
  0.0 112.0 jit_solution(18248829570096529258)
XLA Ops:
  0.6 0.0 copy-start
  0.6 1.2 %copy_bitcast_fusion = f32[8,8,8,256]{3,2,1,0:T(8,128)S(1)} fusion(f32[8,16,8,256]{3,2,1,0:T(8,128)} %bitcast.87), kind=kLoop, calls=%fused_computation | loop fusion | bytes 1048576 | tf_op jit(solution)/shard_map/transpose | solution.py:269
  1.8 1.3 %collective-permute-start = (f32[8,8,8,256]{3,2,1,0:T(8,128)S(1)}, f32[8,8,8,256]{3,2,1,0:T(8,128)S(1)}, u32[]{:S(2)}, u32[]{:S(2)}) collective-permute-start(f32[8,8,8,256]{3,2,1,0:T(8,128)S(1)} %copy_bitcast_fusion), channel_id=1, source_target_pairs={{0,1},{32,33},{64,65},{96,97},{128,129},{160,161},{192,193},{224,2... | collective-permute-start | bytes 1572872 | tf_op jit(solution)/shard_map/ppermute | solution.py:269
  3.1 8.3 %collective-permute-done = f32[8,8,8,256]{3,2,1,0:T(8,128)S(1)} collective-permute-done((f32[8,8,8,256]{3,2,1,0:T(8,128)S(1)}, f32[8,8,8,256]{3,2,1,0:T(8,128)S(1)}, u32[]{:S(2)}, u32[]{:S(2)}) %collective-permute-start) | collective-permute-done | bytes 524320 | tf_op jit(solution)/shard_map/ppermute | solution.py:269
  11.4 0.1 fusion
  11.5 0.0 copy-start.6
  11.5 3.7 %collective-permute-start.1 = (f32[8,8,256]{2,1,0:T(8,128)S(1)}, f32[8,8,256]{2,1,0:T(8,128)S(1)}, u32[]{:S(2)}, u32[]{:S(2)}) collective-permute-start(f32[8,8,256]{2,1,0:T(8,128)S(1)} %get-tuple-element.29), channel_id=1, source_target_pairs={{1,30},{0,2},{33,62},{32,34},{65,94},{64,66},{97,126},{96,98},{129... | collective-permute-start | bytes 196616 | tf_op jit(solution)/shard_map/ppermute | solution.py:277
  15.2 1.3 %collective-permute-start.2 = (f32[8,8,256]{2,1,0:T(8,128)S(1)}, f32[8,8,256]{2,1,0:T(8,128)S(1)}, u32[]{:S(2)}, u32[]{:S(2)}) collective-permute-start(f32[8,8,256]{2,1,0:T(8,128)S(1)} %get-tuple-element.30), channel_id=1, source_target_pairs={{1,28},{0,4},{33,60},{32,36},{65,92},{64,68},{97,124},{96,100},{12... | collective-permute-start | bytes 196616 | tf_op jit(solution)/shard_map/ppermute | solution.py:277
  16.5 1.3 %collective-permute-start.3 = (f32[8,8,256]{2,1,0:T(8,128)S(1)}, f32[8,8,256]{2,1,0:T(8,128)S(1)}, u32[]{:S(2)}, u32[]{:S(2)}) collective-permute-start(f32[8,8,256]{2,1,0:T(8,128)S(1)} %get-tuple-element.31), channel_id=1, source_target_pairs={{1,26},{0,6},{33,58},{32,38},{65,90},{64,70},{97,122},{96,102},{12... | collective-permute-start | bytes 196616 | tf_op jit(solution)/shard_map/ppermute | solution.py:277
  17.8 1.3 %collective-permute-start.4 = (f32[8,8,256]{2,1,0:T(8,128)S(1)}, f32[8,8,256]{2,1,0:T(8,128)S(1)}, u32[]{:S(2)}, u32[]{:S(2)}) collective-permute-start(f32[8,8,256]{2,1,0:T(8,128)S(1)} %get-tuple-element.32), channel_id=1, source_target_pairs={{1,24},{0,8},{33,56},{32,40},{65,88},{64,72},{97,120},{96,104},{12... | collective-permute-start | bytes 196616 | tf_op jit(solution)/shard_map/ppermute | solution.py:277
  19.1 1.8 %collective-permute-start.5 = (f32[8,8,256]{2,1,0:T(8,128)S(1)}, f32[8,8,256]{2,1,0:T(8,128)S(1)}, u32[]{:S(2)}, u32[]{:S(2)}) collective-permute-start(f32[8,8,256]{2,1,0:T(8,128)S(1)} %get-tuple-element.33), channel_id=1, source_target_pairs={{1,22},{0,10},{33,54},{32,42},{65,86},{64,74},{97,118},{96,106},{1... | collective-permute-start | bytes 196616 | tf_op jit(solution)/shard_map/ppermute | solution.py:277
  20.8 0.0 collective-permute-done.1.refs_0_
  20.8 1.3 %collective-permute-start.6 = (f32[8,8,256]{2,1,0:T(8,128)S(1)}, f32[8,8,256]{2,1,0:T(8,128)S(1)}, u32[]{:S(2)}, u32[]{:S(2)}) collective-permute-start(f32[8,8,256]{2,1,0:T(8,128)S(1)} %get-tuple-element.34), channel_id=1, source_target_pairs={{1,20},{0,12},{33,52},{32,44},{65,84},{64,76},{97,116},{96,108},{1... | collective-permute-start | bytes 196616 | tf_op jit(solution)/shard_map/ppermute | solution.py:277
  22.1 0.0 collective-permute-done.2.refs_1_
  22.2 1.3 %collective-permute-start.7 = (f32[8,8,256]{2,1,0:T(8,128)S(1)}, f32[8,8,256]{2,1,0:T(8,128)S(1)}, u32[]{:S(2)}, u32[]{:S(2)}) collective-permute-start(f32[8,8,256]{2,1,0:T(8,128)S(1)} %get-tuple-element.35), channel_id=1, source_target_pairs={{1,18},{0,14},{33,50},{32,46},{65,82},{64,78},{97,114},{96,110},{1... | collective-permute-start | bytes 196616 | tf_op jit(solution)/shard_map/ppermute | solution.py:277
  23.5 0.0 collective-permute-done.3.refs_2_
  23.5 1.3 %collective-permute-start.8 = (f32[8,8,256]{2,1,0:T(8,128)S(1)}, f32[8,8,256]{2,1,0:T(8,128)S(1)}, u32[]{:S(2)}, u32[]{:S(2)}) collective-permute-start(f32[8,8,256]{2,1,0:T(8,128)S(1)} %get-tuple-element.28.own), channel_id=1, source_target_pairs={{1,16},{33,48},{65,80},{97,112},{129,144},{161,176},{193,208},{225... | collective-permute-start | bytes 196616 | tf_op jit(solution)/shard_map/ppermute | solution.py:277
  24.8 0.0 collective-permute-done.4.refs_3_
  24.8 0.0 collective-permute-done.5.refs_4_
  24.8 0.0 collective-permute-done.6.refs_5_
  24.8 0.0 collective-permute-done.7.refs_6_
  24.8 1.2 %collective-permute-done.8.refs_7_ = f32[8,8,256]{2,1,0:T(8,128)S(1)} collective-permute-done((f32[8,8,256]{2,1,0:T(8,128)S(1)}, f32[8,8,256]{2,1,0:T(8,128)S(1)}, u32[]{:S(2)}, u32[]{:S(2)}) %collective-permute-start.8) | collective-permute-done | bytes 65568 | tf_op jit(solution)/shard_map/ppermute | solution.py:277
  26.1 0.0 copy-done.6
  26.1 1.4 %shard_map.68 = (f32[16,9,8,128]{3,2,1,0:T(8,128)}, f32[14,8,128]{2,1,0:T(8,128)S(1)}, f32[2,8,128]{2,1,0:T(8,128)S(1)}) custom-call(s32[2,128]{1,0:T(2,128)S(1)} %copy-done.6, f32[256,256]{1,0:T(8,128)S(1)} %slice.57.a, f32[8,8,256]{2,1,0:T(8,128)S(1)} %get-tuple-element.28.own, f32[8,8,256]{2,1,0:T(8,128)S(1)} %collective-permute-done.1.refs_0_, ...), custom_call_target="tpu_custom_call" | custom-call | bytes 1048576 | tf_op jit(solution)/shard_map/pallas_call | solution.py:279
  27.5 6.8 %all-to-all-start = ((f32[16,9,8,128]{3,2,1,0:T(8,128)}), f32[16,9,8,128]{3,2,1,0:T(8,128)S(1)}, u32[]{:S(2)}, u32[]{:S(2)}) async-start(f32[16,9,8,128]{3,2,1,0:T(8,128)} %get-tuple-element.42), calls=%async_computation | async-start | bytes 1179648 | tf_op jit(solution)/shard_map/all_to_all | solution.py:291
  34.3 1.3 %collective-permute-start.9 = (f32[14,8,128]{2,1,0:T(8,128)S(1)}, f32[14,8,128]{2,1,0:T(8,128)S(1)}, u32[]{:S(2)}, u32[]{:S(2)}) collective-permute-start(f32[14,8,128]{2,1,0:T(8,128)S(1)} %get-tuple-element.40), channel_id=1, source_target_pairs={{0,1},{2,3},{4,5},{6,7},{8,9},{10,11},{12,13},{14,15},{16,17},{18,... | collective-permute-start | bytes 172040 | tf_op jit(solution)/shard_map/ppermute | solution.py:283
  35.6 2.0 %shard_map.69.meta = s32[128]{0:T(128)} custom-call(s32[2,128]{1,0:T(2,128)} %dest.2, s32[2,128]{1,0:T(2,128)} %row_mask, s32[2,64]{1,0:T(2,128)} %col_mask), custom_call_target="tpu_custom_call" | custom-call | tf_op jit(solution)/shard_map/pallas_call | solution.py:284
  37.6 0.0 copy-start.4
  37.6 0.0 collective-permute-done.9.passed
  37.6 7.1 %all-to-all-done.got = f32[16,9,8,128]{3,2,1,0:T(8,128)S(1)} async-done(((f32[16,9,8,128]{3,2,1,0:T(8,128)}), f32[16,9,8,128]{3,2,1,0:T(8,128)S(1)}, u32[]{:S(2)}, u32[]{:S(2)}) %all-to-all-start) | async-done | bytes 589856 | tf_op jit(solution)/shard_map/all_to_all | solution.py:291
  44.7 0.0 copy-done.4
  44.7 0.6 shard_map.70
  45.2 25.3 %all-gather = f32[224,8,128]{2,1,0:T(8,128)S(1)} all-gather(f32[14,8,128]{2,1,0:T(8,128)S(1)} %get-tuple-element.43), channel_id=2, replica_groups=mesh['x'=4,'y'=4,'z'=16,'core'=2] {'z'}, dimensions={0}, use_global_device_ids=true | all-gather | bytes 974848 | tf_op jit(solution)/shard_map/all_gather | solution.py:296
  70.6 10.7 %collective-permute-start.10 = (f32[16,14,8,128]{3,2,1,0:T(8,128)S(1)}, f32[16,14,8,128]{3,2,1,0:T(8,128)S(1)}, u32[]{:S(2)}, u32[]{:S(2)}) collective-permute-start(f32[16,14,8,128]{3,2,1,0:T(8,128)S(1)} %bitcast.84), channel_id=1, source_target_pairs={{0,1},{1,0},{2,3},{3,2},{4,5},{5,4},{6,7},{7,6},{8,9},{9,8},{10,11... | collective-permute-start | bytes 2752520 | tf_op jit(solution)/shard_map/ppermute | solution.py:297
  81.2 2.1 %collective-permute-done.10.oth = f32[16,14,8,128]{3,2,1,0:T(8,128)S(1)} collective-permute-done((f32[16,14,8,128]{3,2,1,0:T(8,128)S(1)}, f32[16,14,8,128]{3,2,1,0:T(8,128)S(1)}, u32[]{:S(2)}, u32[]{:S(2)}) %collective-permute-start.10) | collective-permute-done | bytes 917536 | tf_op jit(solution)/shard_map/ppermute | solution.py:297
  83.3 3.1 %shard_map.71 = (f32[16,96,128]{2,1,0:T(8,128)S(1)}, f32[1024,128]{1,0:T(8,128)S(1)}, f32[128,128]{1,0:T(8,128)S(1)}, f32[128,128]{1,0:T(8,128)S(1)}, f32[128,128]{1,0:T(8,128)S(1)}) custom-call(s32[128]{0:T(128)S(1)} %copy-done.4, f32[16,14,8,128]{3,2,1,0:T(8,128)S(1)} %bitcast.85, f32[16,14,8,128]{3,2,1,0:T(8,128)S(1)} %collective-permute-done.10.oth, ...), custom_call_target="tpu_custom_call" | custom-call | flops 500000000 | bytes 4194304 | tf_op jit(solution)/shard_map/pallas_call | solution.py:299
  86.5 0.0 copy-start.3
  86.5 0.9 copy-done.3
  87.3 3.7 %all-to-all-start.1 = ((f32[16,96,128]{2,1,0:T(8,128)}), f32[16,96,128]{2,1,0:T(8,128)S(1)}, u32[]{:S(2)}, u32[]{:S(2)}) async-start(f32[16,96,128]{2,1,0:T(8,128)} %copy-done.3), calls=%async_computation.1 | async-start | bytes 1572864 | tf_op jit(solution)/shard_map/all_to_all | solution.py:308
  91.1 0.0 copy-start.5
  91.1 0.7 copy-done.5
  91.7 1.2 %copy-done.2 = f32[16,14,8,128]{3,2,1,0:T(8,128)S(1)} copy-done((f32[16,14,8,128]{3,2,1,0:T(8,128)S(1)}, f32[16,14,8,128]{3,2,1,0:T(8,128)}, u32[]{:S(2)}) %copy-start.2) | copy-done | bytes 917528
  92.9 2.9 %shard_map.72 = f32[1024,256]{1,0:T(8,128)} custom-call(s32[128]{0:T(128)S(1)} %copy-done.4, f32[16,14,8,128]{3,2,1,0:T(8,128)S(1)} %bitcast.86, f32[16,14,8,128]{3,2,1,0:T(8,128)S(1)} %copy-done.2, f32[1024,128]{1,0:T(8,128)S(1)} %get-tuple-element.46.plow, f32[128,128]{1,0:T(8,128)S(1)} %get-tuple-element.47.inv0, f32[128,128]{1,0:T(8,128)S(1)} %get-tuple-element.48.inv1, ...), custom_call_target="tpu_custom_call" | custom-call | flops 500000000 | bytes 4194304 | tf_op jit(solution)/shard_map/pallas_call | solution.py:309
  95.8 8.0 %all-to-all-done.1.got = f32[16,96,128]{2,1,0:T(8,128)S(1)} async-done(((f32[16,96,128]{2,1,0:T(8,128)}), f32[16,96,128]{2,1,0:T(8,128)S(1)}, u32[]{:S(2)}, u32[]{:S(2)}) %all-to-all-start.1) | async-done | bytes 786464 | tf_op jit(solution)/shard_map/all_to_all | solution.py:308
  103.8 4.7 %collective-permute-start.11 = (f32[16,64,128]{2,1,0:T(8,128)S(1)}, f32[16,64,128]{2,1,0:T(8,128)S(1)}, u32[]{:S(2)}, u32[]{:S(2)}) collective-permute-start(f32[16,64,128]{2,1,0:T(8,128)S(1)} %slice.75), channel_id=1, source_target_pairs={{0,1},{1,0},{2,3},{3,2},{4,5},{5,4},{6,7},{7,6},{8,9},{9,8},{10,11... | collective-permute-start | bytes 1572872 | tf_op jit(solution)/shard_map/ppermute | solution.py:313
  108.5 1.6 %shard_map.73 = (f32[1024,256]{1,0:T(8,128)S(1)}, f32[128,256]{1,0:T(8,128)S(1)}) custom-call(s32[128]{0:T(128)S(1)} %copy-done.4, f32[1024,256]{1,0:T(8,128)S(1)} %copy-done, f32[16,96,128]{2,1,0:T(8,128)S(1)} %all-to-all-done.1.got, f32[1024,128]{1,0:T(8,128)S(1)} %get-tuple-element.46.plow, f32[128,128]{1,0:T(8,128)S(1)} %get-tuple-element.50.lsrc, ...), custom_call_target="tpu_custom_call" | custom-call | flops 500000000 | bytes 3145728 | tf_op jit(solution)/shard_map/pallas_call | solution.py:314
  110.2 0.0 collective-permute-done.11.oth
  110.2 1.8 %shard_map.74 = f32[1024,256]{1,0:T(8,128)} custom-call(s32[128]{0:T(128)S(1)} %copy-done.4, f32[1024,256]{1,0:T(8,128)S(1)} %get-tuple-element.51.cur, f32[16,64,128]{2,1,0:T(8,128)S(1)} %collective-permute-done.11.oth, f32[128,256]{1,0:T(8,128)S(1)} %get-tuple-element.52.kept), custom_call_target="tpu_custom_call" | custom-call | flops 300000000 | bytes 3145728 | tf_op jit(solution)/shard_map/pallas_call | solution.py:317
  (6 shorter events, 0.1 us)
Async XLA Ops:
  0.6 10.8 %copy-start = (f32[1024,256]{1,0:T(8,128)S(1)}, f32[1024,256]{1,0:T(8,128)}, u32[]{:S(2)}) copy-start(f32[1024,256]{1,0:T(8,128)} %a.1) | copy-start | bytes 3145732
  1.8 9.6 %collective-permute-start = (f32[8,8,8,256]{3,2,1,0:T(8,128)S(1)}, f32[8,8,8,256]{3,2,1,0:T(8,128)S(1)}, u32[]{:S(2)}, u32[]{:S(2)}) collective-permute-start(f32[8,8,8,256]{3,2,1,0:T(8,128)S(1)} %copy_bitcast_fusion), channel_id=1, source_target_pairs={{0,1},{32,33},{64,65},{96,97},{128,129},{160,161},{192,193},{224,2... | collective-permute-start | bytes 1572872 | tf_op jit(solution)/shard_map/ppermute | solution.py:269
  11.5 14.6 %copy-start.6 = (s32[2,128]{1,0:T(2,128)S(1)}, s32[2,128]{1,0:T(2,128)}, u32[]{:S(2)}) copy-start(s32[2,128]{1,0:T(2,128)} %dest.2) | copy-start | bytes 3076
  11.5 9.4 %collective-permute-start.1 = (f32[8,8,256]{2,1,0:T(8,128)S(1)}, f32[8,8,256]{2,1,0:T(8,128)S(1)}, u32[]{:S(2)}, u32[]{:S(2)}) collective-permute-start(f32[8,8,256]{2,1,0:T(8,128)S(1)} %get-tuple-element.29), channel_id=1, source_target_pairs={{1,30},{0,2},{33,62},{32,34},{65,94},{64,66},{97,126},{96,98},{129... | collective-permute-start | bytes 196616 | tf_op jit(solution)/shard_map/ppermute | solution.py:277
  15.2 7.0 %collective-permute-start.2 = (f32[8,8,256]{2,1,0:T(8,128)S(1)}, f32[8,8,256]{2,1,0:T(8,128)S(1)}, u32[]{:S(2)}, u32[]{:S(2)}) collective-permute-start(f32[8,8,256]{2,1,0:T(8,128)S(1)} %get-tuple-element.30), channel_id=1, source_target_pairs={{1,28},{0,4},{33,60},{32,36},{65,92},{64,68},{97,124},{96,100},{12... | collective-permute-start | bytes 196616 | tf_op jit(solution)/shard_map/ppermute | solution.py:277
  16.5 7.0 %collective-permute-start.3 = (f32[8,8,256]{2,1,0:T(8,128)S(1)}, f32[8,8,256]{2,1,0:T(8,128)S(1)}, u32[]{:S(2)}, u32[]{:S(2)}) collective-permute-start(f32[8,8,256]{2,1,0:T(8,128)S(1)} %get-tuple-element.31), channel_id=1, source_target_pairs={{1,26},{0,6},{33,58},{32,38},{65,90},{64,70},{97,122},{96,102},{12... | collective-permute-start | bytes 196616 | tf_op jit(solution)/shard_map/ppermute | solution.py:277
  17.8 7.0 %collective-permute-start.4 = (f32[8,8,256]{2,1,0:T(8,128)S(1)}, f32[8,8,256]{2,1,0:T(8,128)S(1)}, u32[]{:S(2)}, u32[]{:S(2)}) collective-permute-start(f32[8,8,256]{2,1,0:T(8,128)S(1)} %get-tuple-element.32), channel_id=1, source_target_pairs={{1,24},{0,8},{33,56},{32,40},{65,88},{64,72},{97,120},{96,104},{12... | collective-permute-start | bytes 196616 | tf_op jit(solution)/shard_map/ppermute | solution.py:277
  19.1 5.7 %collective-permute-start.5 = (f32[8,8,256]{2,1,0:T(8,128)S(1)}, f32[8,8,256]{2,1,0:T(8,128)S(1)}, u32[]{:S(2)}, u32[]{:S(2)}) collective-permute-start(f32[8,8,256]{2,1,0:T(8,128)S(1)} %get-tuple-element.33), channel_id=1, source_target_pairs={{1,22},{0,10},{33,54},{32,42},{65,86},{64,74},{97,118},{96,106},{1... | collective-permute-start | bytes 196616 | tf_op jit(solution)/shard_map/ppermute | solution.py:277
  20.8 4.0 %collective-permute-start.6 = (f32[8,8,256]{2,1,0:T(8,128)S(1)}, f32[8,8,256]{2,1,0:T(8,128)S(1)}, u32[]{:S(2)}, u32[]{:S(2)}) collective-permute-start(f32[8,8,256]{2,1,0:T(8,128)S(1)} %get-tuple-element.34), channel_id=1, source_target_pairs={{1,20},{0,12},{33,52},{32,44},{65,84},{64,76},{97,116},{96,108},{1... | collective-permute-start | bytes 196616 | tf_op jit(solution)/shard_map/ppermute | solution.py:277
  22.2 2.7 %collective-permute-start.7 = (f32[8,8,256]{2,1,0:T(8,128)S(1)}, f32[8,8,256]{2,1,0:T(8,128)S(1)}, u32[]{:S(2)}, u32[]{:S(2)}) collective-permute-start(f32[8,8,256]{2,1,0:T(8,128)S(1)} %get-tuple-element.35), channel_id=1, source_target_pairs={{1,18},{0,14},{33,50},{32,46},{65,82},{64,78},{97,114},{96,110},{1... | collective-permute-start | bytes 196616 | tf_op jit(solution)/shard_map/ppermute | solution.py:277
  23.5 2.6 %collective-permute-start.8 = (f32[8,8,256]{2,1,0:T(8,128)S(1)}, f32[8,8,256]{2,1,0:T(8,128)S(1)}, u32[]{:S(2)}, u32[]{:S(2)}) collective-permute-start(f32[8,8,256]{2,1,0:T(8,128)S(1)} %get-tuple-element.28.own), channel_id=1, source_target_pairs={{1,16},{33,48},{65,80},{97,112},{129,144},{161,176},{193,208},{225... | collective-permute-start | bytes 196616 | tf_op jit(solution)/shard_map/ppermute | solution.py:277
  27.5 17.1 %all-to-all-start = ((f32[16,9,8,128]{3,2,1,0:T(8,128)}), f32[16,9,8,128]{3,2,1,0:T(8,128)S(1)}, u32[]{:S(2)}, u32[]{:S(2)}) async-start(f32[16,9,8,128]{3,2,1,0:T(8,128)} %get-tuple-element.42), calls=%async_computation | async-start | bytes 1179648 | tf_op jit(solution)/shard_map/all_to_all | solution.py:291
  34.3 3.3 %collective-permute-start.9 = (f32[14,8,128]{2,1,0:T(8,128)S(1)}, f32[14,8,128]{2,1,0:T(8,128)S(1)}, u32[]{:S(2)}, u32[]{:S(2)}) collective-permute-start(f32[14,8,128]{2,1,0:T(8,128)S(1)} %get-tuple-element.40), channel_id=1, source_target_pairs={{0,1},{2,3},{4,5},{6,7},{8,9},{10,11},{12,13},{14,15},{16,17},{18,... | collective-permute-start | bytes 172040 | tf_op jit(solution)/shard_map/ppermute | solution.py:283
  37.6 7.1 %copy-start.4 = (s32[128]{0:T(128)S(1)}, s32[128]{0:T(128)}, u32[]{:S(2)}) copy-start(s32[128]{0:T(128)} %shard_map.69.meta) | copy-start | bytes 1540
  70.6 12.7 %collective-permute-start.10 = (f32[16,14,8,128]{3,2,1,0:T(8,128)S(1)}, f32[16,14,8,128]{3,2,1,0:T(8,128)S(1)}, u32[]{:S(2)}, u32[]{:S(2)}) collective-permute-start(f32[16,14,8,128]{3,2,1,0:T(8,128)S(1)} %bitcast.84), channel_id=1, source_target_pairs={{0,1},{1,0},{2,3},{3,2},{4,5},{5,4},{6,7},{7,6},{8,9},{9,8},{10,11... | collective-permute-start | bytes 2752520 | tf_op jit(solution)/shard_map/ppermute | solution.py:297
  83.3 3.1 %copy-start.1 = (f32[16,14,8,128]{3,2,1,0:T(8,128)}, f32[16,14,8,128]{3,2,1,0:T(8,128)S(1)}, u32[]{:S(2)}) copy-start(f32[16,14,8,128]{3,2,1,0:T(8,128)S(1)} %collective-permute-done.10.oth) | copy-start | bytes 2752516
  86.5 0.9 copy-start.3
  87.3 16.4 %all-to-all-start.1 = ((f32[16,96,128]{2,1,0:T(8,128)}), f32[16,96,128]{2,1,0:T(8,128)S(1)}, u32[]{:S(2)}, u32[]{:S(2)}) async-start(f32[16,96,128]{2,1,0:T(8,128)} %copy-done.3), calls=%async_computation.1 | async-start | bytes 1572864 | tf_op jit(solution)/shard_map/all_to_all | solution.py:308
  91.1 0.7 copy-start.5
  91.7 1.2 %copy-start.2 = (f32[16,14,8,128]{3,2,1,0:T(8,128)S(1)}, f32[16,14,8,128]{3,2,1,0:T(8,128)}, u32[]{:S(2)}) copy-start(f32[16,14,8,128]{3,2,1,0:T(8,128)} %copy-done.1) | copy-start | bytes 2752516
  103.8 6.3 %collective-permute-start.11 = (f32[16,64,128]{2,1,0:T(8,128)S(1)}, f32[16,64,128]{2,1,0:T(8,128)S(1)}, u32[]{:S(2)}, u32[]{:S(2)}) collective-permute-start(f32[16,64,128]{2,1,0:T(8,128)S(1)} %slice.75), channel_id=1, source_target_pairs={{0,1},{1,0},{2,3},{3,2},{4,5},{5,4},{6,7},{7,6},{8,9},{9,8},{10,11... | collective-permute-start | bytes 1572872 | tf_op jit(solution)/shard_map/ppermute | solution.py:313

commit v11 on v10

--- a/solution.py
+++ b/solution.py
@@ -266,19 +266,19 @@
     core = lax.axis_index("core")
     smem = pl.BlockSpec(memory_space=pltpu.SMEM)
     cut = a.reshape(SLOTS, NZ, 8, 2 * W)
-    over = lax.ppermute(cut[:, 8:].transpose(1, 0, 2, 3), ("z", "core"), [(0, 1)])
-    pieces = [jnp.where(core == 0, cut[:, step % 8], over[8 - step]) for step in range(1, 9)]
+    over = lax.ppermute(cut[:, 9:].transpose(1, 0, 2, 3), ("z", "core"), [(0, 1)])
+    pieces = [jnp.where(core == 0, cut[:, step % 9], over[max(7 - step, 0)]) for step in range(1, 10)]
     pieces = lax.optimization_barrier(pieces)
     got = []
     for step in range(1, 9):
-        pairs = [(1, 2 * (NZ - step))]
+        pairs = [(0, 2 * step)]
         if step < 8:
-            pairs.append((0, 2 * step))
+            pairs.append((1, 2 * (NZ - step)))
         got.append(lax.ppermute(pieces[step - 1], ("z", "core"), pairs))
 
     out0, panel, last = call(
         route_kernel, (f32(NP, 9, 8, W), f32(14, 8, W), f32(2, 8, W)), 10, moved=2**20
-    )(dest_rows, a[: 2 * W], pieces[7], *got)
+    )(dest_rows, a[: 2 * W], pieces[8], *got)
     out0, maps = lax.optimization_barrier((out0, (dest_rows, row_mask, col_mask)))
     passed = lax.ppermute(panel, "core", [(0, 1)])
     meta = pl.pallas_call(

time: 113 us -> 115 us (1.018)
  starting transfers between devices: 41.6 us -> 45 us
  waiting for transfers between devices: 26.6 us -> 25.1 us
    ppermute x1, starting transfers between devices: 10.7 us -> 14.5 us  [shards(): oth = lax.ppermute(own, 'core', [(0, 1), (1, 0)])]
    all_to_all x1, waiting for transfers between devices: 7.07 us -> 5.52 us  [shards(): got0 = lax.all_to_all(out0, ('x', 'y'), 0, 0, tiled=True)]
  transfers between devices with their start and end apart: 14 -> 14, of which waited for: 5 -> 6; matrix products, arithmetic and copies ran while one was open for 0% -> 0% of each run, Pallas kernels for 6% -> 6%
where the time goes in v11:
time: 115 us
  starting transfers between devices  45 us (39%)
  waiting for transfers between devices  25.1 us (22%)
  blocking collectives  25.1 us (22%)
  Pallas kernels  13.5 us (12%)
  local copies, waits for them, and re-layouts  3.86 us (3%)
  other arithmetic  1.17 us (1%)
    all_gather x1, blocking collectives, shards(): own = lax.all_gather(payload, 'z', axis=0, tiled=False)  25.1 us
    ppermute x1, starting transfers between devices, shards(): oth = lax.ppermute(own, 'core', [(0, 1), (1, 0)])  14.5 us
    ppermute x8, starting transfers between devices, shards(): got.append(lax.ppermute(pieces[step - 1], ('z', 'core'), pairs))  12.7 us
    ppermute x1, waiting for transfers between devices, shards(): lax.ppermute(cut[:, 9:].transpose(1, 0, 2, 3), ('z', 'core'), [(0, 1)])  8.16 us
    all_to_all x1, waiting for transfers between devices, shards(): got1 = lax.all_to_all(send, ('x', 'y'), 0, 0, tiled=True)  8.01 us
    all_to_all x1, starting transfers between devices, shards(): got0 = lax.all_to_all(out0, ('x', 'y'), 0, 0, tiled=True)  6.75 us
    all_to_all x1, waiting for transfers between devices, shards(): got0 = lax.all_to_all(out0, ('x', 'y'), 0, 0, tiled=True)  5.52 us
    ppermute x1, starting transfers between devices, shards(): oth1 = lax.ppermute(got1[:, :H], 'core', [(0, 1), (1, 0)])  4.67 us
  transfers between devices with their start and end apart: 14, of which 6 were waited for; matrix products, arithmetic and copies ran while one was open for 0% of the time, Pallas kernels for 6%

profile of v11, /device:TPU:1, one launch (start us, length us, event | category | flops | bytes accessed | tf_op | source)
XLA Modules:
  0.0 114.5 jit_solution(5959856115479526266)
XLA Ops:
  0.6 1.1 copy_bitcast_fusion
  1.7 0.0 copy-start
  1.7 1.4 %collective-permute-start = (f32[7,8,8,256]{3,2,1,0:T(8,128)S(1)}, f32[7,8,8,256]{3,2,1,0:T(8,128)S(1)}, u32[]{:S(2)}, u32[]{:S(2)}) collective-permute-start(f32[7,8,8,256]{3,2,1,0:T(8,128)S(1)} %copy_bitcast_fusion), channel_id=1, source_target_pairs={{0,1},{32,33},{64,65},{96,97},{128,129},{160,161},{192,193},{224,2... | collective-permute-start | bytes 1376264 | tf_op jit(solution)/shard_map/ppermute | solution.py:269
  3.1 8.2 %collective-permute-done = f32[7,8,8,256]{3,2,1,0:T(8,128)S(1)} collective-permute-done((f32[7,8,8,256]{3,2,1,0:T(8,128)S(1)}, f32[7,8,8,256]{3,2,1,0:T(8,128)S(1)}, u32[]{:S(2)}, u32[]{:S(2)}) %collective-permute-start) | collective-permute-done | bytes 458784 | tf_op jit(solution)/shard_map/ppermute | solution.py:269
  11.3 1.2 %fusion = (f32[8,8,256]{2,1,0:T(8,128)S(1)}, f32[8,8,256]{2,1,0:T(8,128)S(1)}, f32[8,8,256]{2,1,0:T(8,128)S(1)}, f32[8,8,256]{2,1,0:T(8,128)S(1)}, f32[8,8,256]{...) fusion(f32[8,16,8,256]{3,2,1,0:T(8,128)} %bitcast.94, ...), kind=kLoop, calls=%fused_computation.2 | loop fusion | flops 147456 | bytes 1638401 | tf_op jit(solution)/shard_map/jit(_where)/select_n | solution.py:270
  12.5 0.0 copy-start.6
  12.5 3.8 %collective-permute-start.1 = (f32[8,8,256]{2,1,0:T(8,128)S(1)}, f32[8,8,256]{2,1,0:T(8,128)S(1)}, u32[]{:S(2)}, u32[]{:S(2)}) collective-permute-start(f32[8,8,256]{2,1,0:T(8,128)S(1)} %get-tuple-element.30), channel_id=1, source_target_pairs={{0,2},{1,30},{32,34},{33,62},{64,66},{65,94},{96,98},{97,126},{128... | collective-permute-start | bytes 196616 | tf_op jit(solution)/shard_map/ppermute | solution.py:277
  16.3 1.3 %collective-permute-start.2 = (f32[8,8,256]{2,1,0:T(8,128)S(1)}, f32[8,8,256]{2,1,0:T(8,128)S(1)}, u32[]{:S(2)}, u32[]{:S(2)}) collective-permute-start(f32[8,8,256]{2,1,0:T(8,128)S(1)} %get-tuple-element.31), channel_id=1, source_target_pairs={{0,4},{1,28},{32,36},{33,60},{64,68},{65,92},{96,100},{97,124},{12... | collective-permute-start | bytes 196616 | tf_op jit(solution)/shard_map/ppermute | solution.py:277
  17.6 1.3 %collective-permute-start.3 = (f32[8,8,256]{2,1,0:T(8,128)S(1)}, f32[8,8,256]{2,1,0:T(8,128)S(1)}, u32[]{:S(2)}, u32[]{:S(2)}) collective-permute-start(f32[8,8,256]{2,1,0:T(8,128)S(1)} %get-tuple-element.32), channel_id=1, source_target_pairs={{0,6},{1,26},{32,38},{33,58},{64,70},{65,90},{96,102},{97,122},{12... | collective-permute-start | bytes 196616 | tf_op jit(solution)/shard_map/ppermute | solution.py:277
  18.9 1.3 %collective-permute-start.4 = (f32[8,8,256]{2,1,0:T(8,128)S(1)}, f32[8,8,256]{2,1,0:T(8,128)S(1)}, u32[]{:S(2)}, u32[]{:S(2)}) collective-permute-start(f32[8,8,256]{2,1,0:T(8,128)S(1)} %get-tuple-element.33), channel_id=1, source_target_pairs={{0,8},{1,24},{32,40},{33,56},{64,72},{65,88},{96,104},{97,120},{12... | collective-permute-start | bytes 196616 | tf_op jit(solution)/shard_map/ppermute | solution.py:277
  20.2 1.8 %collective-permute-start.5 = (f32[8,8,256]{2,1,0:T(8,128)S(1)}, f32[8,8,256]{2,1,0:T(8,128)S(1)}, u32[]{:S(2)}, u32[]{:S(2)}) collective-permute-start(f32[8,8,256]{2,1,0:T(8,128)S(1)} %get-tuple-element.34), channel_id=1, source_target_pairs={{0,10},{1,22},{32,42},{33,54},{64,74},{65,86},{96,106},{97,118},{1... | collective-permute-start | bytes 196616 | tf_op jit(solution)/shard_map/ppermute | solution.py:277
  21.9 0.0 collective-permute-done.1.refs_0_
  22.0 1.3 %collective-permute-start.6 = (f32[8,8,256]{2,1,0:T(8,128)S(1)}, f32[8,8,256]{2,1,0:T(8,128)S(1)}, u32[]{:S(2)}, u32[]{:S(2)}) collective-permute-start(f32[8,8,256]{2,1,0:T(8,128)S(1)} %get-tuple-element.35), channel_id=1, source_target_pairs={{0,12},{1,20},{32,44},{33,52},{64,76},{65,84},{96,108},{97,116},{1... | collective-permute-start | bytes 196616 | tf_op jit(solution)/shard_map/ppermute | solution.py:277
  23.3 0.0 collective-permute-done.2.refs_1_
  23.3 1.3 %collective-permute-start.7 = (f32[8,8,256]{2,1,0:T(8,128)S(1)}, f32[8,8,256]{2,1,0:T(8,128)S(1)}, u32[]{:S(2)}, u32[]{:S(2)}) collective-permute-start(f32[8,8,256]{2,1,0:T(8,128)S(1)} %get-tuple-element.36), channel_id=1, source_target_pairs={{0,14},{1,18},{32,46},{33,50},{64,78},{65,82},{96,110},{97,114},{1... | collective-permute-start | bytes 196616 | tf_op jit(solution)/shard_map/ppermute | solution.py:277
  24.6 0.0 collective-permute-done.3.refs_2_
  24.6 0.7 collective-permute-start.8
  25.3 0.0 collective-permute-done.4.refs_3_
  25.3 0.0 collective-permute-done.5.refs_4_
  25.3 0.0 collective-permute-done.6.refs_5_
  25.3 0.6 collective-permute-done.7.refs_6_
  25.9 0.0 collective-permute-done.8.refs_7_
  25.9 1.4 %shard_map.68 = (f32[16,9,8,128]{3,2,1,0:T(8,128)}, f32[14,8,128]{2,1,0:T(8,128)S(1)}, f32[2,8,128]{2,1,0:T(8,128)S(1)}) custom-call(s32[2,128]{1,0:T(2,128)S(1)} %copy-done.6, f32[256,256]{1,0:T(8,128)S(1)} %slice.59.a, f32[8,8,256]{2,1,0:T(8,128)S(1)} %get-tuple-element.29.own, f32[8,8,256]{2,1,0:T(8,128)S(1)} %collective-permute-done.1.refs_0_, ...), custom_call_target="tpu_custom_call" | custom-call | bytes 1048576 | tf_op jit(solution)/shard_map/pallas_call | solution.py:279
  27.3 6.8 %all-to-all-start = ((f32[16,9,8,128]{3,2,1,0:T(8,128)}), f32[16,9,8,128]{3,2,1,0:T(8,128)S(1)}, u32[]{:S(2)}, u32[]{:S(2)}) async-start(f32[16,9,8,128]{3,2,1,0:T(8,128)} %get-tuple-element.44), calls=%async_computation | async-start | bytes 1179648 | tf_op jit(solution)/shard_map/all_to_all | solution.py:291
  34.1 1.3 %collective-permute-start.9 = (f32[14,8,128]{2,1,0:T(8,128)S(1)}, f32[14,8,128]{2,1,0:T(8,128)S(1)}, u32[]{:S(2)}, u32[]{:S(2)}) collective-permute-start(f32[14,8,128]{2,1,0:T(8,128)S(1)} %get-tuple-element.42), channel_id=1, source_target_pairs={{0,1},{2,3},{4,5},{6,7},{8,9},{10,11},{12,13},{14,15},{16,17},{18,... | collective-permute-start | bytes 172040 | tf_op jit(solution)/shard_map/ppermute | solution.py:283
  35.4 2.0 %shard_map.69.meta = s32[128]{0:T(128)} custom-call(s32[2,128]{1,0:T(2,128)} %dest.2, s32[2,128]{1,0:T(2,128)} %row_mask, s32[2,64]{1,0:T(2,128)} %col_mask), custom_call_target="tpu_custom_call" | custom-call | tf_op jit(solution)/shard_map/pallas_call | solution.py:284
  37.4 0.0 copy-start.4
  37.4 0.7 collective-permute-done.9.passed
  38.1 5.5 %all-to-all-done.got = f32[16,9,8,128]{3,2,1,0:T(8,128)S(1)} async-done(((f32[16,9,8,128]{3,2,1,0:T(8,128)}), f32[16,9,8,128]{3,2,1,0:T(8,128)S(1)}, u32[]{:S(2)}, u32[]{:S(2)}) %all-to-all-start) | async-done | bytes 589856 | tf_op jit(solution)/shard_map/all_to_all | solution.py:291
  43.6 0.0 copy-done.4
  43.6 0.6 shard_map.70
  44.2 25.1 %all-gather = f32[224,8,128]{2,1,0:T(8,128)S(1)} all-gather(f32[14,8,128]{2,1,0:T(8,128)S(1)} %get-tuple-element.45), channel_id=2, replica_groups=mesh['x'=4,'y'=4,'z'=16,'core'=2] {'z'}, dimensions={0}, use_global_device_ids=true | all-gather | bytes 974848 | tf_op jit(solution)/shard_map/all_gather | solution.py:296
  69.3 14.5 %collective-permute-start.10 = (f32[16,14,8,128]{3,2,1,0:T(8,128)S(1)}, f32[16,14,8,128]{3,2,1,0:T(8,128)S(1)}, u32[]{:S(2)}, u32[]{:S(2)}) collective-permute-start(f32[16,14,8,128]{3,2,1,0:T(8,128)S(1)} %bitcast.90), channel_id=1, source_target_pairs={{0,1},{1,0},{2,3},{3,2},{4,5},{5,4},{6,7},{7,6},{8,9},{9,8},{10,11... | collective-permute-start | bytes 2752520 | tf_op jit(solution)/shard_map/ppermute | solution.py:297
  83.8 2.1 %collective-permute-done.10.oth = f32[16,14,8,128]{3,2,1,0:T(8,128)S(1)} collective-permute-done((f32[16,14,8,128]{3,2,1,0:T(8,128)S(1)}, f32[16,14,8,128]{3,2,1,0:T(8,128)S(1)}, u32[]{:S(2)}, u32[]{:S(2)}) %collective-permute-start.10) | collective-permute-done | bytes 917536 | tf_op jit(solution)/shard_map/ppermute | solution.py:297
  85.9 3.1 %shard_map.71 = (f32[16,96,128]{2,1,0:T(8,128)S(1)}, f32[1024,128]{1,0:T(8,128)S(1)}, f32[128,128]{1,0:T(8,128)S(1)}, f32[128,128]{1,0:T(8,128)S(1)}, f32[128,128]{1,0:T(8,128)S(1)}) custom-call(s32[128]{0:T(128)S(1)} %copy-done.4, f32[16,14,8,128]{3,2,1,0:T(8,128)S(1)} %bitcast.91, f32[16,14,8,128]{3,2,1,0:T(8,128)S(1)} %collective-permute-done.10.oth, ...), custom_call_target="tpu_custom_call" | custom-call | flops 500000000 | bytes 4194304 | tf_op jit(solution)/shard_map/pallas_call | solution.py:299
  89.0 0.0 copy-done.1
  89.0 0.0 copy-start.3
  89.0 0.9 copy-done.3
  89.9 3.6 %all-to-all-start.1 = ((f32[16,96,128]{2,1,0:T(8,128)}), f32[16,96,128]{2,1,0:T(8,128)S(1)}, u32[]{:S(2)}, u32[]{:S(2)}) async-start(f32[16,96,128]{2,1,0:T(8,128)} %copy-done.3), calls=%async_computation.1 | async-start | bytes 1572864 | tf_op jit(solution)/shard_map/all_to_all | solution.py:308
  93.5 0.0 copy-start.5
  93.5 0.7 copy-done.5
  94.2 1.2 %copy-done.2 = f32[16,14,8,128]{3,2,1,0:T(8,128)S(1)} copy-done((f32[16,14,8,128]{3,2,1,0:T(8,128)S(1)}, f32[16,14,8,128]{3,2,1,0:T(8,128)}, u32[]{:S(2)}) %copy-start.2) | copy-done | bytes 917528
  95.4 2.9 %shard_map.72 = f32[1024,256]{1,0:T(8,128)} custom-call(s32[128]{0:T(128)S(1)} %copy-done.4, f32[16,14,8,128]{3,2,1,0:T(8,128)S(1)} %bitcast.92, f32[16,14,8,128]{3,2,1,0:T(8,128)S(1)} %copy-done.2, f32[1024,128]{1,0:T(8,128)S(1)} %get-tuple-element.48.plow, f32[128,128]{1,0:T(8,128)S(1)} %get-tuple-element.49.inv0, f32[128,128]{1,0:T(8,128)S(1)} %get-tuple-element.50.inv1, ...), custom_call_target="tpu_custom_call" | custom-call | flops 500000000 | bytes 4194304 | tf_op jit(solution)/shard_map/pallas_call | solution.py:309
  98.3 8.0 %all-to-all-done.1.got = f32[16,96,128]{2,1,0:T(8,128)S(1)} async-done(((f32[16,96,128]{2,1,0:T(8,128)}), f32[16,96,128]{2,1,0:T(8,128)S(1)}, u32[]{:S(2)}, u32[]{:S(2)}) %all-to-all-start.1) | async-done | bytes 786464 | tf_op jit(solution)/shard_map/all_to_all | solution.py:308
  106.3 4.7 %collective-permute-start.11 = (f32[16,64,128]{2,1,0:T(8,128)S(1)}, f32[16,64,128]{2,1,0:T(8,128)S(1)}, u32[]{:S(2)}, u32[]{:S(2)}) collective-permute-start(f32[16,64,128]{2,1,0:T(8,128)S(1)} %slice.77), channel_id=1, source_target_pairs={{0,1},{1,0},{2,3},{3,2},{4,5},{5,4},{6,7},{7,6},{8,9},{9,8},{10,11... | collective-permute-start | bytes 1572872 | tf_op jit(solution)/shard_map/ppermute | solution.py:313
  111.0 1.7 %shard_map.73 = (f32[1024,256]{1,0:T(8,128)S(1)}, f32[128,256]{1,0:T(8,128)S(1)}) custom-call(s32[128]{0:T(128)S(1)} %copy-done.4, f32[1024,256]{1,0:T(8,128)S(1)} %copy-done, f32[16,96,128]{2,1,0:T(8,128)S(1)} %all-to-all-done.1.got, f32[1024,128]{1,0:T(8,128)S(1)} %get-tuple-element.48.plow, f32[128,128]{1,0:T(8,128)S(1)} %get-tuple-element.52.lsrc, ...), custom_call_target="tpu_custom_call" | custom-call | flops 500000000 | bytes 3145728 | tf_op jit(solution)/shard_map/pallas_call | solution.py:314
  112.7 0.0 collective-permute-done.11.oth
  112.7 1.8 %shard_map.74 = f32[1024,256]{1,0:T(8,128)} custom-call(s32[128]{0:T(128)S(1)} %copy-done.4, f32[1024,256]{1,0:T(8,128)S(1)} %get-tuple-element.53.cur, f32[16,64,128]{2,1,0:T(8,128)S(1)} %collective-permute-done.11.oth, f32[128,256]{1,0:T(8,128)S(1)} %get-tuple-element.54.kept), custom_call_target="tpu_custom_call" | custom-call | flops 300000000 | bytes 3145728 | tf_op jit(solution)/shard_map/pallas_call | solution.py:317
  (6 shorter events, 0.1 us)
Async XLA Ops:
  1.7 23.6 %copy-start = (f32[1024,256]{1,0:T(8,128)S(1)}, f32[1024,256]{1,0:T(8,128)}, u32[]{:S(2)}) copy-start(f32[1024,256]{1,0:T(8,128)} %a.1) | copy-start | bytes 3145732
  1.7 9.6 %collective-permute-start = (f32[7,8,8,256]{3,2,1,0:T(8,128)S(1)}, f32[7,8,8,256]{3,2,1,0:T(8,128)S(1)}, u32[]{:S(2)}, u32[]{:S(2)}) collective-permute-start(f32[7,8,8,256]{3,2,1,0:T(8,128)S(1)} %copy_bitcast_fusion), channel_id=1, source_target_pairs={{0,1},{32,33},{64,65},{96,97},{128,129},{160,161},{192,193},{224,2... | collective-permute-start | bytes 1376264 | tf_op jit(solution)/shard_map/ppermute | solution.py:269
  12.5 13.4 %copy-start.6 = (s32[2,128]{1,0:T(2,128)S(1)}, s32[2,128]{1,0:T(2,128)}, u32[]{:S(2)}) copy-start(s32[2,128]{1,0:T(2,128)} %dest.2) | copy-start | bytes 3076
  12.5 9.5 %collective-permute-start.1 = (f32[8,8,256]{2,1,0:T(8,128)S(1)}, f32[8,8,256]{2,1,0:T(8,128)S(1)}, u32[]{:S(2)}, u32[]{:S(2)}) collective-permute-start(f32[8,8,256]{2,1,0:T(8,128)S(1)} %get-tuple-element.30), channel_id=1, source_target_pairs={{0,2},{1,30},{32,34},{33,62},{64,66},{65,94},{96,98},{97,126},{128... | collective-permute-start | bytes 196616 | tf_op jit(solution)/shard_map/ppermute | solution.py:277
  16.3 7.0 %collective-permute-start.2 = (f32[8,8,256]{2,1,0:T(8,128)S(1)}, f32[8,8,256]{2,1,0:T(8,128)S(1)}, u32[]{:S(2)}, u32[]{:S(2)}) collective-permute-start(f32[8,8,256]{2,1,0:T(8,128)S(1)} %get-tuple-element.31), channel_id=1, source_target_pairs={{0,4},{1,28},{32,36},{33,60},{64,68},{65,92},{96,100},{97,124},{12... | collective-permute-start | bytes 196616 | tf_op jit(solution)/shard_map/ppermute | solution.py:277
  17.6 7.0 %collective-permute-start.3 = (f32[8,8,256]{2,1,0:T(8,128)S(1)}, f32[8,8,256]{2,1,0:T(8,128)S(1)}, u32[]{:S(2)}, u32[]{:S(2)}) collective-permute-start(f32[8,8,256]{2,1,0:T(8,128)S(1)} %get-tuple-element.32), channel_id=1, source_target_pairs={{0,6},{1,26},{32,38},{33,58},{64,70},{65,90},{96,102},{97,122},{12... | collective-permute-start | bytes 196616 | tf_op jit(solution)/shard_map/ppermute | solution.py:277
  18.9 6.4 %collective-permute-start.4 = (f32[8,8,256]{2,1,0:T(8,128)S(1)}, f32[8,8,256]{2,1,0:T(8,128)S(1)}, u32[]{:S(2)}, u32[]{:S(2)}) collective-permute-start(f32[8,8,256]{2,1,0:T(8,128)S(1)} %get-tuple-element.33), channel_id=1, source_target_pairs={{0,8},{1,24},{32,40},{33,56},{64,72},{65,88},{96,104},{97,120},{12... | collective-permute-start | bytes 196616 | tf_op jit(solution)/shard_map/ppermute | solution.py:277
  20.2 5.1 %collective-permute-start.5 = (f32[8,8,256]{2,1,0:T(8,128)S(1)}, f32[8,8,256]{2,1,0:T(8,128)S(1)}, u32[]{:S(2)}, u32[]{:S(2)}) collective-permute-start(f32[8,8,256]{2,1,0:T(8,128)S(1)} %get-tuple-element.34), channel_id=1, source_target_pairs={{0,10},{1,22},{32,42},{33,54},{64,74},{65,86},{96,106},{97,118},{1... | collective-permute-start | bytes 196616 | tf_op jit(solution)/shard_map/ppermute | solution.py:277
  22.0 3.4 %collective-permute-start.6 = (f32[8,8,256]{2,1,0:T(8,128)S(1)}, f32[8,8,256]{2,1,0:T(8,128)S(1)}, u32[]{:S(2)}, u32[]{:S(2)}) collective-permute-start(f32[8,8,256]{2,1,0:T(8,128)S(1)} %get-tuple-element.35), channel_id=1, source_target_pairs={{0,12},{1,20},{32,44},{33,52},{64,76},{65,84},{96,108},{97,116},{1... | collective-permute-start | bytes 196616 | tf_op jit(solution)/shard_map/ppermute | solution.py:277
  23.3 2.6 %collective-permute-start.7 = (f32[8,8,256]{2,1,0:T(8,128)S(1)}, f32[8,8,256]{2,1,0:T(8,128)S(1)}, u32[]{:S(2)}, u32[]{:S(2)}) collective-permute-start(f32[8,8,256]{2,1,0:T(8,128)S(1)} %get-tuple-element.36), channel_id=1, source_target_pairs={{0,14},{1,18},{32,46},{33,50},{64,78},{65,82},{96,110},{97,114},{1... | collective-permute-start | bytes 196616 | tf_op jit(solution)/shard_map/ppermute | solution.py:277
  24.6 1.3 %collective-permute-start.8 = (f32[8,8,256]{2,1,0:T(8,128)S(1)}, f32[8,8,256]{2,1,0:T(8,128)S(1)}, u32[]{:S(2)}, u32[]{:S(2)}) collective-permute-start(f32[8,8,256]{2,1,0:T(8,128)S(1)} %get-tuple-element.37), channel_id=1, source_target_pairs={{0,16},{32,48},{64,80},{96,112},{128,144},{160,176},{192,208},{224... | collective-permute-start | bytes 196616 | tf_op jit(solution)/shard_map/ppermute | solution.py:277
  27.3 16.3 %all-to-all-start = ((f32[16,9,8,128]{3,2,1,0:T(8,128)}), f32[16,9,8,128]{3,2,1,0:T(8,128)S(1)}, u32[]{:S(2)}, u32[]{:S(2)}) async-start(f32[16,9,8,128]{3,2,1,0:T(8,128)} %get-tuple-element.44), calls=%async_computation | async-start | bytes 1179648 | tf_op jit(solution)/shard_map/all_to_all | solution.py:291
  34.1 4.0 %collective-permute-start.9 = (f32[14,8,128]{2,1,0:T(8,128)S(1)}, f32[14,8,128]{2,1,0:T(8,128)S(1)}, u32[]{:S(2)}, u32[]{:S(2)}) collective-permute-start(f32[14,8,128]{2,1,0:T(8,128)S(1)} %get-tuple-element.42), channel_id=1, source_target_pairs={{0,1},{2,3},{4,5},{6,7},{8,9},{10,11},{12,13},{14,15},{16,17},{18,... | collective-permute-start | bytes 172040 | tf_op jit(solution)/shard_map/ppermute | solution.py:283
  37.4 6.3 %copy-start.4 = (s32[128]{0:T(128)S(1)}, s32[128]{0:T(128)}, u32[]{:S(2)}) copy-start(s32[128]{0:T(128)} %shard_map.69.meta) | copy-start | bytes 1540
  69.3 16.6 %collective-permute-start.10 = (f32[16,14,8,128]{3,2,1,0:T(8,128)S(1)}, f32[16,14,8,128]{3,2,1,0:T(8,128)S(1)}, u32[]{:S(2)}, u32[]{:S(2)}) collective-permute-start(f32[16,14,8,128]{3,2,1,0:T(8,128)S(1)} %bitcast.90), channel_id=1, source_target_pairs={{0,1},{1,0},{2,3},{3,2},{4,5},{5,4},{6,7},{7,6},{8,9},{9,8},{10,11... | collective-permute-start | bytes 2752520 | tf_op jit(solution)/shard_map/ppermute | solution.py:297
  85.9 3.1 %copy-start.1 = (f32[16,14,8,128]{3,2,1,0:T(8,128)}, f32[16,14,8,128]{3,2,1,0:T(8,128)S(1)}, u32[]{:S(2)}) copy-start(f32[16,14,8,128]{3,2,1,0:T(8,128)S(1)} %collective-permute-done.10.oth) | copy-start | bytes 2752516
  89.0 0.9 copy-start.3
  89.9 16.4 %all-to-all-start.1 = ((f32[16,96,128]{2,1,0:T(8,128)}), f32[16,96,128]{2,1,0:T(8,128)S(1)}, u32[]{:S(2)}, u32[]{:S(2)}) async-start(f32[16,96,128]{2,1,0:T(8,128)} %copy-done.3), calls=%async_computation.1 | async-start | bytes 1572864 | tf_op jit(solution)/shard_map/all_to_all | solution.py:308
  93.5 0.7 copy-start.5
  94.2 1.2 %copy-start.2 = (f32[16,14,8,128]{3,2,1,0:T(8,128)S(1)}, f32[16,14,8,128]{3,2,1,0:T(8,128)}, u32[]{:S(2)}) copy-start(f32[16,14,8,128]{3,2,1,0:T(8,128)} %copy-done.1) | copy-start | bytes 2752516
  106.3 6.3 %collective-permute-start.11 = (f32[16,64,128]{2,1,0:T(8,128)S(1)}, f32[16,64,128]{2,1,0:T(8,128)S(1)}, u32[]{:S(2)}, u32[]{:S(2)}) collective-permute-start(f32[16,64,128]{2,1,0:T(8,128)S(1)} %slice.77), channel_id=1, source_target_pairs={{0,1},{1,0},{2,3},{3,2},{4,5},{5,4},{6,7},{7,6},{8,9},{9,8},{10,11... | collective-permute-start | bytes 1572872 | tf_op jit(solution)/shard_map/ppermute | solution.py:313
